TPU v7x, 32 devices: a whole 2x2x4 slice. The times are simulated.
32 devices in a mesh: sensor: 2 (over x), cell: 16 (over z, y, core).
Axes of the slice: x: 2, y: 2, z: 4, core: 2. Of those that a mesh axis runs over, the one named last changes fastest.
Arguments:
- swath: float32 [2, 64, 8192], P('sensor', None, 'cell'), may hold values from -6 to 6
- enc_weight: float32 [2, 64, 192], P('sensor'), may hold values from -0.4375 to 0.4375
- key_weight: float32 [64, 64], replicated, may hold values from -0.75 to 0.75
- value_weight: float32 [64, 64], replicated, may hold values from -0.75 to 0.75
- cell_query: float32 [64, 4096], P(None, 'cell'), may hold values from -6 to 6
- quality: float32 [2, 8192], P('sensor', 'cell'), may hold values from -4 to 302
- sample_cell: int32 [2, 8192], P('sensor', 'cell'), may hold values from 0 to 255
- live: int32 [2, 16], P('sensor', 'cell'), may hold values from 128 to 512
- neighbours: int32 [8, 4096], P(None, 'cell'), may hold values from 0 to 4095, as said below
- hp_weight: float32 [64, 576], replicated, may hold values from -0.25 to 0.25
Outputs:
- joined: float32 [64, 4096], P('sensor', 'cell')
Inputs may be any that keep to these rules, and one draw needn't show every extreme that they name: `neighbours`: a cell range is a patch of 16 x 16 cells, local index row * 16 + column; every neighbour lies within 257 cells of its own cell, either in the cell's own range or in an adjacent one, and then in the first column of the next range or the last column of the previous range.
All inputs are finite; a program needn't handle non-finite values.
Results may differ from a plain program's by a relative error of at most 0.0003.
Values sent between devices are 32-bit elements; how exact they have to be, the bound alone decides.
No kernel may reach another device: no remote copies, remote signals or barrier semaphores. Data moves between devices by JAX's collectives and lax.ppermute only.
A program may use at most 64 MiB of HBM per device.

v0:
```python
import math

import jax
import jax.numpy as jnp
from jax import lax
from jax.sharding import PartitionSpec as P

floor_value = -1e30
highest = lax.Precision.HIGHEST


def passed_along(value, axis, steps):
    count = lax.axis_size(axis)
    initial, last = (max(0, -steps), min(count, count - steps))
    return lax.ppermute(value, axis, [(source, source + steps) for source in range(initial, last)])


def combined_all(value, axis, join):
    pieces = jax.tree.map(lambda part: lax.all_gather(part, axis), value)
    head = jax.tree.map(lambda part: part[0], pieces)
    tail = jax.tree.map(lambda part: part[1:], pieces)
    so_far, _ = lax.scan(lambda so_far, section: (join(so_far, section), None), head, tail)
    return so_far


def extended_2(shard, sides, width):
    for axis, dim in sides:
        devices, length = (lax.axis_size(axis), shard.shape[dim])
        up = [(i, (i + 1) % devices) for i in range(devices - 1)]
        down = [(j, i) for i, j in up]
        last = lax.slice_in_dim(shard, length - width, length, axis=dim)
        initial = lax.slice_in_dim(shard, 0, width, axis=dim)
        before = lax.ppermute(last, axis, up)
        after = lax.ppermute(initial, axis, down)
        shard = jnp.concatenate([before, shard, after], axis=dim)
    return shard


def combine_pools(first, second):
    first_peak, first_total, first_sum = first
    second_peak, second_total, second_sum = second
    joint = jnp.maximum(first_peak, second_peak)
    first_factor = jnp.exp(first_peak - joint)
    second_factor = jnp.exp(second_peak - joint)
    return (
        joint,
        first_total * first_factor + second_total * second_factor,
        first_sum * first_factor[None, :] + second_sum * second_factor[None, :],
    )


def stencil(cube, centre, gathered):
    return jnp.dot(cube[:, 0, :], centre, precision=highest) + jnp.einsum(
        "oki,ikc->oc", cube[:, 1:, :], gathered, precision=highest
    )


def on_device(
    swath,
    enc_weight,
    key_weight,
    value_weight,
    cell_query,
    quality,
    sample_cell,
    live,
    neighbours,
    hp_weight,
):
    signal = swath[0]
    channels = signal.shape[0]
    sample_count = signal.shape[1]
    cell_count = cell_query.shape[1]
    tail_cols = passed_along(signal[:, sample_count - 2 :], "cell", 1)
    padded = jnp.concatenate([tail_cols, signal], axis=1)
    stacked = jnp.concatenate(
        [
            padded[:, 0:sample_count],
            padded[:, 1 : sample_count + 1],
            padded[:, 2 : sample_count + 2],
        ],
        axis=0,
    )
    encoded = jax.nn.gelu(jnp.dot(enc_weight[0], stacked, precision=highest), approximate=False)
    key_rows = jnp.dot(key_weight, encoded, precision=highest)
    value_rows = jnp.dot(value_weight, encoded, precision=highest)
    range_start = lax.axis_index("cell") * cell_count
    local_cell = sample_cell[0]
    query_rows = jnp.take(cell_query, local_cell, axis=1)
    inv_root = 1.0 / math.sqrt(channels)
    score = jnp.sum(query_rows * key_rows, axis=0) * inv_root + quality[0]
    valid = jnp.arange(sample_count, dtype=jnp.int32) < live[0, 0]
    local_peak = jnp.maximum(
        jax.ops.segment_max(jnp.where(valid, score, -jnp.inf), local_cell, cell_count), floor_value
    )
    weights_exp = jnp.where(valid, jnp.exp(score - local_peak[local_cell]), 0.0)
    local_total = jax.ops.segment_sum(weights_exp, local_cell, cell_count)
    local_sum = jax.ops.segment_sum((value_rows * weights_exp[None, :]).T, local_cell, cell_count).T
    prior_key = jnp.dot(key_weight, cell_query, precision=highest)
    prior_score = jnp.sum(cell_query * prior_key, axis=0) * inv_root
    hp_cube = hp_weight.reshape(hp_weight.shape[0], -1, channels)
    out_rows = channels // lax.axis_size("sensor")
    peak_all, total_all, sum_all = combined_all(
        (local_peak, local_total, local_sum), "sensor", combine_pools
    )
    prior_value = jnp.dot(value_weight, cell_query, precision=highest)
    joint = jnp.maximum(peak_all, prior_score)
    pool_factor = jnp.exp(peak_all - joint)
    prior_factor = jnp.exp(prior_score - joint)
    pooled = (sum_all * pool_factor[None, :] + prior_value * prior_factor[None, :]) / (
        total_all * pool_factor + prior_factor
    )[None, :]
    extended = extended_2(pooled, (("cell", 1),), cell_count)
    gathered = jnp.take(extended, neighbours - range_start + cell_count, axis=1)
    own_cube = lax.dynamic_slice_in_dim(hp_cube, lax.axis_index("sensor") * out_rows, out_rows, 0)
    joined = stencil(own_cube, pooled, gathered)
    return joined


def solution(mesh):
    in_specs = (
        P("sensor", None, "cell"),
        P("sensor", None, None),
        P(),
        P(),
        P(None, "cell"),
        P("sensor", "cell"),
        P("sensor", "cell"),
        P("sensor", "cell"),
        P(None, "cell"),
        P(),
    )
    out_specs = P("sensor", "cell")
    return jax.shard_map(
        on_device, mesh=mesh, in_specs=in_specs, out_specs=out_specs, check_vma=False
    )
```

profile of v0, /device:TPU:13, one launch (start us, length us, event | category | flops | bytes accessed | tf_op | source)
XLA Modules:
  0.0 54.8 jit_solution(11274001108198222898)
XLA Ops:
  0.0 0.9 %slice.60 = f32[64,2]{1,0:T(8,128)S(1)} slice(f32[64,512]{1,0:T(8,128)} %bitcast.150), slice={[0:64], [510:512]} | slice | bytes 1024 | tf_op jit(solution)/shard_map/slice | solution.py:74
  0.9 3.7 %collective-permute-start = (f32[64,2]{1,0:T(8,128)S(1)}, f32[64,2]{1,0:T(8,128)S(1)}, u32[]{:S(2)}, u32[]{:S(2)}) collective-permute-start(f32[64,2]{1,0:T(8,128)S(1)} %slice.60), channel_id=1, source_target_pairs={{0,1},{1,2},{2,3},{3,4},{4,5},{5,6},{6,7},{7,8},{8,9},{9,10},{10,1... | collective-permute-start | bytes 1544 | tf_op jit(solution)/shard_map/ppermute | solution.py:15
  4.7 0.7 %copy-done.8 = s32[1,512]{1,0:T(1,128)S(1)} copy-done((s32[1,512]{1,0:T(1,128)S(1)}, s32[1,512]{1,0:T(1,128)}, u32[]{:S(2)}) %copy-start.8) | copy-done | bytes 2072
  5.4 1.0 %gather_fusion = f32[512,64]{1,0:T(8,128)S(1)} fusion(f32[64,256]{0,1:T(8,128)S(1)} %copy.25, s32[1024]{0:T(1024)S(1)} %pad_clamp_fusion), kind=kCustom, calls=%fused_computation | custom fusion | bytes 264192 | tf_op jit(solution)/shard_map/jit(_take)/gather | solution.py:89
  7.3 0.2 fusion.3
  7.7 0.7 %copy-done.2 = f32[1,64,512]{2,1,0:T(8,128)S(1)} copy-done((f32[1,64,512]{2,1,0:T(8,128)S(1)}, f32[1,64,512]{2,1,0:T(8,128)}, u32[]{:S(2)}) %copy-start.2) | copy-done | bytes 131096
  8.6 0.7 %fusion.19 = f32[64,512]{1,0:T(8,128)S(1)} fusion(f32[64,512]{1,0:T(8,128)S(1)} %bitcast.152, f32[64,2]{1,0:T(8,128)S(1)} %collective-permute-done, f32[64,512]{1,0:T(8,128)S(1)} %fusion.17, f32[1,64,192]{2,1,0:T(8,128)S(1)} %copy-done), kind=kOutput, calls=%fused_computation.34 | convolution fusion | flops 77889536 | bytes 442880 | tf_op jit(solution)/shard_map/dot_general | solution.py:84
  9.3 0.3 fusion
  9.6 0.7 %copy-done.7 = f32[1,512]{1,0:T(1,128)S(1)} copy-done((f32[1,512]{1,0:T(1,128)S(1)}, f32[1,512]{1,0:T(1,128)}, u32[]{:S(2)}) %copy-start.7) | copy-done | bytes 2072
  10.3 4.1 %scatter_custom_fusion = f32[256]{0:T(256)S(1)} fusion(s32[512]{0:T(512)S(1)} %bitcast.160, f32[512]{0:T(512)S(1)} %fusion.44, f32[]{:T(128)} %constant.40.clone.1), kind=kCustom, calls=%fused_computation.97 | custom fusion | flops 512 | bytes 1028 | tf_op jit(solution)/shard_map/scatter-max | solution.py:94
  14.4 3.5 %gather_fusion.1 = f32[512]{0:T(512)S(1)} fusion(f32[256]{0:T(256)S(1)} %broadcast_maximum_fusion, s32[1024]{0:T(1024)S(1)} %pad_clamp_fusion), kind=kCustom, calls=%fused_computation.1 | custom fusion | bytes 6144 | tf_op jit(solution)/shard_map/gather | solution.py:96
  17.9 0.3 convolution_multiply_fusion.1
  18.3 2.3 %scatter_custom_fusion.1 = f32[256,64]{1,0:T(8,128)S(1)} fusion(s32[512]{0:T(512)S(1)} %bitcast.161, f32[512,64]{1,0:T(8,128)S(1)} %copy.27, f32[]{:T(128)} %constant.49.clone.1), kind=kCustom, calls=%fused_computation.60 | custom fusion | flops 32768 | bytes 65540 | tf_op jit(solution)/shard_map/scatter-add | solution.py:98
  20.7 3.8 %all-gather = f32[128,256]{1,0:T(8,128)S(1)} all-gather(f32[64,256]{1,0:T(8,128)S(1)} %bitcast.149), channel_id=2, replica_groups=mesh['sensor'=2,'cell'=16] {'sensor'}, dimensions={0}, use_global_device_ids=true | all-gather | bytes 196608 | tf_op jit(solution)/shard_map/all_gather | solution.py:19
  24.6 4.1 %scatter_custom_fusion.2 = f32[256]{0:T(256)S(1)} fusion(s32[512]{0:T(512)S(1)} %bitcast.162, f32[512]{0:T(512)S(1)} %get-tuple-element.30, f32[]{:T(128)} %constant.49.clone.1), kind=kCustom, calls=%fused_computation.93 | custom fusion | flops 512 | bytes 1028 | tf_op jit(solution)/shard_map/scatter-add | solution.py:97
  28.6 3.1 %all-gather.4 = f32[2,1,256]{2,1,0:T(1,128)S(1)} all-gather(f32[1,1,256]{2,1,0:T(1,128)S(1)} %bitcast.170), channel_id=4, replica_groups=mesh['sensor'=2,'cell'=16] {'sensor'}, dimensions={0}, use_global_device_ids=true | all-gather | bytes 3072 | tf_op jit(solution)/shard_map/all_gather | solution.py:19
  31.7 3.1 %all-gather.3 = f32[2,1,256]{2,1,0:T(1,128)S(1)} all-gather(f32[1,1,256]{2,1,0:T(1,128)S(1)} %bitcast.145), channel_id=3, replica_groups=mesh['sensor'=2,'cell'=16] {'sensor'}, dimensions={0}, use_global_device_ids=true | all-gather | bytes 3072 | tf_op jit(solution)/shard_map/all_gather | solution.py:19
  35.0 6.0 %collective-permute-start.1 = (f32[64,256]{1,0:T(8,128)S(1)}, f32[64,256]{1,0:T(8,128)S(1)}, u32[]{:S(2)}, u32[]{:S(2)}) collective-permute-start(f32[64,256]{1,0:T(8,128)S(1)} %fusion.2), channel_id=1, source_target_pairs={{0,1},{1,2},{2,3},{3,4},{4,5},{5,6},{6,7},{7,8},{8,9},{9,10},{10,1... | collective-permute-start | bytes 196616 | tf_op jit(solution)/shard_map/ppermute | solution.py:33
  41.1 1.9 %collective-permute-start.2 = (f32[64,256]{1,0:T(8,128)S(1)}, f32[64,256]{1,0:T(8,128)S(1)}, u32[]{:S(2)}, u32[]{:S(2)}) collective-permute-start(f32[64,256]{1,0:T(8,128)S(1)} %fusion.2), channel_id=1, source_target_pairs={{1,0},{2,1},{3,2},{4,3},{5,4},{6,5},{7,6},{8,7},{9,8},{10,9},{11,1... | collective-permute-start | bytes 196616 | tf_op jit(solution)/shard_map/ppermute | solution.py:34
  43.0 0.3 fusion.42
  43.3 4.2 %collective-permute-done.2 = f32[64,256]{1,0:T(8,128)S(1)} collective-permute-done((f32[64,256]{1,0:T(8,128)S(1)}, f32[64,256]{1,0:T(8,128)S(1)}, u32[]{:S(2)}, u32[]{:S(2)}) %collective-permute-start.2) | collective-permute-done | bytes 65568 | tf_op jit(solution)/shard_map/ppermute | solution.py:34
  47.8 5.5 %gather_fusion.2 = f32[2048,64]{1,0:T(8,128)S(1)} fusion(f32[64,768]{0,1:T(8,128)S(1)} %copy.29, s32[2048]{0:T(1024)S(1)} %broadcast_clamp_fusion), kind=kCustom, calls=%fused_computation.2 | custom fusion | bytes 1056768 | tf_op jit(solution)/shard_map/jit(_take)/gather | solution.py:114
  53.2 0.3 copy.30
  53.6 1.3 %fusion.4 = f32[32,256]{1,0:T(8,128)} fusion(f32[32,256]{1,0:T(8,128)S(1)} %fusion.42, f32[8,256,64]{1,2,0:T(8,128)S(1)} %copy.30, f32[64,9,64]{0,2,1:T(8,128)S(1)} %bitcast.148, s32[]{:T(128)S(6)} %select_n.43, pred[8,256]{1,0:T(8,128)(4,1)S(1)} %compare_and_fusion), kind=kOutput, calls=%fused_computation.15 | convolution fusion | flops 50470912 | bytes 739332 | tf_op jit(solution)/shard_map/oki,ikc->oc/dot_general | solution.py:53
  (39 shorter events, 1.2 us)
Async XLA Ops:
  0.0 8.6 %copy-start = (f32[1,64,192]{2,1,0:T(8,128)S(1)}, f32[1,64,192]{2,1,0:T(8,128)}, u32[]{:S(2)}) copy-start(f32[1,64,192]{2,1,0:T(8,128)} %param.11) | copy-start | bytes 147460
  0.0 5.3 %copy-start.1 = (f32[64,256]{1,0:T(8,128)S(1)}, f32[64,256]{1,0:T(8,128)}, u32[]{:S(2)}) copy-start(f32[64,256]{1,0:T(8,128)} %param.14) | copy-start | bytes 196612
  0.0 4.6 %copy-start.6 = (s32[8,256]{1,0:T(8,128)S(1)}, s32[8,256]{1,0:T(8,128)}, u32[]{:S(2)}) copy-start(s32[8,256]{1,0:T(8,128)} %param.18) | copy-start | bytes 24580
  0.9 6.8 %collective-permute-start = (f32[64,2]{1,0:T(8,128)S(1)}, f32[64,2]{1,0:T(8,128)S(1)}, u32[]{:S(2)}, u32[]{:S(2)}) collective-permute-start(f32[64,2]{1,0:T(8,128)S(1)} %slice.60), channel_id=1, source_target_pairs={{0,1},{1,2},{2,3},{3,4},{4,5},{5,6},{6,7},{7,8},{8,9},{9,10},{10,1... | collective-permute-start | bytes 1544 | tf_op jit(solution)/shard_map/ppermute | solution.py:15
  4.6 0.7 %copy-start.8 = (s32[1,512]{1,0:T(1,128)S(1)}, s32[1,512]{1,0:T(1,128)}, u32[]{:S(2)}) copy-start(s32[1,512]{1,0:T(1,128)} %param.16) | copy-start | bytes 6148
  6.5 0.8 %copy-start.4 = (f32[64,64]{1,0:T(8,128)S(1)}, f32[64,64]{1,0:T(8,128)}, u32[]{:S(2)}) copy-start(f32[64,64]{1,0:T(8,128)} %param.12) | copy-start | bytes 49156
  6.5 1.1 %copy-start.3 = (f32[64,576]{1,0:T(8,128)S(1)}, f32[64,576]{1,0:T(8,128)}, u32[]{:S(2)}) copy-start(f32[64,576]{1,0:T(8,128)} %param.19) | copy-start | bytes 442372
  7.6 0.9 %copy-start.2 = (f32[1,64,512]{2,1,0:T(8,128)S(1)}, f32[1,64,512]{2,1,0:T(8,128)}, u32[]{:S(2)}) copy-start(f32[1,64,512]{2,1,0:T(8,128)} %param.10) | copy-start | bytes 393220
  9.6 0.7 %copy-start.7 = (f32[1,512]{1,0:T(1,128)S(1)}, f32[1,512]{1,0:T(1,128)}, u32[]{:S(2)}) copy-start(f32[1,512]{1,0:T(1,128)} %param.15) | copy-start | bytes 6148
  14.4 3.6 %copy-start.5 = (f32[64,64]{1,0:T(8,128)S(1)}, f32[64,64]{1,0:T(8,128)}, u32[]{:S(2)}) copy-start(f32[64,64]{1,0:T(8,128)} %param.13) | copy-start | bytes 49156
  35.0 8.3 %collective-permute-start.1 = (f32[64,256]{1,0:T(8,128)S(1)}, f32[64,256]{1,0:T(8,128)S(1)}, u32[]{:S(2)}, u32[]{:S(2)}) collective-permute-start(f32[64,256]{1,0:T(8,128)S(1)} %fusion.2), channel_id=1, source_target_pairs={{0,1},{1,2},{2,3},{3,4},{4,5},{5,6},{6,7},{7,8},{8,9},{9,10},{10,1... | collective-permute-start | bytes 196616 | tf_op jit(solution)/shard_map/ppermute | solution.py:33
  41.1 6.5 %collective-permute-start.2 = (f32[64,256]{1,0:T(8,128)S(1)}, f32[64,256]{1,0:T(8,128)S(1)}, u32[]{:S(2)}, u32[]{:S(2)}) collective-permute-start(f32[64,256]{1,0:T(8,128)S(1)} %fusion.2), channel_id=1, source_target_pairs={{1,0},{2,1},{3,2},{4,3},{5,4},{6,5},{7,6},{8,7},{9,8},{10,9},{11,1... | collective-permute-start | bytes 196616 | tf_op jit(solution)/shard_map/ppermute | solution.py:34
where the time goes:
time: 55.2 us; the launch traced here: 54.8 us
  local copies, waits for them, and re-layouts  14 us (25%)
  starting transfers between devices  11.7 us (21%)
  other arithmetic  10.6 us (19%)
  blocking collectives  10 us (18%)
  waiting for transfers between devices  4.24 us (8%)
  matrix products  3.26 us (6%)
  between operations  0.99 us (2%)
    all_gather x3, blocking collectives, combined_all(): pieces = jax.tree.map(lambda part: lax.all_gather(part, axis), value)  10 us
    ppermute x1, starting transfers between devices, extended_2(): before = lax.ppermute(last, axis, up)  6.04 us
    gather x2, local copies, waits for them, and re-layouts, on_device(): gathered = jnp.take(extended, neighbours - range_start + cell_count, axis=1)  5.77 us
    ppermute x1, waiting for transfers between devices, extended_2(): after = lax.ppermute(initial, axis, down)  4.24 us
    scatter-add x1, other arithmetic, on_device(): local_total = jax.ops.segment_sum(weights_exp, local_cell, cell_count)  4.08 us
    another operation x1, other arithmetic, on_device(): jax.ops.segment_max(jnp.where(valid, score, -jnp.inf), local_cell, cell_c...  4.08 us
    ppermute x1, starting transfers between devices, passed_along(): lax.ppermute(value, axis, [(source, source + steps) for source in range(i...  3.7 us
    gather x1, local copies, waits for them, and re-layouts, on_device(): weights_exp = jnp.where(valid, jnp.exp(score - local_peak[local_cell]), 0.0)  3.51 us
  transfers between devices with their start and end apart: 3, of which 1 were waited for; matrix products, arithmetic and copies ran while one was open for 4% of the time, Pallas kernels for 0%

commit v1 on v0

v1 whole, which is shorter than its diff:
```python
import functools
import math

import jax
import jax.numpy as jnp
from jax import lax
from jax.experimental import pallas as pl
from jax.experimental.pallas import tpu as pltpu
from jax.sharding import PartitionSpec as P

FLOOR = -1e30
LANES = 128
ROWS = 8
EXACT = lax.Precision.HIGHEST
CLOSE = lax.Precision.HIGH


def dot(left, right, contract, precision=EXACT):
    return lax.dot_general(
        left,
        right,
        (contract, ((), ())),
        precision=precision,
        preferred_element_type=jnp.float32,
    )


NN = ((1,), (0,))
NT = ((1,), (1,))
TN = ((0,), (0,))


def gelu(x):
    return 0.5 * x * (1.0 + lax.erf(x * math.sqrt(0.5)))


def column_of(row):
    return jnp.transpose(jnp.broadcast_to(row, (LANES, row.shape[1])))


def masked_scores(encoded, key_query, cell_row, quality_row):
    cells = key_query.shape[1]
    cell_column = column_of(cell_row)
    quality_column = column_of(quality_row)
    score = dot(encoded, key_query, TN)
    lane = lax.broadcasted_iota(jnp.int32, cell_column.shape, 1).astype(jnp.float32)
    parts = []
    for start in range(0, cells, LANES):
        mine = cell_column == lane + float(start)
        part = score[:, start : start + LANES] + quality_column
        parts.append(jnp.where(mine, part, -jnp.inf))
    return jnp.concatenate(parts, axis=1)


def stats_block(weighted, total, peak):
    place = lax.broadcasted_iota(jnp.int32, (ROWS, total.shape[1]), 0)
    tail = jnp.where(place == 0, total, jnp.where(place == 1, peak, 0.0))
    return jnp.concatenate([weighted, tail], axis=0)


def tail_kernel(swath_ref, out_ref):
    last = swath_ref[0]
    row = lax.broadcasted_iota(jnp.int32, (ROWS, LANES), 0)
    lane = lax.broadcasted_iota(jnp.int32, (ROWS, LANES), 1)
    first = ((lane == LANES - 2 + row) & (row < 2)).astype(jnp.float32)
    second = ((lane == LANES - 1) & (row == 0)).astype(jnp.float32)
    out_ref[...] = jnp.concatenate([dot(first, last, NT), dot(second, last, NT)], axis=1)


def prepare_kernel(
    swath_ref,
    enc_ref,
    key_ref,
    value_ref,
    query_ref,
    quality_ref,
    cell_ref,
    live_ref,
    near_ref,
    hp_ref,
    first_ref,
    kq_ref,
    rest_ref,
    hpv_ref,
    code_ref,
):
    sensor = lax.axis_index("sensor")
    cell = lax.axis_index("cell")
    channels, slots = swath_ref.shape[1:]
    cells = query_ref.shape[1]
    out_rows = hpv_ref.shape[0] * channels // hp_ref.shape[1]

    signal = swath_ref[0]
    one = jnp.concatenate([jnp.zeros((channels, 1), jnp.float32), signal[:, : slots - 1]], axis=1)
    two = jnp.concatenate([jnp.zeros((channels, 2), jnp.float32), signal[:, : slots - 2]], axis=1)
    stacked = jnp.concatenate([two, one, signal], axis=0)
    before = dot(enc_ref[0], stacked, NN)
    first_ref[...] = before[:, :LANES]
    encoded = gelu(before[:, LANES:])

    query = query_ref[...]
    key_query = dot(key_ref[...], query, TN) * (1.0 / math.sqrt(channels))
    kq_ref[...] = key_query
    own_score = jnp.sum(query * key_query, axis=0, keepdims=True)
    own_score = jnp.where(sensor == 0, own_score, -jnp.inf)

    place = lax.broadcasted_iota(jnp.int32, (1, slots), 1)
    cell_row = jnp.where(place < live_ref[0, 0], cell_ref[...], -1).astype(jnp.float32)
    quality_row = quality_ref[...]
    scores = [
        masked_scores(
            encoded[:, start - LANES : start],
            key_query,
            cell_row[:, start : start + LANES],
            quality_row[:, start : start + LANES],
        )
        for start in range(LANES, slots, LANES)
    ]
    peak = jnp.maximum(own_score, FLOOR)
    for score in scores:
        peak = jnp.maximum(peak, jnp.max(score, axis=0, keepdims=True))
    weight = jnp.exp(own_score - peak)
    weighted = query * weight
    weights = jnp.exp(jnp.concatenate(scores, axis=0) - peak)
    total = weight + jnp.sum(weights, axis=0, keepdims=True)
    weighted = weighted + dot(encoded, weights, NN)
    rest_ref[...] = stats_block(weighted, total, peak)

    own_hp = hp_ref[pl.ds(pl.multiple_of(sensor * out_rows, ROWS), out_rows), :]
    value = value_ref[...]
    for k in range(hp_ref.shape[1] // channels):
        part = dot(own_hp[:, k * channels : (k + 1) * channels], value, NN)
        hpv_ref[k * out_rows : (k + 1) * out_rows, :] = part

    side = math.isqrt(cells)
    shift = side.bit_length() - 1
    odd = lax.rem(cell, 2)
    offset = near_ref[...] - cell * cells
    after = cells + odd * side + lax.shift_right_arithmetic(offset - cells, shift)
    ahead = cells + (1 - odd) * side + lax.shift_right_arithmetic(offset + cells, shift)
    code_ref[...] = jnp.where(offset < 0, ahead, jnp.where(offset < cells, offset, after))


def pool_kernel(
    enc_ref,
    quality_ref,
    cell_ref,
    live_ref,
    first_ref,
    kq_ref,
    rest_ref,
    tail_a_ref,
    tail_b_ref,
    stats_ref,
    pack_a_ref,
    pack_b_ref,
):
    cell = lax.axis_index("cell")
    channels, cells = kq_ref.shape
    odd = lax.rem(cell, 2)
    tail = jnp.where(odd == 1, tail_a_ref[...], tail_b_ref[...])
    tail = jnp.where(cell == 0, 0.0, tail)
    tail = jnp.concatenate([tail, jnp.zeros((LANES - ROWS, LANES), jnp.float32)], axis=0)
    before = first_ref[...] + dot(enc_ref[0, :, : 2 * channels], tail, NT)
    encoded = gelu(before)
    place = lax.broadcasted_iota(jnp.int32, (1, LANES), 1)
    cell_row = jnp.where(place < live_ref[0, 0], cell_ref[:, :LANES], -1).astype(jnp.float32)
    score = masked_scores(encoded, kq_ref[...], cell_row, quality_ref[:, :LANES])
    rest_peak = rest_ref[channels + 1 : channels + 2, :]
    peak = jnp.maximum(rest_peak, jnp.max(score, axis=0, keepdims=True))
    factor = jnp.exp(rest_peak - peak)
    weights = jnp.exp(score - peak)
    total = rest_ref[channels : channels + 1, :] * factor + jnp.sum(weights, axis=0, keepdims=True)
    weighted = rest_ref[:channels, :] * factor + dot(encoded, weights, NN)
    stats = stats_block(weighted, total, peak)
    stats_ref[...] = stats
    side = math.isqrt(cells)
    row = lax.broadcasted_iota(jnp.int32, (2 * side, cells), 0)
    lane = lax.broadcasted_iota(jnp.int32, (2 * side, cells), 1)
    right, left = row * side + side - 1, (row - side) * side
    swapped_right, swapped_left = (row - side) * side + side - 1, row * side
    top = row < side
    pick = jnp.where(
        odd == 1,
        jnp.where(top, swapped_left, swapped_right),
        jnp.where(top, right, left),
    )
    packs = dot((lane == pick).astype(jnp.float32), stats, NT)
    wide = jnp.zeros((2 * side, LANES - packs.shape[1]), jnp.float32)
    packs = jnp.concatenate([packs, wide], axis=1)
    pack_a_ref[...] = packs[:side]
    pack_b_ref[...] = packs[side:]


def combine_kernel(own_ref, other_ref, out_ref):
    channels = own_ref.shape[0] - ROWS
    first, second = own_ref[...], other_ref[...]
    peak = jnp.maximum(first[channels + 1 : channels + 2], second[channels + 1 : channels + 2])
    first_factor = jnp.exp(first[channels + 1 : channels + 2] - peak)
    second_factor = jnp.exp(second[channels + 1 : channels + 2] - peak)
    both = first[: channels + 1] * first_factor + second[: channels + 1] * second_factor
    out_ref[...] = stats_block(both[:channels], both[channels : channels + 1], peak)


def mean_of(channels, first, second):
    first_peak, second_peak = (v[channels + 1 : channels + 2] for v in (first, second))
    peak = jnp.maximum(first_peak, second_peak)
    first_factor = jnp.exp(first_peak - peak)
    second_factor = jnp.exp(second_peak - peak)
    total = (
        first[channels : channels + 1] * first_factor
        + second[channels : channels + 1] * second_factor
    )
    return first[:channels] * (first_factor / total) + second[:channels] * (second_factor / total)


def mix_kernel(
    channels,
    own_ref,
    other_ref,
    own_a_ref,
    other_a_ref,
    own_b_ref,
    other_b_ref,
    hpv_ref,
    code_ref,
    out_ref,
):
    out_rows, cells = out_ref.shape
    pooled = mean_of(channels, own_ref[...], other_ref[...])
    halo = jnp.concatenate(
        [
            halo_mean(channels, own_a_ref[...], other_a_ref[...]),
            halo_mean(channels, own_b_ref[...], other_b_ref[...]),
        ],
        axis=0,
    )
    wide = jnp.zeros((LANES - halo.shape[0], channels), jnp.float32)
    halo = jnp.concatenate([halo, wide], axis=0)
    hpv = hpv_ref[...]
    mixed = dot(hpv, pooled, NN, CLOSE)
    edge = dot(hpv, halo, NT, CLOSE)
    sources = [mixed[:, start : start + LANES] for start in range(0, cells, LANES)] + [edge]
    for start in range(0, cells, LANES):
        total = mixed[:out_rows, start : start + LANES]
        for k in range(code_ref.shape[0]):
            code = jnp.broadcast_to(code_ref[k : k + 1, start : start + LANES], total.shape)
            lane = lax.bitwise_and(code, LANES - 1)
            rows = slice((k + 1) * out_rows, (k + 2) * out_rows)
            taken = None
            for i, source in enumerate(sources):
                here = jnp.take_along_axis(source[rows], lane, axis=1, mode="promise_in_bounds")
                taken = here if taken is None else jnp.where(code >= i * LANES, here, taken)
            total = total + taken
        out_ref[:, start : start + LANES] = total


def halo_mean(channels, first, second):
    first_peak, second_peak = (v[:, channels + 1 : channels + 2] for v in (first, second))
    peak = jnp.maximum(first_peak, second_peak)
    first_factor = jnp.exp(first_peak - peak)
    second_factor = jnp.exp(second_peak - peak)
    total = (
        first[:, channels : channels + 1] * first_factor
        + second[:, channels : channels + 1] * second_factor
    )
    return first[:, :channels] * (first_factor / total) + second[:, :channels] * (
        second_factor / total
    )


def shape_of(*shape, dtype=jnp.float32):
    return jax.ShapeDtypeStruct(shape, dtype)


def swaps(sensors, cells):
    def listed(partner):
        return [(s * cells + c, partner(s, c)) for s in range(sensors) for c in range(cells)]

    def near(flip):
        return listed(lambda s, c: (s ^ flip) * cells + (c ^ 1))

    def far(flip):
        def partner(s, c):
            if c in (0, cells - 1):
                return (s ^ 1) * cells + c
            return (s ^ flip) * cells + ((c - 1) ^ 1) + 1

        return listed(partner)

    def across(flip):
        return listed(lambda s, c: (s ^ flip) * cells + c)

    return near, far, across


def on_device(
    swath,
    enc_weight,
    key_weight,
    value_weight,
    cell_query,
    quality,
    sample_cell,
    live,
    neighbours,
    hp_weight,
):
    sensors, ranges = lax.axis_size("sensor"), lax.axis_size("cell")
    channels, slots = swath.shape[1:]
    cells = cell_query.shape[1]
    side = math.isqrt(cells)
    out_rows = channels // sensors
    stencil = hp_weight.shape[1] // channels
    vmem = pl.BlockSpec(memory_space=pltpu.VMEM)
    smem = pl.BlockSpec(memory_space=pltpu.SMEM)
    axes = ("sensor", "cell")
    near, far, across = swaps(sensors, ranges)

    tail = pl.pallas_call(
        tail_kernel,
        grid=(1,),
        in_specs=[pl.BlockSpec((1, channels, LANES), lambda i: (0, 0, slots // LANES - 1))],
        out_specs=pl.BlockSpec((ROWS, LANES), lambda i: (0, 0)),
        out_shape=shape_of(ROWS, LANES),
    )(swath)
    tail_a = lax.ppermute(tail, axes, near(0))
    tail_b = lax.ppermute(tail, axes, far(0))

    first, key_query, rest, hpv, code = pl.pallas_call(
        prepare_kernel,
        in_specs=[vmem] * 7 + [smem] + [vmem] * 2,
        out_specs=[vmem] * 5,
        out_shape=[
            shape_of(channels, LANES),
            shape_of(channels, cells),
            shape_of(channels + ROWS, cells),
            shape_of(stencil * out_rows, channels),
            shape_of(*neighbours.shape, dtype=jnp.int32),
        ],
        cost_estimate=pl.CostEstimate(
            flops=200_000_000, bytes_accessed=800_000, transcendentals=200_000
        ),
    )(
        swath,
        enc_weight,
        key_weight,
        value_weight,
        cell_query,
        quality,
        sample_cell,
        live,
        neighbours,
        hp_weight,
    )

    stats, pack_a, pack_b = pl.pallas_call(
        pool_kernel,
        in_specs=[vmem] * 3 + [smem] + [vmem] * 5,
        out_specs=[vmem] * 3,
        out_shape=[
            shape_of(channels + ROWS, cells),
            shape_of(side, LANES),
            shape_of(side, LANES),
        ],
    )(enc_weight, quality, sample_cell, live, first, key_query, rest, tail_a, tail_b)

    flip = 1
    while flip * 2 < sensors:
        others = [lax.ppermute(v, axes, across(flip)) for v in (stats, pack_a, pack_b)]
        stats = pl.pallas_call(
            combine_kernel,
            in_specs=[vmem] * 2,
            out_specs=vmem,
            out_shape=shape_of(channels + ROWS, cells),
        )(stats, others[0])
        pack_a, pack_b = [
            pl.pallas_call(
                functools.partial(combine_packs, channels),
                in_specs=[vmem] * 2,
                out_specs=vmem,
                out_shape=shape_of(side, LANES),
            )(mine, other)
            for mine, other in ((pack_a, others[1]), (pack_b, others[2]))
        ]
        flip *= 2

    other = lax.ppermute(stats, axes, across(flip))
    own_a = lax.ppermute(pack_a, axes, near(0))
    own_b = lax.ppermute(pack_b, axes, far(0))
    other_a = lax.ppermute(pack_a, axes, near(flip))
    other_b = lax.ppermute(pack_b, axes, far(flip))

    return pl.pallas_call(
        functools.partial(mix_kernel, channels),
        in_specs=[vmem] * 8,
        out_specs=vmem,
        out_shape=shape_of(out_rows, cells),
    )(stats, other, own_a, other_a, own_b, other_b, hpv, code)


def combine_packs(channels, own_ref, other_ref, out_ref):
    first, second = own_ref[...], other_ref[...]
    first_peak, second_peak = (v[:, channels + 1 : channels + 2] for v in (first, second))
    peak = jnp.maximum(first_peak, second_peak)
    both = first * jnp.exp(first_peak - peak) + second * jnp.exp(second_peak - peak)
    lane = lax.broadcasted_iota(jnp.int32, both.shape, 1)
    out_ref[...] = jnp.where(lane == channels + 1, peak, both)


def solution(mesh):
    in_specs = (
        P("sensor", None, "cell"),
        P("sensor", None, None),
        P(),
        P(),
        P(None, "cell"),
        P("sensor", "cell"),
        P("sensor", "cell"),
        P("sensor", "cell"),
        P(None, "cell"),
        P(),
    )
    out_specs = P("sensor", "cell")
    return jax.shard_map(
        on_device, mesh=mesh, in_specs=in_specs, out_specs=out_specs, check_vma=False
    )
```

time: 55.2 us -> 23 us (0.42)
  local copies, waits for them, and re-layouts: 14 us -> 1.2 us
  other arithmetic: 10.6 us -> 0 us
  Pallas kernels: 0 us -> 10.2 us
  blocking collectives: 10 us -> 0 us
  starting transfers between devices: 11.7 us -> 7.51 us
  matrix products: 3.26 us -> 0 us
  waiting for transfers between devices: 4.24 us -> 3.17 us
    gather x5 -> x0, local copies, waits for them, and re-layouts: 10.4 us -> none  [the longest x2 5.77 us: on_device(): gathered = jnp.take(extended, neighbours - range_start + cell_count, axis=1)]
    pallas_call x0 -> x4, Pallas kernels: none -> 10.2 us  [the longest x1 3.51 us: on_device(): pl.pallas_call(prepare_kernel, in_specs=[vmem] * 7 + [smem] + [vmem] * 2,...]
    all_gather x3 -> x0, blocking collectives: 10 us -> none  [combined_all(): pieces = jax.tree.map(lambda part: lax.all_gather(part, axis), value)]
    scatter-add x2 -> x0, other arithmetic: 6.37 us -> none  [the longest x1 4.08 us: on_device(): local_total = jax.ops.segment_sum(weights_exp, local_cell, cell_count)]
    ppermute x3 -> x7, starting transfers between devices: 11.7 us -> 7.51 us  [the longest x1 2.56 us: on_device(): other_b = lax.ppermute(pack_b, axes, far(flip))]
    another operation x1 -> x0, other arithmetic: 4.08 us -> none  [on_device(): jax.ops.segment_max(jnp.where(valid, score, -jnp.inf), local_cell, cell_c...]
    dot_general x7 -> x0, matrix products: 3.26 us -> none  [the longest x1 1.29 us: stencil(): jnp.einsum('oki,ikc->oc', cube[:, 1:, :], gathered, precision=highest)]
    unnamed x21 -> x14, local copies, waits for them, and re-layouts: 2.35 us -> 1.2 us
  transfers between devices with their start and end apart: 3 -> 7, of which waited for: 1 -> 2; matrix products, arithmetic and copies ran while one was open for 4% -> 0% of each run, Pallas kernels for 0% -> 15%
where the time goes in v1:
time: 23 us; the launch traced here: 22.8 us
  Pallas kernels  10.2 us (44%)
  starting transfers between devices  7.51 us (33%)
  waiting for transfers between devices  3.17 us (14%)
  local copies, waits for them, and re-layouts  1.2 us (5%)
  between operations  0.71 us (3%)
    pallas_call x1, Pallas kernels, on_device(): pl.pallas_call(prepare_kernel, in_specs=[vmem] * 7 + [smem] + [vmem] * 2,...  3.51 us
    pallas_call x1, Pallas kernels, on_device(): pl.pallas_call(pool_kernel, in_specs=[vmem] * 3 + [smem] + [vmem] * 5, ou...  2.61 us
    ppermute x1, starting transfers between devices, on_device(): other_b = lax.ppermute(pack_b, axes, far(flip))  2.56 us
    pallas_call x1, Pallas kernels, on_device(): pl.pallas_call(functools.partial(mix_kernel, channels), in_specs=[vmem] *...  2.43 us
    ppermute x1, starting transfers between devices, on_device(): tail_b = lax.ppermute(tail, axes, far(0))  1.8 us
    ppermute x1, waiting for transfers between devices, on_device(): own_b = lax.ppermute(pack_b, axes, far(0))  1.66 us
    pallas_call x1, Pallas kernels, on_device(): pl.pallas_call(tail_kernel, grid=(1,), in_specs=[pl.BlockSpec((1, channel...  1.62 us
    ppermute x1, waiting for transfers between devices, on_device(): other_b = lax.ppermute(pack_b, axes, far(flip))  1.5 us
  transfers between devices with their start and end apart: 7, of which 2 were waited for; matrix products, arithmetic and copies ran while one was open for 0% of the time, Pallas kernels for 15%

profile of v1, /device:TPU:13, one launch (start us, length us, event | category | flops | bytes accessed | tf_op | source)
XLA Modules:
  0.0 22.8 jit_solution(13099554846507510100)
XLA Ops:
  0.0 1.6 %shard_map.101 = f32[8,128]{1,0:T(8,128)} custom-call(f32[1,64,512]{2,1,0:T(8,128)} %swath_ref.3), custom_call_target="tpu_custom_call" | custom-call | tf_op jit(solution)/shard_map/pallas_call | solution.py:320
  1.6 1.8 %collective-permute-start.1 = (f32[8,128]{1,0:T(8,128)}, f32[8,128]{1,0:T(8,128)S(1)}, u32[]{:S(2)}, u32[]{:S(2)}) collective-permute-start(f32[8,128]{1,0:T(8,128)} %shard_map.101), channel_id=1, source_target_pairs={{0,16},{1,2},{2,1},{3,4},{4,3},{5,6},{6,5},{7,8},{8,7},{9,10},{10,... | collective-permute-start | bytes 12296 | tf_op jit(solution)/shard_map/ppermute | solution.py:328
  3.4 0.0 collective-permute-start
  4.1 3.5 %shard_map.100 = (f32[64,128]{1,0:T(8,128)}, f32[64,256]{1,0:T(8,128)}, f32[72,256]{1,0:T(8,128)}, f32[288,64]{1,0:T(8,128)}, s32[8,256]{1,0:T(8,128)}) custom-call(f32[1,64,512]{2,1,0:T(8,128)} %swath_ref.3, f32[1,64,192]{2,1,0:T(8,128)} %enc_ref.3, f32[64,64]{1,0:T(8,128)} %key_ref.1, f32[64,64]{1,0:T(8,128)} %value_ref.1, f32[64,256]{1,0:T(8,128)} %query_ref.1, ...), custom_call_target="tpu_custom_call" | custom-call | flops 200000000 | bytes 800000 | tf_op jit(solution)/shard_map/pallas_call | solution.py:330
  7.6 0.0 collective-permute-done.1.tail_b_ref
  7.6 0.0 collective-permute-done.tail_a_ref
  7.6 0.0 copy-start.6
  7.6 0.6 %copy-done.5 = f32[8,128]{1,0:T(8,128)} copy-done((f32[8,128]{1,0:T(8,128)}, f32[8,128]{1,0:T(8,128)S(1)}, u32[]{:S(2)}) %copy-start.5) | copy-done | bytes 4120
  8.2 0.0 copy-done.6
  8.2 2.6 %shard_map.102 = (f32[72,256]{1,0:T(8,128)}, f32[16,128]{1,0:T(8,128)}, f32[16,128]{1,0:T(8,128)}) custom-call(f32[1,64,192]{2,1,0:T(8,128)} %enc_ref.3, f32[1,512]{1,0:T(1,128)} %quality_ref.3, s32[1,512]{1,0:T(1,128)} %cell_ref.3, s32[1,1]{1,0:T(1,128)S(6)} %copy.11.live_ref, f32[64,128]{1,0:T(8,128)} %get-tuple-element.13.first_ref, ...), custom_call_target="tpu_custom_call" | custom-call | tf_op jit(solution)/shard_map/pallas_call | solution.py:357
  10.8 1.2 %collective-permute-start.2 = (f32[72,256]{1,0:T(8,128)}, f32[72,256]{1,0:T(8,128)S(1)}, u32[]{:S(2)}, u32[]{:S(2)}) collective-permute-start(f32[72,256]{1,0:T(8,128)} %get-tuple-element.16.own_ref), channel_id=1, source_target_pairs={{0,16},{1,17},{2,18},{3,19},{4,20},{5,21},{6,22},{7,23},{8,24},{9,... | collective-permute-start | bytes 221192 | tf_op jit(solution)/shard_map/ppermute | solution.py:388
  12.0 0.9 %collective-permute-start.4 = (f32[16,128]{1,0:T(8,128)}, f32[16,128]{1,0:T(8,128)S(1)}, u32[]{:S(2)}, u32[]{:S(2)}) collective-permute-start(f32[16,128]{1,0:T(8,128)} %get-tuple-element.17), channel_id=1, source_target_pairs={{0,17},{1,16},{2,19},{3,18},{4,21},{5,20},{6,23},{7,22},{8,25},{9,... | collective-permute-start | bytes 24584 | tf_op jit(solution)/shard_map/ppermute | solution.py:391
  12.9 0.0 collective-permute-start.3
  13.0 2.6 %collective-permute-start.6 = (f32[16,128]{1,0:T(8,128)}, f32[16,128]{1,0:T(8,128)S(1)}, u32[]{:S(2)}, u32[]{:S(2)}) collective-permute-start(f32[16,128]{1,0:T(8,128)} %get-tuple-element.18), channel_id=1, source_target_pairs={{0,16},{1,18},{2,17},{3,20},{4,19},{5,22},{6,21},{7,24},{8,23},{9,... | collective-permute-start | bytes 24584 | tf_op jit(solution)/shard_map/ppermute | solution.py:392
  15.5 1.0 %collective-permute-start.5 = (f32[16,128]{1,0:T(8,128)}, f32[16,128]{1,0:T(8,128)S(1)}, u32[]{:S(2)}, u32[]{:S(2)}) collective-permute-start(f32[16,128]{1,0:T(8,128)} %get-tuple-element.18), channel_id=1, source_target_pairs={{0,16},{1,2},{2,1},{3,4},{4,3},{5,6},{6,5},{7,8},{8,7},{9,10},{10,... | collective-permute-start | bytes 24584 | tf_op jit(solution)/shard_map/ppermute | solution.py:390
  16.5 0.0 collective-permute-done.4.other_a_ref
  16.5 0.0 collective-permute-done.3.own_a_ref
  16.5 0.0 copy-start.2
  16.5 1.5 %collective-permute-done.6.other_b_ref = f32[16,128]{1,0:T(8,128)S(1)} collective-permute-done((f32[16,128]{1,0:T(8,128)}, f32[16,128]{1,0:T(8,128)S(1)}, u32[]{:S(2)}, u32[]{:S(2)}) %collective-permute-start.6) | collective-permute-done | bytes 8224 | tf_op jit(solution)/shard_map/ppermute | solution.py:392
  18.0 1.7 %collective-permute-done.5.own_b_ref = f32[16,128]{1,0:T(8,128)S(1)} collective-permute-done((f32[16,128]{1,0:T(8,128)}, f32[16,128]{1,0:T(8,128)S(1)}, u32[]{:S(2)}, u32[]{:S(2)}) %collective-permute-start.5) | collective-permute-done | bytes 8224 | tf_op jit(solution)/shard_map/ppermute | solution.py:390
  19.7 0.0 collective-permute-done.2.other_ref
  19.7 0.6 %copy-done.4 = f32[16,128]{1,0:T(8,128)} copy-done((f32[16,128]{1,0:T(8,128)}, f32[16,128]{1,0:T(8,128)S(1)}, u32[]{:S(2)}) %copy-start.4) | copy-done | bytes 8216
  20.3 0.0 copy-done
  20.3 2.4 %shard_map.103 = f32[32,256]{1,0:T(8,128)} custom-call(f32[72,256]{1,0:T(8,128)} %get-tuple-element.16.own_ref, f32[72,256]{1,0:T(8,128)} %copy-done, f32[16,128]{1,0:T(8,128)} %copy-done.2, f32[16,128]{1,0:T(8,128)} %copy-done.1, f32[16,128]{1,0:T(8,128)} %copy-done.4, f32[16,128]{1,0:T(8,128)} %copy-done.3, f32[288,64]{1,0:T(8,128)} %get-tuple-element.19.hpv_ref, ...), custom_call_target="tpu_custom_call" | custom-call | tf_op jit(solution)/shard_map/pallas_call | solution.py:394
  (8 shorter events, 0.0 us)
Async XLA Ops:
  1.6 6.0 %collective-permute-start.1 = (f32[8,128]{1,0:T(8,128)}, f32[8,128]{1,0:T(8,128)S(1)}, u32[]{:S(2)}, u32[]{:S(2)}) collective-permute-start(f32[8,128]{1,0:T(8,128)} %shard_map.101), channel_id=1, source_target_pairs={{0,16},{1,2},{2,1},{3,4},{4,3},{5,6},{6,5},{7,8},{8,7},{9,10},{10,... | collective-permute-start | bytes 12296 | tf_op jit(solution)/shard_map/ppermute | solution.py:328
  3.4 4.2 %collective-permute-start = (f32[8,128]{1,0:T(8,128)}, f32[8,128]{1,0:T(8,128)S(1)}, u32[]{:S(2)}, u32[]{:S(2)}) collective-permute-start(f32[8,128]{1,0:T(8,128)} %shard_map.101), channel_id=1, source_target_pairs={{0,1},{1,0},{2,3},{3,2},{4,5},{5,4},{6,7},{7,6},{8,9},{9,8},{10,11... | collective-permute-start | bytes 12296 | tf_op jit(solution)/shard_map/ppermute | solution.py:327
  7.6 0.6 %copy-start.5 = (f32[8,128]{1,0:T(8,128)}, f32[8,128]{1,0:T(8,128)S(1)}, u32[]{:S(2)}) copy-start(f32[8,128]{1,0:T(8,128)S(1)} %collective-permute-done.1.tail_b_ref) | copy-start | bytes 12292
  7.6 0.6 %copy-start.6 = (f32[8,128]{1,0:T(8,128)}, f32[8,128]{1,0:T(8,128)S(1)}, u32[]{:S(2)}) copy-start(f32[8,128]{1,0:T(8,128)S(1)} %collective-permute-done.tail_a_ref) | copy-start | bytes 12292
  10.8 8.9 %collective-permute-start.2 = (f32[72,256]{1,0:T(8,128)}, f32[72,256]{1,0:T(8,128)S(1)}, u32[]{:S(2)}, u32[]{:S(2)}) collective-permute-start(f32[72,256]{1,0:T(8,128)} %get-tuple-element.16.own_ref), channel_id=1, source_target_pairs={{0,16},{1,17},{2,18},{3,19},{4,20},{5,21},{6,22},{7,23},{8,24},{9,... | collective-permute-start | bytes 221192 | tf_op jit(solution)/shard_map/ppermute | solution.py:388
  12.0 4.5 %collective-permute-start.4 = (f32[16,128]{1,0:T(8,128)}, f32[16,128]{1,0:T(8,128)S(1)}, u32[]{:S(2)}, u32[]{:S(2)}) collective-permute-start(f32[16,128]{1,0:T(8,128)} %get-tuple-element.17), channel_id=1, source_target_pairs={{0,17},{1,16},{2,19},{3,18},{4,21},{5,20},{6,23},{7,22},{8,25},{9,... | collective-permute-start | bytes 24584 | tf_op jit(solution)/shard_map/ppermute | solution.py:391
  12.9 3.6 %collective-permute-start.3 = (f32[16,128]{1,0:T(8,128)}, f32[16,128]{1,0:T(8,128)S(1)}, u32[]{:S(2)}, u32[]{:S(2)}) collective-permute-start(f32[16,128]{1,0:T(8,128)} %get-tuple-element.17), channel_id=1, source_target_pairs={{0,1},{1,0},{2,3},{3,2},{4,5},{5,4},{6,7},{7,6},{8,9},{9,8},{10,11... | collective-permute-start | bytes 24584 | tf_op jit(solution)/shard_map/ppermute | solution.py:389
  13.0 5.1 %collective-permute-start.6 = (f32[16,128]{1,0:T(8,128)}, f32[16,128]{1,0:T(8,128)S(1)}, u32[]{:S(2)}, u32[]{:S(2)}) collective-permute-start(f32[16,128]{1,0:T(8,128)} %get-tuple-element.18), channel_id=1, source_target_pairs={{0,16},{1,18},{2,17},{3,20},{4,19},{5,22},{6,21},{7,24},{8,23},{9,... | collective-permute-start | bytes 24584 | tf_op jit(solution)/shard_map/ppermute | solution.py:392
  15.5 4.2 %collective-permute-start.5 = (f32[16,128]{1,0:T(8,128)}, f32[16,128]{1,0:T(8,128)S(1)}, u32[]{:S(2)}, u32[]{:S(2)}) collective-permute-start(f32[16,128]{1,0:T(8,128)} %get-tuple-element.18), channel_id=1, source_target_pairs={{0,16},{1,2},{2,1},{3,4},{4,3},{5,6},{6,5},{7,8},{8,7},{9,10},{10,... | collective-permute-start | bytes 24584 | tf_op jit(solution)/shard_map/ppermute | solution.py:390
  16.5 3.2 %copy-start.1 = (f32[16,128]{1,0:T(8,128)}, f32[16,128]{1,0:T(8,128)S(1)}, u32[]{:S(2)}) copy-start(f32[16,128]{1,0:T(8,128)S(1)} %collective-permute-done.4.other_a_ref) | copy-start | bytes 24580
  16.5 3.2 %copy-start.2 = (f32[16,128]{1,0:T(8,128)}, f32[16,128]{1,0:T(8,128)S(1)}, u32[]{:S(2)}) copy-start(f32[16,128]{1,0:T(8,128)S(1)} %collective-permute-done.3.own_a_ref) | copy-start | bytes 24580
  18.0 1.7 %copy-start.3 = (f32[16,128]{1,0:T(8,128)}, f32[16,128]{1,0:T(8,128)S(1)}, u32[]{:S(2)}) copy-start(f32[16,128]{1,0:T(8,128)S(1)} %collective-permute-done.6.other_b_ref) | copy-start | bytes 24580
  19.7 0.6 %copy-start.4 = (f32[16,128]{1,0:T(8,128)}, f32[16,128]{1,0:T(8,128)S(1)}, u32[]{:S(2)}) copy-start(f32[16,128]{1,0:T(8,128)S(1)} %collective-permute-done.5.own_b_ref) | copy-start | bytes 24580
  19.7 0.6 %copy-start = (f32[72,256]{1,0:T(8,128)}, f32[72,256]{1,0:T(8,128)S(1)}, u32[]{:S(2)}) copy-start(f32[72,256]{1,0:T(8,128)S(1)} %collective-permute-done.2.other_ref) | copy-start | bytes 221188

commit v2 on v1

--- a/solution.py
+++ b/solution.py
@@ -13,6 +13,7 @@
 ROWS = 8
 EXACT = lax.Precision.HIGHEST
 CLOSE = lax.Precision.HIGH
+SMALL = pltpu.CompilerParams(vmem_limit_bytes=8 * 1024 * 1024)
 
 
 def dot(left, right, contract, precision=EXACT):
@@ -323,6 +324,7 @@
         in_specs=[pl.BlockSpec((1, channels, LANES), lambda i: (0, 0, slots // LANES - 1))],
         out_specs=pl.BlockSpec((ROWS, LANES), lambda i: (0, 0)),
         out_shape=shape_of(ROWS, LANES),
+        compiler_params=SMALL,
     )(swath)
     tail_a = lax.ppermute(tail, axes, near(0))
     tail_b = lax.ppermute(tail, axes, far(0))
@@ -338,6 +340,7 @@
             shape_of(stencil * out_rows, channels),
             shape_of(*neighbours.shape, dtype=jnp.int32),
         ],
+        compiler_params=SMALL,
         cost_estimate=pl.CostEstimate(
             flops=200_000_000, bytes_accessed=800_000, transcendentals=200_000
         ),
@@ -363,6 +366,7 @@
             shape_of(side, LANES),
             shape_of(side, LANES),
         ],
+        compiler_params=SMALL,
     )(enc_weight, quality, sample_cell, live, first, key_query, rest, tail_a, tail_b)
 
     flip = 1
@@ -373,6 +377,7 @@
             in_specs=[vmem] * 2,
             out_specs=vmem,
             out_shape=shape_of(channels + ROWS, cells),
+            compiler_params=SMALL,
         )(stats, others[0])
         pack_a, pack_b = [
             pl.pallas_call(
@@ -380,6 +385,7 @@
                 in_specs=[vmem] * 2,
                 out_specs=vmem,
                 out_shape=shape_of(side, LANES),
+                compiler_params=SMALL,
             )(mine, other)
             for mine, other in ((pack_a, others[1]), (pack_b, others[2]))
         ]
@@ -396,6 +402,7 @@
         in_specs=[vmem] * 8,
         out_specs=vmem,
         out_shape=shape_of(out_rows, cells),
+        compiler_params=SMALL,
     )(stats, other, own_a, other_a, own_b, other_b, hpv, code)
 
 

time: 23 us -> 21.7 us (0.943)
  Pallas kernels: 10.2 us -> 4.33 us
  local copies, waits for them, and re-layouts: 1.2 us -> 5.71 us
    unnamed x14 -> x20, local copies, waits for them, and re-layouts: 1.2 us -> 5.71 us
    pallas_call x1, Pallas kernels: 3.51 us -> 1.68 us  [on_device(): pl.pallas_call(prepare_kernel, in_specs=[vmem] * 7 + [smem] + [vmem] * 2,...]
    pallas_call x1, Pallas kernels: 2.61 us -> 1.01 us  [on_device(): pl.pallas_call(pool_kernel, in_specs=[vmem] * 3 + [smem] + [vmem] * 5, ou...]
    pallas_call x1, Pallas kernels: 1.62 us -> 0.26 us  [on_device(): pl.pallas_call(tail_kernel, grid=(1,), in_specs=[pl.BlockSpec((1, channel...]
    pallas_call x1, Pallas kernels: 2.43 us -> 1.38 us  [on_device(): pl.pallas_call(functools.partial(mix_kernel, channels), in_specs=[vmem] *...]
  transfers between devices with their start and end apart: 7 -> 7, of which waited for: 2 -> 2; matrix products, arithmetic and copies ran while one was open for 0% -> 0% of each run, Pallas kernels for 15% -> 8%
where the time goes in v2:
time: 21.7 us; the launch traced here: 21.3 us
  starting transfers between devices  7.59 us (35%)
  local copies, waits for them, and re-layouts  5.71 us (26%)
  Pallas kernels  4.33 us (20%)
  waiting for transfers between devices  2.97 us (14%)
  between operations  0.71 us (3%)
    unnamed x20, local copies, waits for them, and re-layouts  5.71 us
    ppermute x1, starting transfers between devices, on_device(): other_b = lax.ppermute(pack_b, axes, far(flip))  2.56 us
    ppermute x1, starting transfers between devices, on_device(): tail_b = lax.ppermute(tail, axes, far(0))  1.83 us
    pallas_call x1, Pallas kernels, on_device(): pl.pallas_call(prepare_kernel, in_specs=[vmem] * 7 + [smem] + [vmem] * 2,...  1.68 us
    ppermute x1, waiting for transfers between devices, on_device(): own_b = lax.ppermute(pack_b, axes, far(0))  1.66 us
    pallas_call x1, Pallas kernels, on_device(): pl.pallas_call(functools.partial(mix_kernel, channels), in_specs=[vmem] *...  1.38 us
    ppermute x1, waiting for transfers between devices, on_device(): other_b = lax.ppermute(pack_b, axes, far(flip))  1.3 us
    ppermute x1, starting transfers between devices, on_device(): other = lax.ppermute(stats, axes, across(flip))  1.26 us
  transfers between devices with their start and end apart: 7, of which 2 were waited for; matrix products, arithmetic and copies ran while one was open for 0% of the time, Pallas kernels for 8%

profile of v2, /device:TPU:13, one launch (start us, length us, event | category | flops | bytes accessed | tf_op | source)
XLA Modules:
  0.0 21.3 jit_solution(81122498274886300)
XLA Ops:
  0.0 0.9 %copy-done = f32[1,64,512]{2,1,0:T(8,128)S(1)} copy-done((f32[1,64,512]{2,1,0:T(8,128)S(1)}, f32[1,64,512]{2,1,0:T(8,128)}, u32[]{:S(2)}) %copy-start) | copy-done | bytes 131096
  0.9 0.3 %shard_map.101 = f32[8,128]{1,0:T(8,128)S(1)} custom-call(f32[1,64,512]{2,1,0:T(8,128)S(1)} %copy-done), custom_call_target="tpu_custom_call" | custom-call | tf_op jit(solution)/shard_map/pallas_call | solution.py:321
  1.2 1.8 %collective-permute-start.1 = (f32[8,128]{1,0:T(8,128)S(1)}, f32[8,128]{1,0:T(8,128)S(1)}, u32[]{:S(2)}, u32[]{:S(2)}) collective-permute-start(f32[8,128]{1,0:T(8,128)S(1)} %shard_map.101), channel_id=1, source_target_pairs={{0,16},{1,2},{2,1},{3,4},{4,3},{5,6},{6,5},{7,8},{8,7},{9,10},{10,... | collective-permute-start | bytes 12296 | tf_op jit(solution)/shard_map/ppermute | solution.py:330
  3.0 0.0 collective-permute-start
  3.7 0.0 copy-start.2
  3.7 0.8 %copy-done.2 = f32[1,64,192]{2,1,0:T(8,128)S(1)} copy-done((f32[1,64,192]{2,1,0:T(8,128)S(1)}, f32[1,64,192]{2,1,0:T(8,128)}, u32[]{:S(2)}) %copy-start.2) | copy-done | bytes 49176
  4.5 0.9 %copy-done.5 = f32[64,576]{1,0:T(8,128)S(1)} copy-done((f32[64,576]{1,0:T(8,128)S(1)}, f32[64,576]{1,0:T(8,128)}, u32[]{:S(2)}) %copy-start.5) | copy-done | bytes 147480
  5.4 0.8 %copy-done.6 = f32[64,256]{1,0:T(8,128)S(1)} copy-done((f32[64,256]{1,0:T(8,128)S(1)}, f32[64,256]{1,0:T(8,128)}, u32[]{:S(2)}) %copy-start.6) | copy-done | bytes 65560
  6.3 0.8 %copy-done.7 = f32[64,64]{1,0:T(8,128)S(1)} copy-done((f32[64,64]{1,0:T(8,128)S(1)}, f32[64,64]{1,0:T(8,128)}, u32[]{:S(2)}) %copy-start.7) | copy-done | bytes 16408
  7.0 0.8 %copy-done.8 = f32[64,64]{1,0:T(8,128)S(1)} copy-done((f32[64,64]{1,0:T(8,128)S(1)}, f32[64,64]{1,0:T(8,128)}, u32[]{:S(2)}) %copy-start.8) | copy-done | bytes 16408
  7.8 0.7 %copy-done.9 = s32[8,256]{1,0:T(8,128)S(1)} copy-done((s32[8,256]{1,0:T(8,128)S(1)}, s32[8,256]{1,0:T(8,128)}, u32[]{:S(2)}) %copy-start.9) | copy-done | bytes 8216
  8.5 1.7 %shard_map.100 = (f32[64,128]{1,0:T(8,128)S(1)}, f32[64,256]{1,0:T(8,128)S(1)}, f32[72,256]{1,0:T(8,128)S(1)}, f32[288,64]{1,0:T(8,128)S(1)}, s32[8,256]{1,0:T(8,128)S(1)}) custom-call(f32[1,64,512]{2,1,0:T(8,128)S(1)} %copy-done.1, f32[1,64,192]{2,1,0:T(8,128)S(1)} %copy-done.2, f32[64,64]{1,0:T(8,128)S(1)} %copy-done.7, f32[64,64]{1,0:T(8,128)S(1)} %copy-done.8, ...), custom_call_target="tpu_custom_call" | custom-call | flops 200000000 | bytes 800000 | tf_op jit(solution)/shard_map/pallas_call | solution.py:332
  10.2 0.0 collective-permute-done.1.tail_b_ref
  10.2 0.0 collective-permute-done.tail_a_ref
  10.2 1.0 %shard_map.102 = (f32[72,256]{1,0:T(8,128)S(1)}, f32[16,128]{1,0:T(8,128)S(1)}, f32[16,128]{1,0:T(8,128)S(1)}) custom-call(f32[1,64,192]{2,1,0:T(8,128)S(1)} %copy-done.2, f32[1,512]{1,0:T(1,128)S(1)} %copy-done.3, s32[1,512]{1,0:T(1,128)S(1)} %copy-done.4, s32[1,1]{1,0:T(1,128)S(6)} %copy.11.live_ref, f32[64,128]{1,0:T(8,128)S(1)} %get-tuple-element.13.first_ref, ...), custom_call_target="tpu_custom_call" | custom-call | tf_op jit(solution)/shard_map/pallas_call | solution.py:360
  11.2 1.3 %collective-permute-start.2 = (f32[72,256]{1,0:T(8,128)S(1)}, f32[72,256]{1,0:T(8,128)S(1)}, u32[]{:S(2)}, u32[]{:S(2)}) collective-permute-start(f32[72,256]{1,0:T(8,128)S(1)} %get-tuple-element.16.own_ref), channel_id=1, source_target_pairs={{0,16},{1,17},{2,18},{3,19},{4,20},{5,21},{6,22},{7,23},{8,24},{9,... | collective-permute-start | bytes 221192 | tf_op jit(solution)/shard_map/ppermute | solution.py:394
  12.5 0.9 %collective-permute-start.4 = (f32[16,128]{1,0:T(8,128)S(1)}, f32[16,128]{1,0:T(8,128)S(1)}, u32[]{:S(2)}, u32[]{:S(2)}) collective-permute-start(f32[16,128]{1,0:T(8,128)S(1)} %get-tuple-element.17), channel_id=1, source_target_pairs={{0,17},{1,16},{2,19},{3,18},{4,21},{5,20},{6,23},{7,22},{8,25},{9,... | collective-permute-start | bytes 24584 | tf_op jit(solution)/shard_map/ppermute | solution.py:397
  13.4 0.0 collective-permute-start.3
  13.4 2.6 %collective-permute-start.6 = (f32[16,128]{1,0:T(8,128)S(1)}, f32[16,128]{1,0:T(8,128)S(1)}, u32[]{:S(2)}, u32[]{:S(2)}) collective-permute-start(f32[16,128]{1,0:T(8,128)S(1)} %get-tuple-element.18), channel_id=1, source_target_pairs={{0,16},{1,18},{2,17},{3,20},{4,19},{5,22},{6,21},{7,24},{8,23},{9,... | collective-permute-start | bytes 24584 | tf_op jit(solution)/shard_map/ppermute | solution.py:398
  16.0 1.0 %collective-permute-start.5 = (f32[16,128]{1,0:T(8,128)S(1)}, f32[16,128]{1,0:T(8,128)S(1)}, u32[]{:S(2)}, u32[]{:S(2)}) collective-permute-start(f32[16,128]{1,0:T(8,128)S(1)} %get-tuple-element.18), channel_id=1, source_target_pairs={{0,16},{1,2},{2,1},{3,4},{4,3},{5,6},{6,5},{7,8},{8,7},{9,10},{10,... | collective-permute-start | bytes 24584 | tf_op jit(solution)/shard_map/ppermute | solution.py:396
  17.0 0.0 collective-permute-done.3.own_a_ref
  17.0 1.3 %collective-permute-done.6.other_b_ref = f32[16,128]{1,0:T(8,128)S(1)} collective-permute-done((f32[16,128]{1,0:T(8,128)S(1)}, f32[16,128]{1,0:T(8,128)S(1)}, u32[]{:S(2)}, u32[]{:S(2)}) %collective-permute-start.6) | collective-permute-done | bytes 8224 | tf_op jit(solution)/shard_map/ppermute | solution.py:398
  18.3 1.7 %collective-permute-done.5.own_b_ref = f32[16,128]{1,0:T(8,128)S(1)} collective-permute-done((f32[16,128]{1,0:T(8,128)S(1)}, f32[16,128]{1,0:T(8,128)S(1)}, u32[]{:S(2)}, u32[]{:S(2)}) %collective-permute-start.5) | collective-permute-done | bytes 8224 | tf_op jit(solution)/shard_map/ppermute | solution.py:396
  19.9 1.4 %shard_map.103 = f32[32,256]{1,0:T(8,128)} custom-call(f32[72,256]{1,0:T(8,128)S(1)} %get-tuple-element.16.own_ref, f32[72,256]{1,0:T(8,128)S(1)} %collective-permute-done.2.other_ref, f32[16,128]{1,0:T(8,128)S(1)} %collective-permute-done.3.own_a_ref, f32[16,128]{1,0:T(8,128)S(1)} %collective-permute-done.4.other_a_ref, ...), custom_call_target="tpu_custom_call" | custom-call | tf_op jit(solution)/shard_map/pallas_call | solution.py:400
  (14 shorter events, 0.0 us)
Async XLA Ops:
  0.0 0.9 %copy-start = (f32[1,64,512]{2,1,0:T(8,128)S(1)}, f32[1,64,512]{2,1,0:T(8,128)}, u32[]{:S(2)}) copy-start(f32[1,64,512]{2,1,0:T(8,128)} %swath_ref.3) | copy-start | bytes 393220
  0.9 2.7 %copy-start.1 = (f32[1,64,512]{2,1,0:T(8,128)S(1)}, f32[1,64,512]{2,1,0:T(8,128)}, u32[]{:S(2)}) copy-start(f32[1,64,512]{2,1,0:T(8,128)} %swath_ref.3) | copy-start | bytes 393220
  0.9 2.8 %copy-start.3 = (f32[1,512]{1,0:T(1,128)S(1)}, f32[1,512]{1,0:T(1,128)}, u32[]{:S(2)}) copy-start(f32[1,512]{1,0:T(1,128)} %quality_ref.3) | copy-start | bytes 6148
  0.9 2.8 %copy-start.4 = (s32[1,512]{1,0:T(1,128)S(1)}, s32[1,512]{1,0:T(1,128)}, u32[]{:S(2)}) copy-start(s32[1,512]{1,0:T(1,128)} %cell_ref.3) | copy-start | bytes 6148
  1.2 9.0 %collective-permute-start.1 = (f32[8,128]{1,0:T(8,128)S(1)}, f32[8,128]{1,0:T(8,128)S(1)}, u32[]{:S(2)}, u32[]{:S(2)}) collective-permute-start(f32[8,128]{1,0:T(8,128)S(1)} %shard_map.101), channel_id=1, source_target_pairs={{0,16},{1,2},{2,1},{3,4},{4,3},{5,6},{6,5},{7,8},{8,7},{9,10},{10,... | collective-permute-start | bytes 12296 | tf_op jit(solution)/shard_map/ppermute | solution.py:330
  3.0 7.2 %collective-permute-start = (f32[8,128]{1,0:T(8,128)S(1)}, f32[8,128]{1,0:T(8,128)S(1)}, u32[]{:S(2)}, u32[]{:S(2)}) collective-permute-start(f32[8,128]{1,0:T(8,128)S(1)} %shard_map.101), channel_id=1, source_target_pairs={{0,1},{1,0},{2,3},{3,2},{4,5},{5,4},{6,7},{7,6},{8,9},{9,8},{10,11... | collective-permute-start | bytes 12296 | tf_op jit(solution)/shard_map/ppermute | solution.py:329
  3.7 0.8 %copy-start.2 = (f32[1,64,192]{2,1,0:T(8,128)S(1)}, f32[1,64,192]{2,1,0:T(8,128)}, u32[]{:S(2)}) copy-start(f32[1,64,192]{2,1,0:T(8,128)} %enc_ref.3) | copy-start | bytes 147460
  4.5 0.9 %copy-start.5 = (f32[64,576]{1,0:T(8,128)S(1)}, f32[64,576]{1,0:T(8,128)}, u32[]{:S(2)}) copy-start(f32[64,576]{1,0:T(8,128)} %hp_ref.1) | copy-start | bytes 442372
  5.4 0.8 %copy-start.6 = (f32[64,256]{1,0:T(8,128)S(1)}, f32[64,256]{1,0:T(8,128)}, u32[]{:S(2)}) copy-start(f32[64,256]{1,0:T(8,128)} %query_ref.1) | copy-start | bytes 196612
  6.3 0.8 %copy-start.7 = (f32[64,64]{1,0:T(8,128)S(1)}, f32[64,64]{1,0:T(8,128)}, u32[]{:S(2)}) copy-start(f32[64,64]{1,0:T(8,128)} %key_ref.1) | copy-start | bytes 49156
  7.0 0.8 %copy-start.8 = (f32[64,64]{1,0:T(8,128)S(1)}, f32[64,64]{1,0:T(8,128)}, u32[]{:S(2)}) copy-start(f32[64,64]{1,0:T(8,128)} %value_ref.1) | copy-start | bytes 49156
  7.8 0.7 %copy-start.9 = (s32[8,256]{1,0:T(8,128)S(1)}, s32[8,256]{1,0:T(8,128)}, u32[]{:S(2)}) copy-start(s32[8,256]{1,0:T(8,128)} %near_ref.1) | copy-start | bytes 24580
  11.2 8.7 %collective-permute-start.2 = (f32[72,256]{1,0:T(8,128)S(1)}, f32[72,256]{1,0:T(8,128)S(1)}, u32[]{:S(2)}, u32[]{:S(2)}) collective-permute-start(f32[72,256]{1,0:T(8,128)S(1)} %get-tuple-element.16.own_ref), channel_id=1, source_target_pairs={{0,16},{1,17},{2,18},{3,19},{4,20},{5,21},{6,22},{7,23},{8,24},{9,... | collective-permute-start | bytes 221192 | tf_op jit(solution)/shard_map/ppermute | solution.py:394
  12.5 4.5 %collective-permute-start.4 = (f32[16,128]{1,0:T(8,128)S(1)}, f32[16,128]{1,0:T(8,128)S(1)}, u32[]{:S(2)}, u32[]{:S(2)}) collective-permute-start(f32[16,128]{1,0:T(8,128)S(1)} %get-tuple-element.17), channel_id=1, source_target_pairs={{0,17},{1,16},{2,19},{3,18},{4,21},{5,20},{6,23},{7,22},{8,25},{9,... | collective-permute-start | bytes 24584 | tf_op jit(solution)/shard_map/ppermute | solution.py:397
  13.4 3.6 %collective-permute-start.3 = (f32[16,128]{1,0:T(8,128)S(1)}, f32[16,128]{1,0:T(8,128)S(1)}, u32[]{:S(2)}, u32[]{:S(2)}) collective-permute-start(f32[16,128]{1,0:T(8,128)S(1)} %get-tuple-element.17), channel_id=1, source_target_pairs={{0,1},{1,0},{2,3},{3,2},{4,5},{5,4},{6,7},{7,6},{8,9},{9,8},{10,11... | collective-permute-start | bytes 24584 | tf_op jit(solution)/shard_map/ppermute | solution.py:395
  13.4 4.9 %collective-permute-start.6 = (f32[16,128]{1,0:T(8,128)S(1)}, f32[16,128]{1,0:T(8,128)S(1)}, u32[]{:S(2)}, u32[]{:S(2)}) collective-permute-start(f32[16,128]{1,0:T(8,128)S(1)} %get-tuple-element.18), channel_id=1, source_target_pairs={{0,16},{1,18},{2,17},{3,20},{4,19},{5,22},{6,21},{7,24},{8,23},{9,... | collective-permute-start | bytes 24584 | tf_op jit(solution)/shard_map/ppermute | solution.py:398
  16.0 4.0 %collective-permute-start.5 = (f32[16,128]{1,0:T(8,128)S(1)}, f32[16,128]{1,0:T(8,128)S(1)}, u32[]{:S(2)}, u32[]{:S(2)}) collective-permute-start(f32[16,128]{1,0:T(8,128)S(1)} %get-tuple-element.18), channel_id=1, source_target_pairs={{0,16},{1,2},{2,1},{3,4},{4,3},{5,6},{6,5},{7,8},{8,7},{9,10},{10,... | collective-permute-start | bytes 24584 | tf_op jit(solution)/shard_map/ppermute | solution.py:396

commit v3 on v0

v3 whole, which is shorter than its diff:
```python
import math

import jax
import jax.numpy as jnp
from jax import lax
from jax.experimental import pallas as pl
from jax.experimental.pallas import tpu as pltpu
from jax.sharding import PartitionSpec as P

FLOOR = -1e30
LANES = 128
ROWS = 8
LATE = 2
EXACT = lax.Precision.HIGHEST
CLOSE = lax.Precision.HIGH
NN = ((1,), (0,))
NT = ((1,), (1,))


def dot(left, right, contract, precision=EXACT):
    return lax.dot_general(
        left,
        right,
        (contract, ((), ())),
        precision=precision,
        preferred_element_type=jnp.float32,
    )


def iota(shape, dim):
    return lax.broadcasted_iota(jnp.int32, shape, dim)


def gelu(x):
    return 0.5 * x * (1.0 + lax.erf(x * math.sqrt(0.5)))


def widened(value, lanes=LANES):
    gap = jnp.zeros((value.shape[0], lanes - value.shape[1]), value.dtype)
    return jnp.concatenate([value, gap], axis=1)


def with_peak(block, peak, channels):
    return jnp.where(iota(block.shape, 1) == channels + 1, peak, block)


def merged(first, second, channels):
    first_peak, second_peak = (v[:, channels + 1 : channels + 2] for v in (first, second))
    peak = jnp.maximum(first_peak, second_peak)
    both = first * jnp.exp(first_peak - peak) + second * jnp.exp(second_peak - peak)
    return both, peak


def mean_of(first, second, channels):
    both, _ = merged(first, second, channels)
    return both / both[:, channels : channels + 1]


def with_late(rest, key_query, late, cell_ids, slot_cells, slot_quality, channels):
    peak = rest[:, channels + 1 : channels + 2]
    scores = []
    for j in range(LATE):
        score = jnp.sum(key_query * late[j : j + 1, :channels], axis=1, keepdims=True)
        score = score + slot_quality[:, j : j + 1]
        score = jnp.where(cell_ids == slot_cells[:, j : j + 1], score, -jnp.inf)
        peak = jnp.maximum(peak, score)
        scores.append(score)
    block = rest * jnp.exp(rest[:, channels + 1 : channels + 2] - peak)
    for j, score in enumerate(scores):
        block = block + jnp.exp(score - peak) * late[j : j + 1, :]
    return with_peak(block, peak, channels)


def load_kernel(*refs):
    count = (len(refs) - 2) // 2
    sources, targets, tail_ref, sems = refs[:count], refs[count:-2], refs[-2], refs[-1]
    copies = [
        pltpu.make_async_copy(source, target, sems.at[i])
        for i, (source, target) in enumerate(zip(sources, targets))
    ]
    for copy in copies:
        copy.start()
    copies[0].wait()
    swath_ref = targets[0]
    last = swath_ref[0, :, swath_ref.shape[2] - LANES :]
    row, lane = iota((ROWS, LANES), 0), iota((ROWS, LANES), 1)
    first = ((lane == LANES - 2 + row) & (row < 2)).astype(jnp.float32)
    second = ((lane == LANES - 1) & (row == 0)).astype(jnp.float32)
    tail_ref[...] = jnp.concatenate([dot(first, last, NT), dot(second, last, NT)], axis=1)
    for copy in copies[1:]:
        copy.wait()


def prepare_kernel(
    swath_ref,
    enc_ref,
    key_ref,
    query_ref,
    quality_ref,
    cell_ref,
    live_ref,
    late_ref,
    kq_ref,
    rest_ref,
    edge_kq_ref,
    edge_rest_ref,
    ids_ref,
):
    sensor = lax.axis_index("sensor")
    odd = lax.rem(lax.axis_index("cell"), 2)
    channels, slots = swath_ref.shape[1:]
    cells = query_ref.shape[1]
    side = math.isqrt(cells)

    signal = swath_ref[0]
    one = jnp.concatenate([jnp.zeros((channels, 1), jnp.float32), signal[:, : slots - 1]], axis=1)
    two = jnp.concatenate([jnp.zeros((channels, 2), jnp.float32), signal[:, : slots - 2]], axis=1)
    stacked = jnp.concatenate([two, one, signal], axis=0)
    before = dot(enc_ref[0], stacked, NN)
    late_ref[...] = jnp.transpose(before[:, :LANES])[:ROWS, :]
    encoded = gelu(before)

    query = jnp.transpose(query_ref[...])
    key_query = dot(query, key_ref[...], NN) * (1.0 / math.sqrt(channels))
    kq_ref[...] = key_query
    own_score = jnp.sum(query * key_query, axis=1, keepdims=True)
    own_score = jnp.where(sensor == 0, own_score, -jnp.inf)

    slot = iota((1, slots), 1)
    ids = jnp.where(slot < live_ref[0, 0], cell_ref[...], -1)
    ids_ref[...] = ids[:, :LANES]
    ids = jnp.where(slot < LATE, -1, ids)
    score = dot(key_query, encoded, NN) + quality_ref[...]
    score = jnp.where(iota((cells, slots), 0) == ids, score, -jnp.inf)
    peak = jnp.maximum(jnp.max(score, axis=1, keepdims=True), jnp.maximum(own_score, FLOOR))
    weights = jnp.exp(score - peak)
    place = iota((LANES - channels, slots), 0)
    tokens = jnp.concatenate([encoded, (place == 0).astype(jnp.float32)], axis=0)
    block = dot(weights, tokens, NT, CLOSE)
    own = widened(query)
    own = jnp.where(iota(own.shape, 1) == channels, 1.0, own)
    rest_ref[...] = with_peak(block + own * jnp.exp(own_score - peak), peak, channels)

    for ref, edge_ref in ((kq_ref, edge_kq_ref), (rest_ref, edge_rest_ref)):
        left = ref[pl.ds(0, side, stride=side), :]
        right = ref[pl.ds(side - 1, side, stride=side), :]
        edge_ref[:side, :] = jnp.where(odd == 1, left, right)
        edge_ref[side:, :] = jnp.where(odd == 1, right, left)


def edge_kernel(
    enc_ref,
    tail_a_ref,
    tail_b_ref,
    late_ref,
    ids_ref,
    quality_ref,
    kq_ref,
    rest_ref,
    edge_ref,
    tokens_ref,
):
    cell = lax.axis_index("cell")
    odd = lax.rem(cell, 2)
    channels = kq_ref.shape[1]
    side = rest_ref.shape[0] // 2
    tail = jnp.where(odd == 1, tail_a_ref[...], tail_b_ref[...])
    tail = jnp.where(cell == 0, 0.0, tail)
    before = late_ref[...] + dot(tail, enc_ref[0, :, : 2 * channels], NT)
    tokens = widened(gelu(before))
    tokens = jnp.where(iota(tokens.shape, 1) == channels, 1.0, tokens)
    tokens_ref[...] = tokens
    row = iota((2 * side, 1), 0)
    top = row < side
    at = jnp.where(top, row, row - side) * side
    at = at + jnp.where(top == (odd == 1), 0, side - 1)
    edge_ref[...] = with_late(
        rest_ref[...], kq_ref[...], tokens, at, ids_ref[...], quality_ref[:, :LANES], channels
    )


def pool_kernel(tokens_ref, ids_ref, quality_ref, kq_ref, rest_ref, stats_ref):
    cells, channels = kq_ref.shape
    stats_ref[...] = with_late(
        rest_ref[...],
        kq_ref[...],
        tokens_ref[...],
        iota((cells, 1), 0),
        ids_ref[...],
        quality_ref[:, :LANES],
        channels,
    )


def merge_kernel(channels, own_ref, other_ref, out_ref):
    both, peak = merged(own_ref[...], other_ref[...], channels)
    out_ref[...] = with_peak(both, peak, channels)


def weights_kernel(value_ref, near_ref, hp_ref, after_ref, hpv_ref, code_ref):
    del after_ref
    sensor = lax.axis_index("sensor")
    cell = lax.axis_index("cell")
    channels = value_ref.shape[0]
    cells = near_ref.shape[1]
    side = math.isqrt(cells)
    out_rows = hpv_ref.shape[0] * channels // hp_ref.shape[1]
    own_hp = hp_ref[pl.ds(pl.multiple_of(sensor * out_rows, ROWS), out_rows), :]
    value = value_ref[...]
    taps = [
        own_hp[:, k * channels : (k + 1) * channels] for k in range(hp_ref.shape[1] // channels)
    ]
    hpv_ref[...] = dot(jnp.concatenate(taps, axis=0), value, NN)

    shift = side.bit_length() - 1
    odd = lax.rem(cell, 2)
    offset = near_ref[...] - cell * cells
    after = cells + odd * side + lax.shift_right_arithmetic(offset - cells, shift)
    ahead = cells + (1 - odd) * side + lax.shift_right_arithmetic(offset + cells, shift)
    code_ref[...] = jnp.where(offset < 0, ahead, jnp.where(offset < cells, offset, after))


def edge_mean_kernel(channels, own_ref, other_ref, a_ref, b_ref):
    mean = mean_of(own_ref[...], other_ref[...], channels)
    side = a_ref.shape[0]
    a_ref[...] = mean[:side]
    b_ref[...] = mean[side:]


def picked(sources, first, code_ref, total, start, out_rows, base):
    for k in range(code_ref.shape[0]):
        code = jnp.broadcast_to(code_ref[k : k + 1, start : start + LANES], total.shape)
        lane = lax.bitwise_and(code, LANES - 1)
        rows = slice((k + base) * out_rows, (k + base + 1) * out_rows)
        taken = 0.0
        for i, source in enumerate(sources, first):
            here = jnp.take_along_axis(source[rows], lane, axis=1, mode="promise_in_bounds")
            taken = jnp.where(lax.shift_right_logical(code, 7) == i, here, taken)
        total = total + taken
    return total


def own_kernel(channels, own_ref, other_ref, hpv_ref, code_ref, out_ref):
    out_rows, cells = out_ref.shape
    mean = mean_of(own_ref[...], other_ref[...], channels)[:, :channels]
    mixed = dot(hpv_ref[...], mean, NT, CLOSE)
    sources = [mixed[:, start : start + LANES] for start in range(0, cells, LANES)]
    for i, start in enumerate(range(0, cells, LANES)):
        out_ref[:, start : start + LANES] = picked(
            sources, 0, code_ref, sources[i][:out_rows], start, out_rows, 1
        )


def halo_kernel(channels, b_ref, a_ref, partial_ref, hpv_ref, code_ref, out_ref):
    out_rows, cells = out_ref.shape
    halo = jnp.concatenate([a_ref[...], b_ref[...]], axis=0)[:, :channels]
    gap = jnp.zeros((LANES - halo.shape[0], channels), jnp.float32)
    halo = jnp.concatenate([halo, gap], axis=0)
    edge = dot(hpv_ref[out_rows:, :], halo, NT, CLOSE)
    for start in range(0, cells, LANES):
        out_ref[:, start : start + LANES] = picked(
            [edge],
            cells // LANES,
            code_ref,
            partial_ref[:, start : start + LANES],
            start,
            out_rows,
            0,
        )


def swaps(sensors, cells):
    def listed(partner):
        return [(s * cells + c, partner(s, c)) for s in range(sensors) for c in range(cells)]

    def far(s, c):
        if c in (0, cells - 1):
            return (s ^ 1) * cells + c
        return s * cells + ((c - 1) ^ 1) + 1

    near = listed(lambda s, c: s * cells + (c ^ 1))

    def across(flip):
        return listed(lambda s, c: (s ^ flip) * cells + c)

    return near, listed(far), across


def on_device(
    swath,
    enc_weight,
    key_weight,
    value_weight,
    cell_query,
    quality,
    sample_cell,
    live,
    neighbours,
    hp_weight,
):
    sensors, ranges = lax.axis_size("sensor"), lax.axis_size("cell")
    channels = swath.shape[1]
    cells = cell_query.shape[1]
    side = math.isqrt(cells)
    out_rows = channels // sensors
    stencil = hp_weight.shape[1] // channels
    vmem = pl.BlockSpec(memory_space=pltpu.VMEM)
    axes = ("sensor", "cell")
    near, far, across = swaps(sensors, ranges)

    def shape(*sizes, dtype=jnp.float32):
        return jax.ShapeDtypeStruct(sizes, dtype)

    def call(kernel, args, outs, cost=None, **more):
        single = not isinstance(outs, list)
        specs = dict(in_specs=[vmem] * len(args), out_specs=vmem if single else [vmem] * len(outs))
        specs.update(more)
        return pl.pallas_call(
            kernel,
            out_shape=outs,
            compiler_params=pltpu.CompilerParams(vmem_limit_bytes=8 * 1024 * 1024),
            cost_estimate=cost
            and pl.CostEstimate(flops=cost, bytes_accessed=cost // 100, transcendentals=0),
            **specs,
        )(*args)

    def bound(kernel):
        return lambda *refs: kernel(channels, *refs)

    args = [
        swath,
        enc_weight,
        key_weight,
        value_weight,
        cell_query,
        quality,
        sample_cell,
        neighbours,
        hp_weight,
    ]
    loaded = call(
        load_kernel,
        [pltpu.with_memory_space_constraint(a, pltpu.HBM) for a in args],
        [shape(*a.shape, dtype=a.dtype) for a in args] + [shape(ROWS, LANES)],
        in_specs=[pl.BlockSpec(memory_space=pltpu.HBM)] * len(args),
        scratch_shapes=[pltpu.SemaphoreType.DMA((len(args),))],
    )
    swath, enc_weight, key_weight, value_weight, cell_query = loaded[:5]
    quality, sample_cell, neighbours, hp_weight, tail = loaded[5:]
    tail_b = lax.ppermute(tail, axes, far)
    tail_a = lax.ppermute(tail, axes, near)

    late, key_query, rest, edge_kq, edge_rest, ids = call(
        prepare_kernel,
        [swath, enc_weight, key_weight, cell_query, quality, sample_cell, live],
        [
            shape(ROWS, channels),
            shape(cells, channels),
            shape(cells, LANES),
            shape(2 * side, channels),
            shape(2 * side, LANES),
            shape(1, LANES, dtype=jnp.int32),
        ],
        cost=200_000_000,
        in_specs=[vmem] * 6 + [pl.BlockSpec(memory_space=pltpu.SMEM)],
    )
    edge, tokens = call(
        edge_kernel,
        [enc_weight, tail_a, tail_b, late, ids, quality, edge_kq, edge_rest],
        [shape(2 * side, LANES), shape(ROWS, LANES)],
    )

    def merge(mine, other):
        return call(bound(merge_kernel), [mine, other], shape(*mine.shape))

    flip = 1
    stats = None
    while flip * 2 < sensors:
        if stats is None:
            stats = call(
                pool_kernel, [tokens, ids, quality, key_query, rest], shape(cells, LANES)
            )
        edge = merge(edge, lax.ppermute(edge, axes, across(flip)))
        stats = merge(stats, lax.ppermute(stats, axes, across(flip)))
        flip *= 2

    other_edge = lax.ppermute(edge, axes, across(flip))
    if stats is None:
        stats = call(pool_kernel, [tokens, ids, quality, key_query, rest], shape(cells, LANES), cost=100_000_000)
    other = lax.ppermute(stats, axes, across(flip))
    mean_a, mean_b = call(
        bound(edge_mean_kernel),
        [edge, other_edge],
        [shape(side, LANES), shape(side, LANES)],
        cost=10_000_000_000,
    )
    halo_b = lax.ppermute(mean_b, axes, far)
    halo_a = lax.ppermute(mean_a, axes, near)
    hpv, code = call(
        weights_kernel,
        [value_weight, neighbours, hp_weight, mean_a],
        [shape(stencil * out_rows, channels), shape(*neighbours.shape, dtype=jnp.int32)],
    )
    partial = call(
        bound(own_kernel), [stats, other, hpv, code], shape(out_rows, cells), cost=200_000_000
    )
    return call(
        bound(halo_kernel), [halo_b, halo_a, partial, hpv, code], shape(out_rows, cells)
    )


def solution(mesh):
    in_specs = (
        P("sensor", None, "cell"),
        P("sensor", None, None),
        P(),
        P(),
        P(None, "cell"),
        P("sensor", "cell"),
        P("sensor", "cell"),
        P("sensor", "cell"),
        P(None, "cell"),
        P(),
    )
    out_specs = P("sensor", "cell")
    return jax.shard_map(
        on_device, mesh=mesh, in_specs=in_specs, out_specs=out_specs, check_vma=False
    )
```

time: 55.2 us -> 16.9 us (0.31)
  the two profiles are of different devices: /device:TPU:13 before, /device:TPU:0 now
where the time goes in v3:
time: 16.9 us; the launch traced here: 16.7 us
  Pallas kernels  6.55 us (39%)
  starting transfers between devices  6.42 us (38%)
  waiting for transfers between devices  3.05 us (18%)
  between operations  0.72 us (4%)
    pallas_call x8, Pallas kernels, call(): pl.pallas_call(kernel, out_shape=outs, compiler_params=pltpu.CompilerPara...  6.55 us
    ppermute x1, starting transfers between devices, on_device(): tail_b = lax.ppermute(tail, axes, far)  2.56 us
    ppermute x1, waiting for transfers between devices, on_device(): other = lax.ppermute(stats, axes, across(flip))  2.07 us
    ppermute x1, starting transfers between devices, on_device(): other_edge = lax.ppermute(edge, axes, across(flip))  1.2 us
    ppermute x1, starting transfers between devices, on_device(): halo_b = lax.ppermute(mean_b, axes, far)  1.18 us
    ppermute x1, waiting for transfers between devices, on_device(): other_edge = lax.ppermute(edge, axes, across(flip))  0.97 us
    ppermute x1, starting transfers between devices, on_device(): other = lax.ppermute(stats, axes, across(flip))  0.96 us
    ppermute x1, starting transfers between devices, on_device(): tail_a = lax.ppermute(tail, axes, near)  0.52 us
  transfers between devices with their start and end apart: 6, of which 2 were waited for; matrix products, arithmetic and copies ran while one was open for 0% of the time, Pallas kernels for 22%

profile of v3, /device:TPU:0, one launch (start us, length us, event | category | flops | bytes accessed | tf_op | source)
XLA Modules:
  0.0 16.7 jit_solution(17861298394469955376)
XLA Ops:
  0.0 1.3 %shard_map.100 = (f32[1,64,512]{2,1,0:T(8,128)S(1)}, f32[1,64,192]{2,1,0:T(8,128)S(1)}, f32[64,64]{1,0:T(8,128)S(1)}, f32[64,64]{1,0:T(8,128)S(1)}, f32[64,256]{...) custom-call(f32[1,64,512]{2,1,0:T(8,128)} %refs_0_.1, ...), custom_call_target="tpu_custom_call" | custom-call | tf_op jit(solution)/shard_map/pallas_call | solution.py:318
  1.3 0.5 %collective-permute-start = (f32[8,128]{1,0:T(8,128)S(1)}, f32[8,128]{1,0:T(8,128)S(1)}, u32[]{:S(2)}, u32[]{:S(2)}) collective-permute-start(f32[8,128]{1,0:T(8,128)S(1)} %get-tuple-element.28), channel_id=1, source_target_pairs={{0,1},{1,0},{2,3},{3,2},{4,5},{5,4},{6,7},{7,6},{8,9},{9,8},{10,11... | collective-permute-start | bytes 12296 | tf_op jit(solution)/shard_map/ppermute | solution.py:351
  1.8 2.6 %collective-permute-start.1 = (f32[8,128]{1,0:T(8,128)S(1)}, f32[8,128]{1,0:T(8,128)S(1)}, u32[]{:S(2)}, u32[]{:S(2)}) collective-permute-start(f32[8,128]{1,0:T(8,128)S(1)} %get-tuple-element.28), channel_id=1, source_target_pairs={{0,16},{1,2},{2,1},{3,4},{4,3},{5,6},{6,5},{7,8},{8,7},{9,10},{10,... | collective-permute-start | bytes 12296 | tf_op jit(solution)/shard_map/ppermute | solution.py:350
  5.0 1.8 %shard_map.101 = (f32[8,64]{1,0:T(8,128)S(1)}, f32[256,64]{1,0:T(8,128)S(1)}, f32[256,128]{1,0:T(8,128)S(1)}, f32[32,64]{1,0:T(8,128)S(1)}, f32[32,128]{1,0:T(8,128)S(1)}, /*index=5*/s32[1,128]{1,0:T(1,128)S(1)}) custom-call(f32[1,64,512]{2,1,0:T(8,128)S(1)} %get-tuple-element.29.swath_ref, f32[1,64,192]{2,1,0:T(8,128)S(1)} %get-tuple-element.27.enc_ref, ...), custom_call_target="tpu_custom_call" | custom-call | flops 200000000 | bytes 2000000 | tf_op jit(solution)/shard_map/pallas_call | solution.py:318
  6.8 0.0 collective-permute-done.tail_a_ref
  6.8 0.0 collective-permute-done.1.tail_b_ref
  6.8 0.5 %shard_map.102 = (f32[32,128]{1,0:T(8,128)S(1)}, f32[8,128]{1,0:T(8,128)S(1)}) custom-call(f32[1,64,192]{2,1,0:T(8,128)S(1)} %get-tuple-element.27.enc_ref, f32[8,128]{1,0:T(8,128)S(1)} %collective-permute-done.tail_a_ref, f32[8,128]{1,0:T(8,128)S(1)} %collective-permute-done.1.tail_b_ref, f32[8,64]{1,0:T(8,128)S(1)} %get-tuple-element.34.late_ref, ...), custom_call_target="tpu_custom_call" | custom-call | tf_op jit(solution)/shard_map/pallas_call | solution.py:318
  7.4 1.2 %collective-permute-start.2 = (f32[32,128]{1,0:T(8,128)S(1)}, f32[32,128]{1,0:T(8,128)S(1)}, u32[]{:S(2)}, u32[]{:S(2)}) collective-permute-start(f32[32,128]{1,0:T(8,128)S(1)} %get-tuple-element.38.refs_0_), channel_id=1, source_target_pairs={{0,16},{1,17},{2,18},{3,19},{4,20},{5,21},{6,22},{7,23},{8,24},{9,... | collective-permute-start | bytes 49160 | tf_op jit(solution)/shard_map/ppermute | solution.py:387
  8.6 0.7 %shard_map.104.refs_0_ = f32[256,128]{1,0:T(8,128)S(1)} custom-call(f32[8,128]{1,0:T(8,128)S(1)} %get-tuple-element.41.tokens_ref, s32[1,128]{1,0:T(1,128)S(1)} %get-tuple-element.35.ids_ref, f32[1,512]{1,0:T(1,128)S(1)} %get-tuple-element.32.quality_ref, f32[256,64]{1,0:T(8,128)S(1)} %get-tuple-element.42.kq_ref, f32[256,128]{1,0:T(8,128)S(1)} %get-tuple-element.43.rest_ref), custom_call_target="tpu_custom_call" | custom-call | flops 100000000 | bytes 1000000 | tf_op jit(solution)/shard_map/pallas_call | solution.py:318
  9.2 1.0 %collective-permute-start.5 = (f32[256,128]{1,0:T(8,128)S(1)}, f32[256,128]{1,0:T(8,128)S(1)}, u32[]{:S(2)}, u32[]{:S(2)}) collective-permute-start(f32[256,128]{1,0:T(8,128)S(1)} %shard_map.104.refs_0_), channel_id=1, source_target_pairs={{0,16},{1,17},{2,18},{3,19},{4,20},{5,21},{6,22},{7,23},{8,24},{9,... | collective-permute-start | bytes 393224 | tf_op jit(solution)/shard_map/ppermute | solution.py:390
  10.2 1.0 %collective-permute-done.2.refs_1_ = f32[32,128]{1,0:T(8,128)S(1)} collective-permute-done((f32[32,128]{1,0:T(8,128)S(1)}, f32[32,128]{1,0:T(8,128)S(1)}, u32[]{:S(2)}, u32[]{:S(2)}) %collective-permute-start.2) | collective-permute-done | bytes 16416 | tf_op jit(solution)/shard_map/ppermute | solution.py:387
  11.2 0.2 shard_map.103
  11.3 1.2 %collective-permute-start.3 = (f32[16,128]{1,0:T(8,128)S(1)}, f32[16,128]{1,0:T(8,128)S(1)}, u32[]{:S(2)}, u32[]{:S(2)}) collective-permute-start(f32[16,128]{1,0:T(8,128)S(1)} %get-tuple-element.39), channel_id=1, source_target_pairs={{0,16},{1,2},{2,1},{3,4},{4,3},{5,6},{6,5},{7,8},{8,7},{9,10},{10,... | collective-permute-start | bytes 24584 | tf_op jit(solution)/shard_map/ppermute | solution.py:397
  12.5 0.0 collective-permute-start.4
  12.5 0.3 %shard_map.105 = (f32[288,64]{1,0:T(8,128)S(1)}, s32[8,256]{1,0:T(8,128)S(1)}) custom-call(f32[64,64]{1,0:T(8,128)S(1)} %get-tuple-element.44.value_ref, s32[8,256]{1,0:T(8,128)S(1)} %get-tuple-element.45.near_ref, f32[64,576]{1,0:T(8,128)S(1)} %get-tuple-element.46.hp_ref, f32[16,128]{1,0:T(8,128)S(1)} %get-tuple-element.40.after_ref), custom_call_target="tpu_custom_call" | custom-call | tf_op jit(solution)/shard_map/pallas_call | solution.py:318
  12.8 2.1 %collective-permute-done.5.refs_1_ = f32[256,128]{1,0:T(8,128)S(1)} collective-permute-done((f32[256,128]{1,0:T(8,128)S(1)}, f32[256,128]{1,0:T(8,128)S(1)}, u32[]{:S(2)}, u32[]{:S(2)}) %collective-permute-start.5) | collective-permute-done | bytes 131104 | tf_op jit(solution)/shard_map/ppermute | solution.py:390
  14.9 0.8 %shard_map.106.refs_2_ = f32[32,256]{1,0:T(8,128)S(1)} custom-call(f32[256,128]{1,0:T(8,128)S(1)} %shard_map.104.refs_0_, f32[256,128]{1,0:T(8,128)S(1)} %collective-permute-done.5.refs_1_, f32[288,64]{1,0:T(8,128)S(1)} %get-tuple-element.47.refs_2_.refs_3_, s32[8,256]{1,0:T(8,128)S(1)} %get-tuple-element.48.refs_3_.refs_4_), custom_call_target="tpu_custom_call" | custom-call | flops 200000000 | bytes 2000000 | tf_op jit(solution)/shard_map/pallas_call | solution.py:318
  15.7 0.0 collective-permute-done.3.refs_0_
  15.7 0.0 collective-permute-done.4.refs_1_
  15.7 1.0 %shard_map.107 = f32[32,256]{1,0:T(8,128)} custom-call(f32[16,128]{1,0:T(8,128)S(1)} %collective-permute-done.3.refs_0_, f32[16,128]{1,0:T(8,128)S(1)} %collective-permute-done.4.refs_1_, f32[32,256]{1,0:T(8,128)S(1)} %shard_map.106.refs_2_, f32[288,64]{1,0:T(8,128)S(1)} %get-tuple-element.47.refs_2_.refs_3_, s32[8,256]{1,0:T(8,128)S(1)} %get-tuple-element.48.refs_3_.refs_4_), custom_call_target="tpu_custom_call" | custom-call | tf_op jit(solution)/shard_map/pallas_call | solution.py:318
Async XLA Ops:
  1.3 5.5 %collective-permute-start = (f32[8,128]{1,0:T(8,128)S(1)}, f32[8,128]{1,0:T(8,128)S(1)}, u32[]{:S(2)}, u32[]{:S(2)}) collective-permute-start(f32[8,128]{1,0:T(8,128)S(1)} %get-tuple-element.28), channel_id=1, source_target_pairs={{0,1},{1,0},{2,3},{3,2},{4,5},{5,4},{6,7},{7,6},{8,9},{9,8},{10,11... | collective-permute-start | bytes 12296 | tf_op jit(solution)/shard_map/ppermute | solution.py:351
  1.8 5.0 %collective-permute-start.1 = (f32[8,128]{1,0:T(8,128)S(1)}, f32[8,128]{1,0:T(8,128)S(1)}, u32[]{:S(2)}, u32[]{:S(2)}) collective-permute-start(f32[8,128]{1,0:T(8,128)S(1)} %get-tuple-element.28), channel_id=1, source_target_pairs={{0,16},{1,2},{2,1},{3,4},{4,3},{5,6},{6,5},{7,8},{8,7},{9,10},{10,... | collective-permute-start | bytes 12296 | tf_op jit(solution)/shard_map/ppermute | solution.py:350
  7.4 3.8 %collective-permute-start.2 = (f32[32,128]{1,0:T(8,128)S(1)}, f32[32,128]{1,0:T(8,128)S(1)}, u32[]{:S(2)}, u32[]{:S(2)}) collective-permute-start(f32[32,128]{1,0:T(8,128)S(1)} %get-tuple-element.38.refs_0_), channel_id=1, source_target_pairs={{0,16},{1,17},{2,18},{3,19},{4,20},{5,21},{6,22},{7,23},{8,24},{9,... | collective-permute-start | bytes 49160 | tf_op jit(solution)/shard_map/ppermute | solution.py:387
  9.2 5.7 %collective-permute-start.5 = (f32[256,128]{1,0:T(8,128)S(1)}, f32[256,128]{1,0:T(8,128)S(1)}, u32[]{:S(2)}, u32[]{:S(2)}) collective-permute-start(f32[256,128]{1,0:T(8,128)S(1)} %shard_map.104.refs_0_), channel_id=1, source_target_pairs={{0,16},{1,17},{2,18},{3,19},{4,20},{5,21},{6,22},{7,23},{8,24},{9,... | collective-permute-start | bytes 393224 | tf_op jit(solution)/shard_map/ppermute | solution.py:390
  11.3 4.4 %collective-permute-start.3 = (f32[16,128]{1,0:T(8,128)S(1)}, f32[16,128]{1,0:T(8,128)S(1)}, u32[]{:S(2)}, u32[]{:S(2)}) collective-permute-start(f32[16,128]{1,0:T(8,128)S(1)} %get-tuple-element.39), channel_id=1, source_target_pairs={{0,16},{1,2},{2,1},{3,4},{4,3},{5,6},{6,5},{7,8},{8,7},{9,10},{10,... | collective-permute-start | bytes 24584 | tf_op jit(solution)/shard_map/ppermute | solution.py:397
  12.5 3.2 %collective-permute-start.4 = (f32[16,128]{1,0:T(8,128)S(1)}, f32[16,128]{1,0:T(8,128)S(1)}, u32[]{:S(2)}, u32[]{:S(2)}) collective-permute-start(f32[16,128]{1,0:T(8,128)S(1)} %get-tuple-element.40.after_ref), channel_id=1, source_target_pairs={{0,1},{1,0},{2,3},{3,2},{4,5},{5,4},{6,7},{7,6},{8,9},{9,8},{10,11... | collective-permute-start | bytes 24584 | tf_op jit(solution)/shard_map/ppermute | solution.py:398

commit v4 on v3

--- a/solution.py
+++ b/solution.py
@@ -91,6 +91,24 @@
         copy.wait()
 
 
+def scored(key_query, encoded, quality, ids, cells):
+    score = dot(key_query, encoded, NN) + quality
+    return jnp.where(cells == ids, score, -jnp.inf)
+
+
+def block_of(score, encoded, query, key_query, counted, channels):
+    own_score = jnp.sum(query * key_query, axis=1, keepdims=True)
+    own_score = jnp.where(counted, own_score, -jnp.inf)
+    peak = jnp.maximum(jnp.max(score, axis=1, keepdims=True), jnp.maximum(own_score, FLOOR))
+    weights = jnp.exp(score - peak)
+    place = iota((LANES - channels, encoded.shape[1]), 0)
+    tokens = jnp.concatenate([encoded, (place == 0).astype(jnp.float32)], axis=0)
+    own = widened(query)
+    own = jnp.where(iota(own.shape, 1) == channels, 1.0, own)
+    block = dot(weights, tokens, NT, CLOSE) + own * jnp.exp(own_score - peak)
+    return block, peak
+
+
 def prepare_kernel(
     swath_ref,
     enc_ref,
@@ -102,15 +120,11 @@
     late_ref,
     kq_ref,
     rest_ref,
-    edge_kq_ref,
-    edge_rest_ref,
     ids_ref,
 ):
     sensor = lax.axis_index("sensor")
-    odd = lax.rem(lax.axis_index("cell"), 2)
     channels, slots = swath_ref.shape[1:]
     cells = query_ref.shape[1]
-    side = math.isqrt(cells)
 
     signal = swath_ref[0]
     one = jnp.concatenate([jnp.zeros((channels, 1), jnp.float32), signal[:, : slots - 1]], axis=1)
@@ -123,81 +137,98 @@
     query = jnp.transpose(query_ref[...])
     key_query = dot(query, key_ref[...], NN) * (1.0 / math.sqrt(channels))
     kq_ref[...] = key_query
-    own_score = jnp.sum(query * key_query, axis=1, keepdims=True)
-    own_score = jnp.where(sensor == 0, own_score, -jnp.inf)
 
     slot = iota((1, slots), 1)
     ids = jnp.where(slot < live_ref[0, 0], cell_ref[...], -1)
     ids_ref[...] = ids[:, :LANES]
     ids = jnp.where(slot < LATE, -1, ids)
-    score = dot(key_query, encoded, NN) + quality_ref[...]
-    score = jnp.where(iota((cells, slots), 0) == ids, score, -jnp.inf)
-    peak = jnp.maximum(jnp.max(score, axis=1, keepdims=True), jnp.maximum(own_score, FLOOR))
-    weights = jnp.exp(score - peak)
-    place = iota((LANES - channels, slots), 0)
-    tokens = jnp.concatenate([encoded, (place == 0).astype(jnp.float32)], axis=0)
-    block = dot(weights, tokens, NT, CLOSE)
-    own = widened(query)
-    own = jnp.where(iota(own.shape, 1) == channels, 1.0, own)
-    rest_ref[...] = with_peak(block + own * jnp.exp(own_score - peak), peak, channels)
-
-    for ref, edge_ref in ((kq_ref, edge_kq_ref), (rest_ref, edge_rest_ref)):
-        left = ref[pl.ds(0, side, stride=side), :]
-        right = ref[pl.ds(side - 1, side, stride=side), :]
-        edge_ref[:side, :] = jnp.where(odd == 1, left, right)
-        edge_ref[side:, :] = jnp.where(odd == 1, right, left)
-
-
-def edge_kernel(
+    score = scored(key_query, encoded, quality_ref[...], ids, iota((cells, 1), 0))
+    block, peak = block_of(score, encoded, query, key_query, sensor == 0, channels)
+    rest_ref[...] = with_peak(block, peak, channels)
+
+
+def pool_kernel(
     enc_ref,
+    tail_b_ref,
     tail_a_ref,
-    tail_b_ref,
     late_ref,
     ids_ref,
     quality_ref,
     kq_ref,
     rest_ref,
-    edge_ref,
-    tokens_ref,
+    stats_ref,
+    pack_ref,
+    block_ref,
 ):
     cell = lax.axis_index("cell")
     odd = lax.rem(cell, 2)
-    channels = kq_ref.shape[1]
-    side = rest_ref.shape[0] // 2
+    cells, channels = kq_ref.shape
+    side, half = pack_ref.shape[0], cells // 2
     tail = jnp.where(odd == 1, tail_a_ref[...], tail_b_ref[...])
     tail = jnp.where(cell == 0, 0.0, tail)
     before = late_ref[...] + dot(tail, enc_ref[0, :, : 2 * channels], NT)
     tokens = widened(gelu(before))
     tokens = jnp.where(iota(tokens.shape, 1) == channels, 1.0, tokens)
-    tokens_ref[...] = tokens
-    row = iota((2 * side, 1), 0)
-    top = row < side
-    at = jnp.where(top, row, row - side) * side
-    at = at + jnp.where(top == (odd == 1), 0, side - 1)
-    edge_ref[...] = with_late(
-        rest_ref[...], kq_ref[...], tokens, at, ids_ref[...], quality_ref[:, :LANES], channels
-    )
-
-
-def pool_kernel(tokens_ref, ids_ref, quality_ref, kq_ref, rest_ref, stats_ref):
-    cells, channels = kq_ref.shape
-    stats_ref[...] = with_late(
+    block = with_late(
         rest_ref[...],
         kq_ref[...],
-        tokens_ref[...],
+        tokens,
         iota((cells, 1), 0),
         ids_ref[...],
         quality_ref[:, :LANES],
         channels,
     )
-
-
-def merge_kernel(channels, own_ref, other_ref, out_ref):
+    block_ref[...] = block
+    stats_ref[:half, :] = jnp.concatenate(
+        [block[:half, :channels], block[half:, :channels]], axis=1
+    )
+    total, peak = (block[:, channels + i : channels + i + 1] for i in range(2))
+    lane = iota((half, LANES), 1)
+    columns = jnp.where(lane == 0, total[:half], jnp.where(lane == 1, total[half:], 0.0))
+    columns = jnp.where(lane == 2, peak[:half], jnp.where(lane == 3, peak[half:], columns))
+    stats_ref[half:, :] = jnp.transpose(columns)[:ROWS, :]
+    left = block_ref[pl.ds(0, side, stride=side), :]
+    right = block_ref[pl.ds(side - 1, side, stride=side), :]
+    pack_ref[...] = jnp.where(odd == 1, right, left)
+
+
+def shares(first, second):
+    peak = jnp.maximum(first[2:4], second[2:4])
+    first_factor = jnp.exp(first[2:4] - peak)
+    second_factor = jnp.exp(second[2:4] - peak)
+    total = first[0:2] * first_factor + second[0:2] * second_factor
+    return first_factor, second_factor, total, peak
+
+
+def spread(row_pair, width):
+    square = jnp.concatenate(
+        [row_pair, jnp.zeros((LANES - row_pair.shape[0], row_pair.shape[1]), jnp.float32)], axis=0
+    )
+    columns = jnp.transpose(square)
+    lane = iota((columns.shape[0], width), 1)
+    return jnp.where(lane < width // 2, columns[:, 0:1], columns[:, 1:2])
+
+
+def merge_pack_kernel(channels, own_ref, other_ref, out_ref):
     both, peak = merged(own_ref[...], other_ref[...], channels)
     out_ref[...] = with_peak(both, peak, channels)
 
 
-def weights_kernel(value_ref, near_ref, hp_ref, after_ref, hpv_ref, code_ref):
+def merge_kernel(own_ref, other_ref, out_ref):
+    half = own_ref.shape[0] - ROWS
+    first_factor, second_factor, total, peak = shares(own_ref[half:, :], other_ref[half:, :])
+    first_sum = own_ref[:half, :] * spread(first_factor, LANES)
+    out_ref[:half, :] = first_sum + other_ref[:half, :] * spread(second_factor, LANES)
+    rest = jnp.zeros((ROWS - 4, total.shape[1]), jnp.float32)
+    out_ref[half:, :] = jnp.concatenate([total, peak, rest], axis=0)
+
+
+def halves(value):
+    high = value.astype(jnp.bfloat16)
+    return high, (value - high.astype(jnp.float32)).astype(jnp.bfloat16)
+
+
+def weights_kernel(value_ref, near_ref, hp_ref, after_ref, hpv_ref, taps_ref, code_ref):
     del after_ref
     sensor = lax.axis_index("sensor")
     cell = lax.axis_index("cell")
@@ -210,7 +241,10 @@
     taps = [
         own_hp[:, k * channels : (k + 1) * channels] for k in range(hp_ref.shape[1] // channels)
     ]
-    hpv_ref[...] = dot(jnp.concatenate(taps, axis=0), value, NN)
+    hpv = dot(jnp.concatenate(taps, axis=0), value, NN)
+    hpv_ref[...] = hpv
+    high, low = halves(hpv[out_rows:])
+    taps_ref[...] = jnp.concatenate([high, high, low], axis=1)
 
     shift = side.bit_length() - 1
     odd = lax.rem(cell, 2)
@@ -220,11 +254,16 @@
     code_ref[...] = jnp.where(offset < 0, ahead, jnp.where(offset < cells, offset, after))
 
 
-def edge_mean_kernel(channels, own_ref, other_ref, a_ref, b_ref):
-    mean = mean_of(own_ref[...], other_ref[...], channels)
-    side = a_ref.shape[0]
-    a_ref[...] = mean[:side]
-    b_ref[...] = mean[side:]
+def mean_kernel(own_ref, other_ref, mean_ref, pack_ref):
+    odd = lax.rem(lax.axis_index("cell"), 2)
+    half = mean_ref.shape[0]
+    side = half // pack_ref.shape[0]
+    first_factor, second_factor, total, _ = shares(own_ref[half:, :], other_ref[half:, :])
+    mean = own_ref[:half, :] * spread(first_factor / total, LANES)
+    mean_ref[...] = mean + other_ref[:half, :] * spread(second_factor / total, LANES)
+    left = mean_ref[pl.ds(0, half // side, stride=side), :]
+    right = mean_ref[pl.ds(side - 1, half // side, stride=side), :]
+    pack_ref[...] = jnp.where(odd == 1, left, right)
 
 
 def picked(sources, first, code_ref, total, start, out_rows, base):
@@ -240,23 +279,28 @@
     return total
 
 
-def own_kernel(channels, own_ref, other_ref, hpv_ref, code_ref, out_ref):
+def own_kernel(mean_ref, hpv_ref, code_ref, out_ref):
     out_rows, cells = out_ref.shape
-    mean = mean_of(own_ref[...], other_ref[...], channels)[:, :channels]
-    mixed = dot(hpv_ref[...], mean, NT, CLOSE)
-    sources = [mixed[:, start : start + LANES] for start in range(0, cells, LANES)]
+    mean, hpv = mean_ref[...], hpv_ref[...]
+    gap = jnp.zeros(hpv.shape, jnp.float32)
+    mixed = [
+        dot(jnp.concatenate(pair, axis=1), mean, NT, CLOSE) for pair in ((hpv, gap), (gap, hpv))
+    ]
     for i, start in enumerate(range(0, cells, LANES)):
         out_ref[:, start : start + LANES] = picked(
-            sources, 0, code_ref, sources[i][:out_rows], start, out_rows, 1
+            mixed, 0, code_ref, mixed[i][:out_rows], start, out_rows, 1
         )
 
 
-def halo_kernel(channels, b_ref, a_ref, partial_ref, hpv_ref, code_ref, out_ref):
+def halo_kernel(
+    channels, a_ref, own_b_ref, other_b_ref, partial_ref, taps_ref, code_ref, out_ref
+):
     out_rows, cells = out_ref.shape
-    halo = jnp.concatenate([a_ref[...], b_ref[...]], axis=0)[:, :channels]
+    a, b = a_ref[...], mean_of(own_b_ref[...], other_b_ref[...], channels)
+    halo = jnp.concatenate([a[:, :channels], a[:, channels:], b[:, :channels]], axis=0)
     gap = jnp.zeros((LANES - halo.shape[0], channels), jnp.float32)
-    halo = jnp.concatenate([halo, gap], axis=0)
-    edge = dot(hpv_ref[out_rows:, :], halo, NT, CLOSE)
+    high, low = halves(jnp.concatenate([halo, gap], axis=0))
+    edge = dot(taps_ref[...], jnp.concatenate([high, low, high], axis=1), NT, None)
     for start in range(0, cells, LANES):
         out_ref[:, start : start + LANES] = picked(
             [edge],
@@ -273,17 +317,20 @@
     def listed(partner):
         return [(s * cells + c, partner(s, c)) for s in range(sensors) for c in range(cells)]
 
-    def far(s, c):
-        if c in (0, cells - 1):
-            return (s ^ 1) * cells + c
-        return s * cells + ((c - 1) ^ 1) + 1
+    def far(flip):
+        def partner(s, c):
+            if c in (0, cells - 1):
+                return (s ^ 1) * cells + c
+            return (s ^ flip) * cells + ((c - 1) ^ 1) + 1
+
+        return listed(partner)
 
     near = listed(lambda s, c: s * cells + (c ^ 1))
 
     def across(flip):
         return listed(lambda s, c: (s ^ flip) * cells + c)
 
-    return near, listed(far), across
+    return near, far, across
 
 
 def on_device(
@@ -347,65 +394,59 @@
     )
     swath, enc_weight, key_weight, value_weight, cell_query = loaded[:5]
     quality, sample_cell, neighbours, hp_weight, tail = loaded[5:]
-    tail_b = lax.ppermute(tail, axes, far)
+    tail_b = lax.ppermute(tail, axes, far(0))
     tail_a = lax.ppermute(tail, axes, near)
 
-    late, key_query, rest, edge_kq, edge_rest, ids = call(
+    late, key_query, rest, ids = call(
         prepare_kernel,
         [swath, enc_weight, key_weight, cell_query, quality, sample_cell, live],
         [
             shape(ROWS, channels),
             shape(cells, channels),
             shape(cells, LANES),
-            shape(2 * side, channels),
-            shape(2 * side, LANES),
             shape(1, LANES, dtype=jnp.int32),
         ],
         cost=200_000_000,
         in_specs=[vmem] * 6 + [pl.BlockSpec(memory_space=pltpu.SMEM)],
     )
-    edge, tokens = call(
-        edge_kernel,
-        [enc_weight, tail_a, tail_b, late, ids, quality, edge_kq, edge_rest],
-        [shape(2 * side, LANES), shape(ROWS, LANES)],
-    )
-
-    def merge(mine, other):
-        return call(bound(merge_kernel), [mine, other], shape(*mine.shape))
+    stats, pack = call(
+        pool_kernel,
+        [enc_weight, tail_b, tail_a, late, ids, quality, key_query, rest],
+        [shape(cells // 2 + ROWS, LANES), shape(side, LANES)],
+        scratch_shapes=[pltpu.VMEM((cells, LANES), jnp.float32)],
+    )
 
     flip = 1
-    stats = None
     while flip * 2 < sensors:
-        if stats is None:
-            stats = call(
-                pool_kernel, [tokens, ids, quality, key_query, rest], shape(cells, LANES)
-            )
-        edge = merge(edge, lax.ppermute(edge, axes, across(flip)))
-        stats = merge(stats, lax.ppermute(stats, axes, across(flip)))
+        other, other_pack = (lax.ppermute(v, axes, across(flip)) for v in (stats, pack))
+        stats = call(merge_kernel, [stats, other], shape(*stats.shape))
+        pack = call(bound(merge_pack_kernel), [pack, other_pack], shape(*pack.shape))
         flip *= 2
 
-    other_edge = lax.ppermute(edge, axes, across(flip))
-    if stats is None:
-        stats = call(pool_kernel, [tokens, ids, quality, key_query, rest], shape(cells, LANES), cost=100_000_000)
     other = lax.ppermute(stats, axes, across(flip))
-    mean_a, mean_b = call(
-        bound(edge_mean_kernel),
-        [edge, other_edge],
-        [shape(side, LANES), shape(side, LANES)],
-        cost=10_000_000_000,
-    )
-    halo_b = lax.ppermute(mean_b, axes, far)
+    other_b = lax.ppermute(pack, axes, far(flip))
+    own_b = lax.ppermute(pack, axes, far(0))
+    hpv, taps, code = call(
+        weights_kernel,
+        [value_weight, neighbours, hp_weight, stats],
+        [
+            shape(stencil * out_rows, channels),
+            shape((stencil - 1) * out_rows, 3 * channels, dtype=jnp.bfloat16),
+            shape(*neighbours.shape, dtype=jnp.int32),
+        ],
+        cost=100_000_000,
+    )
+    mean, mean_a = call(
+        mean_kernel,
+        [stats, other],
+        [shape(cells // 2, LANES), shape(side // 2, LANES)],
+    )
     halo_a = lax.ppermute(mean_a, axes, near)
-    hpv, code = call(
-        weights_kernel,
-        [value_weight, neighbours, hp_weight, mean_a],
-        [shape(stencil * out_rows, channels), shape(*neighbours.shape, dtype=jnp.int32)],
-    )
-    partial = call(
-        bound(own_kernel), [stats, other, hpv, code], shape(out_rows, cells), cost=200_000_000
-    )
+    partial = call(own_kernel, [mean, hpv, code], shape(out_rows, cells), cost=200_000_000)
     return call(
-        bound(halo_kernel), [halo_b, halo_a, partial, hpv, code], shape(out_rows, cells)
+        bound(halo_kernel),
+        [halo_a, own_b, other_b, partial, taps, code],
+        shape(out_rows, cells),
     )
 
 

time: 16.9 us -> 15.9 us (0.941)
  the two profiles are of different devices: /device:TPU:0 before, /device:TPU:13 now
where the time goes in v4:
time: 15.9 us; the launch traced here: 15.7 us
  starting transfers between devices  6.37 us (40%)
  Pallas kernels  6.35 us (40%)
  waiting for transfers between devices  2.27 us (14%)
  between operations  0.71 us (4%)
    pallas_call x7, Pallas kernels, call(): pl.pallas_call(kernel, out_shape=outs, compiler_params=pltpu.CompilerPara...  6.35 us
    ppermute x1, waiting for transfers between devices, on_device(): other_b = lax.ppermute(pack, axes, far(flip))  2.26 us
    ppermute x1, starting transfers between devices, on_device(): own_b = lax.ppermute(pack, axes, far(0))  1.91 us
    ppermute x1, starting transfers between devices, on_device(): tail_b = lax.ppermute(tail, axes, far(0))  1.86 us
    ppermute x1, starting transfers between devices, on_device(): other = lax.ppermute(stats, axes, across(flip))  1.25 us
    ppermute x1, starting transfers between devices, on_device(): other_b = lax.ppermute(pack, axes, far(flip))  0.7 us
    ppermute x1, starting transfers between devices, on_device(): halo_a = lax.ppermute(mean_a, axes, near)  0.63 us
  transfers between devices with their start and end apart: 6, of which 1 were waited for; matrix products, arithmetic and copies ran while one was open for 0% of the time, Pallas kernels for 19%

profile of v4, /device:TPU:13, one launch (start us, length us, event | category | flops | bytes accessed | tf_op | source)
XLA Modules:
  0.0 15.7 jit_solution(15658697330090783979)
XLA Ops:
  0.0 1.3 %shard_map.100 = (f32[1,64,512]{2,1,0:T(8,128)S(1)}, f32[1,64,192]{2,1,0:T(8,128)S(1)}, f32[64,64]{1,0:T(8,128)S(1)}, f32[64,64]{1,0:T(8,128)S(1)}, f32[64,256]{...) custom-call(f32[1,64,512]{2,1,0:T(8,128)} %refs_0_.1, ...), custom_call_target="tpu_custom_call" | custom-call | tf_op jit(solution)/shard_map/pallas_call | solution.py:365
  1.3 1.9 %collective-permute-start = (f32[8,128]{1,0:T(8,128)S(1)}, f32[8,128]{1,0:T(8,128)S(1)}, u32[]{:S(2)}, u32[]{:S(2)}) collective-permute-start(f32[8,128]{1,0:T(8,128)S(1)} %get-tuple-element.27), channel_id=1, source_target_pairs={{0,16},{1,2},{2,1},{3,4},{4,3},{5,6},{6,5},{7,8},{8,7},{9,10},{10,... | collective-permute-start | bytes 12296 | tf_op jit(solution)/shard_map/ppermute | solution.py:397
  3.2 0.0 collective-permute-start.1
  3.8 1.8 %shard_map.101 = (f32[8,64]{1,0:T(8,128)S(1)}, f32[256,64]{1,0:T(8,128)S(1)}, f32[256,128]{1,0:T(8,128)S(1)}, s32[1,128]{1,0:T(1,128)S(1)}) custom-call(f32[1,64,512]{2,1,0:T(8,128)S(1)} %get-tuple-element.28.swath_ref, f32[1,64,192]{2,1,0:T(8,128)S(1)} %get-tuple-element.26.enc_ref, f32[64,64]{1,0:T(8,128)S(1)} %get-tuple-element.29.key_ref, ...), custom_call_target="tpu_custom_call" | custom-call | flops 200000000 | bytes 2000000 | tf_op jit(solution)/shard_map/pallas_call | solution.py:365
  5.6 0.0 collective-permute-done.tail_b_ref
  5.6 0.0 collective-permute-done.1.tail_a_ref
  5.6 0.8 %shard_map.102 = (f32[136,128]{1,0:T(8,128)S(1)}, f32[16,128]{1,0:T(8,128)S(1)}) custom-call(f32[1,64,192]{2,1,0:T(8,128)S(1)} %get-tuple-element.26.enc_ref, f32[8,128]{1,0:T(8,128)S(1)} %collective-permute-done.tail_b_ref, f32[8,128]{1,0:T(8,128)S(1)} %collective-permute-done.1.tail_a_ref, f32[8,64]{1,0:T(8,128)S(1)} %get-tuple-element.33.late_ref, ...), custom_call_target="tpu_custom_call" | custom-call | tf_op jit(solution)/shard_map/pallas_call | solution.py:365
  6.4 1.2 %collective-permute-start.2 = (f32[136,128]{1,0:T(8,128)S(1)}, f32[136,128]{1,0:T(8,128)S(1)}, u32[]{:S(2)}, u32[]{:S(2)}) collective-permute-start(f32[136,128]{1,0:T(8,128)S(1)} %get-tuple-element.37.own_ref.after_ref), channel_id=1, source_target_pairs={{0,16},{1,17},{2,18},{3,19},{4,20},{5,21},{6,22},{7,23},{8,24},{9,... | collective-permute-start | bytes 208904 | tf_op jit(solution)/shard_map/ppermute | solution.py:426
  7.7 1.9 %collective-permute-start.4 = (f32[16,128]{1,0:T(8,128)S(1)}, f32[16,128]{1,0:T(8,128)S(1)}, u32[]{:S(2)}, u32[]{:S(2)}) collective-permute-start(f32[16,128]{1,0:T(8,128)S(1)} %get-tuple-element.39), channel_id=1, source_target_pairs={{0,16},{1,2},{2,1},{3,4},{4,3},{5,6},{6,5},{7,8},{8,7},{9,10},{10,... | collective-permute-start | bytes 24584 | tf_op jit(solution)/shard_map/ppermute | solution.py:428
  9.6 0.7 %collective-permute-start.5 = (f32[16,128]{1,0:T(8,128)S(1)}, f32[16,128]{1,0:T(8,128)S(1)}, u32[]{:S(2)}, u32[]{:S(2)}) collective-permute-start(f32[16,128]{1,0:T(8,128)S(1)} %get-tuple-element.39), channel_id=1, source_target_pairs={{0,16},{1,18},{2,17},{3,20},{4,19},{5,22},{6,21},{7,24},{8,23},{9,... | collective-permute-start | bytes 24584 | tf_op jit(solution)/shard_map/ppermute | solution.py:427
  10.3 0.4 %shard_map.104 = (f32[288,64]{1,0:T(8,128)S(1)}, bf16[256,192]{1,0:T(8,128)(2,1)S(1)}, s32[8,256]{1,0:T(8,128)S(1)}) custom-call(f32[64,64]{1,0:T(8,128)S(1)} %get-tuple-element.41.value_ref, s32[8,256]{1,0:T(8,128)S(1)} %get-tuple-element.42.near_ref, f32[64,576]{1,0:T(8,128)S(1)} %get-tuple-element.43.hp_ref, ...), custom_call_target="tpu_custom_call" | custom-call | flops 100000000 | bytes 1000000 | tf_op jit(solution)/shard_map/pallas_call | solution.py:365
  10.7 0.0 collective-permute-done.2.other_ref
  10.7 0.2 %shard_map.103 = (f32[128,128]{1,0:T(8,128)S(1)}, f32[8,128]{1,0:T(8,128)S(1)}) custom-call(f32[136,128]{1,0:T(8,128)S(1)} %get-tuple-element.37.own_ref.after_ref, f32[136,128]{1,0:T(8,128)S(1)} %collective-permute-done.2.other_ref), custom_call_target="tpu_custom_call" | custom-call | tf_op jit(solution)/shard_map/pallas_call | solution.py:365
  11.0 0.6 %collective-permute-start.3 = (f32[8,128]{1,0:T(8,128)S(1)}, f32[8,128]{1,0:T(8,128)S(1)}, u32[]{:S(2)}, u32[]{:S(2)}) collective-permute-start(f32[8,128]{1,0:T(8,128)S(1)} %get-tuple-element.38), channel_id=1, source_target_pairs={{0,1},{1,0},{2,3},{3,2},{4,5},{5,4},{6,7},{7,6},{8,9},{9,8},{10,11... | collective-permute-start | bytes 12296 | tf_op jit(solution)/shard_map/ppermute | solution.py:444
  11.6 0.6 %shard_map.105.refs_3_ = f32[32,256]{1,0:T(8,128)S(1)} custom-call(f32[128,128]{1,0:T(8,128)S(1)} %get-tuple-element.40.mean_ref, f32[288,64]{1,0:T(8,128)S(1)} %get-tuple-element.44.hpv_ref, s32[8,256]{1,0:T(8,128)S(1)} %get-tuple-element.45.code_ref.refs_5_), custom_call_target="tpu_custom_call" | custom-call | flops 200000000 | bytes 2000000 | tf_op jit(solution)/shard_map/pallas_call | solution.py:365
  12.2 0.0 collective-permute-done.4.refs_1_
  12.2 2.3 %collective-permute-done.5.refs_2_ = f32[16,128]{1,0:T(8,128)S(1)} collective-permute-done((f32[16,128]{1,0:T(8,128)S(1)}, f32[16,128]{1,0:T(8,128)S(1)}, u32[]{:S(2)}, u32[]{:S(2)}) %collective-permute-start.5) | collective-permute-done | bytes 8224 | tf_op jit(solution)/shard_map/ppermute | solution.py:427
  14.5 0.0 collective-permute-done.3.refs_0_
  14.5 1.2 %shard_map.106 = f32[32,256]{1,0:T(8,128)} custom-call(f32[8,128]{1,0:T(8,128)S(1)} %collective-permute-done.3.refs_0_, f32[16,128]{1,0:T(8,128)S(1)} %collective-permute-done.4.refs_1_, f32[16,128]{1,0:T(8,128)S(1)} %collective-permute-done.5.refs_2_, f32[32,256]{1,0:T(8,128)S(1)} %shard_map.105.refs_3_, bf16[256,192]{1,0:T(8,128)(2,1)S(1)} %get-tuple-element.46.refs_4_, ...), custom_call_target="tpu_custom_call" | custom-call | tf_op jit(solution)/shard_map/pallas_call | solution.py:365
Async XLA Ops:
  1.3 4.3 %collective-permute-start = (f32[8,128]{1,0:T(8,128)S(1)}, f32[8,128]{1,0:T(8,128)S(1)}, u32[]{:S(2)}, u32[]{:S(2)}) collective-permute-start(f32[8,128]{1,0:T(8,128)S(1)} %get-tuple-element.27), channel_id=1, source_target_pairs={{0,16},{1,2},{2,1},{3,4},{4,3},{5,6},{6,5},{7,8},{8,7},{9,10},{10,... | collective-permute-start | bytes 12296 | tf_op jit(solution)/shard_map/ppermute | solution.py:397
  3.2 2.5 %collective-permute-start.1 = (f32[8,128]{1,0:T(8,128)S(1)}, f32[8,128]{1,0:T(8,128)S(1)}, u32[]{:S(2)}, u32[]{:S(2)}) collective-permute-start(f32[8,128]{1,0:T(8,128)S(1)} %get-tuple-element.27), channel_id=1, source_target_pairs={{0,1},{1,0},{2,3},{3,2},{4,5},{5,4},{6,7},{7,6},{8,9},{9,8},{10,11... | collective-permute-start | bytes 12296 | tf_op jit(solution)/shard_map/ppermute | solution.py:398
  6.4 4.3 %collective-permute-start.2 = (f32[136,128]{1,0:T(8,128)S(1)}, f32[136,128]{1,0:T(8,128)S(1)}, u32[]{:S(2)}, u32[]{:S(2)}) collective-permute-start(f32[136,128]{1,0:T(8,128)S(1)} %get-tuple-element.37.own_ref.after_ref), channel_id=1, source_target_pairs={{0,16},{1,17},{2,18},{3,19},{4,20},{5,21},{6,22},{7,23},{8,24},{9,... | collective-permute-start | bytes 208904 | tf_op jit(solution)/shard_map/ppermute | solution.py:426
  7.7 4.5 %collective-permute-start.4 = (f32[16,128]{1,0:T(8,128)S(1)}, f32[16,128]{1,0:T(8,128)S(1)}, u32[]{:S(2)}, u32[]{:S(2)}) collective-permute-start(f32[16,128]{1,0:T(8,128)S(1)} %get-tuple-element.39), channel_id=1, source_target_pairs={{0,16},{1,2},{2,1},{3,4},{4,3},{5,6},{6,5},{7,8},{8,7},{9,10},{10,... | collective-permute-start | bytes 24584 | tf_op jit(solution)/shard_map/ppermute | solution.py:428
  9.6 4.9 %collective-permute-start.5 = (f32[16,128]{1,0:T(8,128)S(1)}, f32[16,128]{1,0:T(8,128)S(1)}, u32[]{:S(2)}, u32[]{:S(2)}) collective-permute-start(f32[16,128]{1,0:T(8,128)S(1)} %get-tuple-element.39), channel_id=1, source_target_pairs={{0,16},{1,18},{2,17},{3,20},{4,19},{5,22},{6,21},{7,24},{8,23},{9,... | collective-permute-start | bytes 24584 | tf_op jit(solution)/shard_map/ppermute | solution.py:427
  11.0 3.5 %collective-permute-start.3 = (f32[8,128]{1,0:T(8,128)S(1)}, f32[8,128]{1,0:T(8,128)S(1)}, u32[]{:S(2)}, u32[]{:S(2)}) collective-permute-start(f32[8,128]{1,0:T(8,128)S(1)} %get-tuple-element.38), channel_id=1, source_target_pairs={{0,1},{1,0},{2,3},{3,2},{4,5},{5,4},{6,7},{7,6},{8,9},{9,8},{10,11... | collective-permute-start | bytes 12296 | tf_op jit(solution)/shard_map/ppermute | solution.py:444

commit v5 on v4

--- a/solution.py
+++ b/solution.py
@@ -15,6 +15,7 @@
 CLOSE = lax.Precision.HIGH
 NN = ((1,), (0,))
 NT = ((1,), (1,))
+TN = ((0,), (0,))
 
 
 def dot(left, right, contract, precision=EXACT):
@@ -56,33 +57,18 @@
     return both / both[:, channels : channels + 1]
 
 
-def with_late(rest, key_query, late, cell_ids, slot_cells, slot_quality, channels):
-    peak = rest[:, channels + 1 : channels + 2]
-    scores = []
-    for j in range(LATE):
-        score = jnp.sum(key_query * late[j : j + 1, :channels], axis=1, keepdims=True)
-        score = score + slot_quality[:, j : j + 1]
-        score = jnp.where(cell_ids == slot_cells[:, j : j + 1], score, -jnp.inf)
-        peak = jnp.maximum(peak, score)
-        scores.append(score)
-    block = rest * jnp.exp(rest[:, channels + 1 : channels + 2] - peak)
-    for j, score in enumerate(scores):
-        block = block + jnp.exp(score - peak) * late[j : j + 1, :]
-    return with_peak(block, peak, channels)
-
-
 def load_kernel(*refs):
-    count = (len(refs) - 2) // 2
-    sources, targets, tail_ref, sems = refs[:count], refs[count:-2], refs[-2], refs[-1]
-    copies = [
-        pltpu.make_async_copy(source, target, sems.at[i])
-        for i, (source, target) in enumerate(zip(sources, targets))
-    ]
+    *refs, tail_ref, last_ref, sems = refs
+    count = len(refs) // 2
+    sources, targets = refs[:count], refs[count:]
+    swath_ref = sources[0]
+    copies = [(swath_ref.at[0, :, pl.ds(swath_ref.shape[2] - LANES, LANES)], last_ref)]
+    copies += list(zip(sources, targets))
+    copies = [pltpu.make_async_copy(*ends, sems.at[i]) for i, ends in enumerate(copies)]
     for copy in copies:
         copy.start()
     copies[0].wait()
-    swath_ref = targets[0]
-    last = swath_ref[0, :, swath_ref.shape[2] - LANES :]
+    last = last_ref[...]
     row, lane = iota((ROWS, LANES), 0), iota((ROWS, LANES), 1)
     first = ((lane == LANES - 2 + row) & (row < 2)).astype(jnp.float32)
     second = ((lane == LANES - 1) & (row == 0)).astype(jnp.float32)
@@ -91,22 +77,26 @@
         copy.wait()
 
 
-def scored(key_query, encoded, quality, ids, cells):
-    score = dot(key_query, encoded, NN) + quality
-    return jnp.where(cells == ids, score, -jnp.inf)
-
-
-def block_of(score, encoded, query, key_query, counted, channels):
-    own_score = jnp.sum(query * key_query, axis=1, keepdims=True)
-    own_score = jnp.where(counted, own_score, -jnp.inf)
-    peak = jnp.maximum(jnp.max(score, axis=1, keepdims=True), jnp.maximum(own_score, FLOOR))
-    weights = jnp.exp(score - peak)
-    place = iota((LANES - channels, encoded.shape[1]), 0)
-    tokens = jnp.concatenate([encoded, (place == 0).astype(jnp.float32)], axis=0)
-    own = widened(query)
-    own = jnp.where(iota(own.shape, 1) == channels, 1.0, own)
-    block = dot(weights, tokens, NT, CLOSE) + own * jnp.exp(own_score - peak)
-    return block, peak
+def halves(value):
+    high = value.astype(jnp.bfloat16)
+    return high, (value - high.astype(jnp.float32)).astype(jnp.bfloat16)
+
+
+def parts(value):
+    high = value.astype(jnp.bfloat16)
+    rest = value - high.astype(jnp.float32)
+    middle = rest.astype(jnp.bfloat16)
+    return high, middle, (rest - middle.astype(jnp.float32)).astype(jnp.bfloat16)
+
+
+def packed(block, channels):
+    half = block.shape[0] // 2
+    sums = jnp.concatenate([block[:half, :channels], block[half:, :channels]], axis=1)
+    total, peak = (block[:, channels + i : channels + i + 1] for i in range(2))
+    lane = iota((half, LANES), 1)
+    columns = jnp.where(lane == 0, total[:half], jnp.where(lane == 1, total[half:], 0.0))
+    columns = jnp.where(lane == 2, peak[:half], jnp.where(lane == 3, peak[half:], columns))
+    return sums, jnp.transpose(columns)[:ROWS, :]
 
 
 def prepare_kernel(
@@ -117,79 +107,132 @@
     quality_ref,
     cell_ref,
     live_ref,
-    late_ref,
+    before_ref,
+    ids_ref,
+    late_kq_ref,
+    late_rest_ref,
+    stats_ref,
+    pack_ref,
     kq_ref,
-    rest_ref,
-    ids_ref,
+    block_ref,
 ):
     sensor = lax.axis_index("sensor")
+    odd = lax.rem(lax.axis_index("cell"), 2)
     channels, slots = swath_ref.shape[1:]
     cells = query_ref.shape[1]
+    side, half = pack_ref.shape[0], cells // 2
 
     signal = swath_ref[0]
     one = jnp.concatenate([jnp.zeros((channels, 1), jnp.float32), signal[:, : slots - 1]], axis=1)
     two = jnp.concatenate([jnp.zeros((channels, 2), jnp.float32), signal[:, : slots - 2]], axis=1)
     stacked = jnp.concatenate([two, one, signal], axis=0)
     before = dot(enc_ref[0], stacked, NN)
-    late_ref[...] = jnp.transpose(before[:, :LANES])[:ROWS, :]
+    before_ref[...] = jnp.transpose(before[:, :LANES])[:ROWS, :]
     encoded = gelu(before)
 
-    query = jnp.transpose(query_ref[...])
-    key_query = dot(query, key_ref[...], NN) * (1.0 / math.sqrt(channels))
+    query = query_ref[...]
+    key_query = dot(key_ref[...], query, TN) * (1.0 / math.sqrt(channels))
+    key_query = jnp.transpose(jnp.concatenate([key_query, key_query], axis=0))
+    query = jnp.transpose(jnp.concatenate([query, jnp.zeros(query.shape, jnp.float32)], axis=0))
     kq_ref[...] = key_query
-
+    own_score = jnp.sum(query * key_query, axis=1, keepdims=True)
+    own_score = jnp.where(sensor == 0, own_score, -jnp.inf)
+
+    high, middle, low = parts(key_query)
+    mixed = jnp.where(iota(high.shape, 1) < channels, high, low)
+    token_high, token_middle, token_low = parts(encoded)
+    score = dot(
+        jnp.concatenate([high, middle, mixed], axis=1),
+        jnp.concatenate(
+            [token_high, token_middle, token_high, token_middle, token_low, token_high], axis=0
+        ),
+        NN,
+        None,
+    )
     slot = iota((1, slots), 1)
     ids = jnp.where(slot < live_ref[0, 0], cell_ref[...], -1)
     ids_ref[...] = ids[:, :LANES]
     ids = jnp.where(slot < LATE, -1, ids)
-    score = scored(key_query, encoded, quality_ref[...], ids, iota((cells, 1), 0))
-    block, peak = block_of(score, encoded, query, key_query, sensor == 0, channels)
-    rest_ref[...] = with_peak(block, peak, channels)
+    score = jnp.where(iota((cells, slots), 0) == ids, score + quality_ref[...], -jnp.inf)
+    peak = jnp.maximum(jnp.max(score, axis=1, keepdims=True), jnp.maximum(own_score, FLOOR))
+    weights = jnp.exp(score - peak)
+    place = iota((LANES - channels, slots), 0)
+    tokens = jnp.concatenate([encoded, (place == 0).astype(jnp.float32)], axis=0)
+    high, low = halves(jnp.transpose(tokens))
+    weights_high, weights_low = halves(weights)
+    wide = dot(weights_high, jnp.concatenate([high, low], axis=1), NN, None)
+    block = wide[:, :LANES] + wide[:, LANES:] + dot(weights_low, high, NN, None)
+    own = jnp.where(iota(query.shape, 1) == channels, 1.0, query)
+    block = with_peak(block + own * jnp.exp(own_score - peak), peak, channels)
+    block_ref[...] = block
+    stats_ref[:half, :], stats_ref[half:, :] = packed(block, channels)
+    left = block_ref[pl.ds(0, side, stride=side), :]
+    right = block_ref[pl.ds(side - 1, side, stride=side), :]
+    pack_ref[...] = jnp.where(odd == 1, right, left)
+    late_kq_ref[...] = jnp.zeros(late_kq_ref.shape, jnp.float32)
+    late_rest_ref[...] = jnp.zeros(late_rest_ref.shape, jnp.float32)
+    for j in range(LATE):
+        at = cell_ref[0, j]
+        late_kq_ref[j : j + 1, :] = kq_ref[pl.ds(at, 1), :]
+        late_rest_ref[j : j + 1, :] = block_ref[pl.ds(at, 1), :]
 
 
 def pool_kernel(
     enc_ref,
+    tail_a_ref,
     tail_b_ref,
-    tail_a_ref,
-    late_ref,
+    before_ref,
     ids_ref,
     quality_ref,
-    kq_ref,
+    late_kq_ref,
+    late_rest_ref,
     rest_ref,
+    rest_pack_ref,
     stats_ref,
     pack_ref,
-    block_ref,
 ):
     cell = lax.axis_index("cell")
     odd = lax.rem(cell, 2)
-    cells, channels = kq_ref.shape
-    side, half = pack_ref.shape[0], cells // 2
+    channels = before_ref.shape[1]
+    side, half = pack_ref.shape[0], stats_ref.shape[0] - ROWS
     tail = jnp.where(odd == 1, tail_a_ref[...], tail_b_ref[...])
     tail = jnp.where(cell == 0, 0.0, tail)
-    before = late_ref[...] + dot(tail, enc_ref[0, :, : 2 * channels], NT)
+    before = before_ref[...] + dot(tail, enc_ref[0, :, : 2 * channels], NT)
     tokens = widened(gelu(before))
+    score = jnp.sum(tokens * late_kq_ref[...], axis=1, keepdims=True)
     tokens = jnp.where(iota(tokens.shape, 1) == channels, 1.0, tokens)
-    block = with_late(
-        rest_ref[...],
-        kq_ref[...],
-        tokens,
-        iota((cells, 1), 0),
-        ids_ref[...],
-        quality_ref[:, :LANES],
-        channels,
-    )
-    block_ref[...] = block
-    stats_ref[:half, :] = jnp.concatenate(
-        [block[:half, :channels], block[half:, :channels]], axis=1
-    )
-    total, peak = (block[:, channels + i : channels + i + 1] for i in range(2))
-    lane = iota((half, LANES), 1)
-    columns = jnp.where(lane == 0, total[:half], jnp.where(lane == 1, total[half:], 0.0))
-    columns = jnp.where(lane == 2, peak[:half], jnp.where(lane == 3, peak[half:], columns))
-    stats_ref[half:, :] = jnp.transpose(columns)[:ROWS, :]
-    left = block_ref[pl.ds(0, side, stride=side), :]
-    right = block_ref[pl.ds(side - 1, side, stride=side), :]
-    pack_ref[...] = jnp.where(odd == 1, right, left)
+    rest = late_rest_ref[...]
+    rest_peak = rest[:, channels + 1 : channels + 2]
+    ids = ids_ref[...]
+    rows = []
+    for j in range(LATE):
+        rest_peak = rest[j : j + 1, channels + 1 : channels + 2]
+        peak, found = rest_peak, []
+        for i in range(LATE):
+            here = score[i : i + 1] + quality_ref[:, i : i + 1]
+            if i != j:
+                here = jnp.where(ids[:, i : i + 1] == ids[:, j : j + 1], here, -jnp.inf)
+            found.append(here)
+            peak = jnp.maximum(peak, here)
+        row = rest[j : j + 1] * jnp.exp(rest_peak - peak)
+        for i, here in enumerate(found):
+            row = row + tokens[i : i + 1] * jnp.exp(here - peak)
+        rows.append(with_peak(row, peak, channels))
+    sums, ends, pack = rest_ref[:half, :], rest_ref[half:, :], rest_pack_ref[...]
+    lane = iota(sums.shape, 1)
+    of_sum = iota(sums.shape, 0) + jnp.where(lane < channels, 0, half)
+    kind = iota(ends.shape, 0)
+    of_end = iota(ends.shape, 1) + jnp.where(lax.rem(kind, 2) == 0, 0, half)
+    of_pack = iota((side, 1), 0) * side + jnp.where(odd == 1, side - 1, 0)
+    for j, row in enumerate(rows):
+        at = ids[:, j : j + 1]
+        twice = jnp.concatenate([row[:, :channels], row[:, :channels]], axis=1)
+        sums = jnp.where(of_sum == at, twice, sums)
+        total, peak = (row[:, channels + i : channels + i + 1] for i in range(2))
+        ends = jnp.where((of_end == at) & (kind < 4), jnp.where(kind < 2, total, peak), ends)
+        pack = jnp.where(of_pack == at, row, pack)
+    stats_ref[:half, :], stats_ref[half:, :] = sums, ends
+    pack_ref[...] = pack
 
 
 def shares(first, second):
@@ -223,12 +266,11 @@
     out_ref[half:, :] = jnp.concatenate([total, peak, rest], axis=0)
 
 
-def halves(value):
-    high = value.astype(jnp.bfloat16)
-    return high, (value - high.astype(jnp.float32)).astype(jnp.bfloat16)
-
-
-def weights_kernel(value_ref, near_ref, hp_ref, after_ref, hpv_ref, taps_ref, code_ref):
+def copy_kernel(in_ref, out_ref):
+    out_ref[...] = in_ref[...]
+
+
+def weights_kernel(value_ref, near_ref, hp_ref, after_ref, hpv_ref, taps_ref, code_ref, halo_ref):
     del after_ref
     sensor = lax.axis_index("sensor")
     cell = lax.axis_index("cell")
@@ -252,6 +294,8 @@
     after = cells + odd * side + lax.shift_right_arithmetic(offset - cells, shift)
     ahead = cells + (1 - odd) * side + lax.shift_right_arithmetic(offset + cells, shift)
     code_ref[...] = jnp.where(offset < 0, ahead, jnp.where(offset < cells, offset, after))
+    halo = jnp.where(offset < 0, ahead, after) - cells
+    halo_ref[...] = jnp.where((offset < 0) | (offset >= cells), halo, LANES - 1)
 
 
 def mean_kernel(own_ref, other_ref, mean_ref, pack_ref):
@@ -266,19 +310,6 @@
     pack_ref[...] = jnp.where(odd == 1, left, right)
 
 
-def picked(sources, first, code_ref, total, start, out_rows, base):
-    for k in range(code_ref.shape[0]):
-        code = jnp.broadcast_to(code_ref[k : k + 1, start : start + LANES], total.shape)
-        lane = lax.bitwise_and(code, LANES - 1)
-        rows = slice((k + base) * out_rows, (k + base + 1) * out_rows)
-        taken = 0.0
-        for i, source in enumerate(sources, first):
-            here = jnp.take_along_axis(source[rows], lane, axis=1, mode="promise_in_bounds")
-            taken = jnp.where(lax.shift_right_logical(code, 7) == i, here, taken)
-        total = total + taken
-    return total
-
-
 def own_kernel(mean_ref, hpv_ref, code_ref, out_ref):
     out_rows, cells = out_ref.shape
     mean, hpv = mean_ref[...], hpv_ref[...]
@@ -286,14 +317,30 @@
     mixed = [
         dot(jnp.concatenate(pair, axis=1), mean, NT, CLOSE) for pair in ((hpv, gap), (gap, hpv))
     ]
+    lanes = lax.bitwise_and(code_ref[...], LANES - 1)
+    places = lax.shift_right_logical(code_ref[...], LANES.bit_length() - 1)
     for i, start in enumerate(range(0, cells, LANES)):
-        out_ref[:, start : start + LANES] = picked(
-            mixed, 0, code_ref, mixed[i][:out_rows], start, out_rows, 1
-        )
+        total = mixed[i][:out_rows]
+        for k in range(code_ref.shape[0]):
+            rows = slice((k + 1) * out_rows, (k + 2) * out_rows)
+            lane, place = (
+                jnp.broadcast_to(v[k : k + 1, start : start + LANES], total.shape)
+                for v in (lanes, places)
+            )
+            taken = 0.0
+            for source, values in enumerate(mixed):
+                here = taken_lanes(values[rows], lane)
+                taken = jnp.where(place == source, here, taken)
+            total = total + taken
+        out_ref[:, start : start + LANES] = total
+
+
+def taken_lanes(values, lane):
+    return jnp.take_along_axis(values, lane, axis=1, mode="promise_in_bounds")
 
 
 def halo_kernel(
-    channels, a_ref, own_b_ref, other_b_ref, partial_ref, taps_ref, code_ref, out_ref
+    channels, a_ref, own_b_ref, other_b_ref, partial_ref, taps_ref, lanes_ref, out_ref
 ):
     out_rows, cells = out_ref.shape
     a, b = a_ref[...], mean_of(own_b_ref[...], other_b_ref[...], channels)
@@ -301,16 +348,13 @@
     gap = jnp.zeros((LANES - halo.shape[0], channels), jnp.float32)
     high, low = halves(jnp.concatenate([halo, gap], axis=0))
     edge = dot(taps_ref[...], jnp.concatenate([high, low, high], axis=1), NT, None)
+    lanes = lanes_ref[...]
     for start in range(0, cells, LANES):
-        out_ref[:, start : start + LANES] = picked(
-            [edge],
-            cells // LANES,
-            code_ref,
-            partial_ref[:, start : start + LANES],
-            start,
-            out_rows,
-            0,
-        )
+        total = partial_ref[:, start : start + LANES]
+        for k in range(lanes.shape[0]):
+            lane = jnp.broadcast_to(lanes[k : k + 1, start : start + LANES], total.shape)
+            total = total + taken_lanes(edge[k * out_rows : (k + 1) * out_rows], lane)
+        out_ref[:, start : start + LANES] = total
 
 
 def swaps(sensors, cells):
@@ -390,30 +434,46 @@
         [pltpu.with_memory_space_constraint(a, pltpu.HBM) for a in args],
         [shape(*a.shape, dtype=a.dtype) for a in args] + [shape(ROWS, LANES)],
         in_specs=[pl.BlockSpec(memory_space=pltpu.HBM)] * len(args),
-        scratch_shapes=[pltpu.SemaphoreType.DMA((len(args),))],
+        scratch_shapes=[
+            pltpu.VMEM((channels, LANES), jnp.float32),
+            pltpu.SemaphoreType.DMA((len(args) + 1,)),
+        ],
     )
     swath, enc_weight, key_weight, value_weight, cell_query = loaded[:5]
     quality, sample_cell, neighbours, hp_weight, tail = loaded[5:]
     tail_b = lax.ppermute(tail, axes, far(0))
     tail_a = lax.ppermute(tail, axes, near)
 
-    late, key_query, rest, ids = call(
+    before, ids, late_kq, late_rest, rest, rest_pack = call(
         prepare_kernel,
         [swath, enc_weight, key_weight, cell_query, quality, sample_cell, live],
         [
             shape(ROWS, channels),
-            shape(cells, channels),
-            shape(cells, LANES),
             shape(1, LANES, dtype=jnp.int32),
+            shape(ROWS, LANES),
+            shape(ROWS, LANES),
+            shape(cells // 2 + ROWS, LANES),
+            shape(side, LANES),
         ],
         cost=200_000_000,
         in_specs=[vmem] * 6 + [pl.BlockSpec(memory_space=pltpu.SMEM)],
+        scratch_shapes=[pltpu.VMEM((cells, LANES), jnp.float32)] * 2,
     )
     stats, pack = call(
         pool_kernel,
-        [enc_weight, tail_b, tail_a, late, ids, quality, key_query, rest],
-        [shape(cells // 2 + ROWS, LANES), shape(side, LANES)],
-        scratch_shapes=[pltpu.VMEM((cells, LANES), jnp.float32)],
+        [
+            enc_weight,
+            tail_a,
+            tail_b,
+            before,
+            ids,
+            quality,
+            late_kq,
+            late_rest,
+            rest,
+            rest_pack,
+        ],
+        [shape(*rest.shape), shape(*rest_pack.shape)],
     )
 
     flip = 1
@@ -425,17 +485,19 @@
 
     other = lax.ppermute(stats, axes, across(flip))
     other_b = lax.ppermute(pack, axes, far(flip))
-    own_b = lax.ppermute(pack, axes, far(0))
-    hpv, taps, code = call(
+    pack_again = call(copy_kernel, [pack], shape(*pack.shape), cost=100_000_000)
+    hpv, taps, code, lanes = call(
         weights_kernel,
-        [value_weight, neighbours, hp_weight, stats],
+        [value_weight, neighbours, hp_weight, pack_again],
         [
             shape(stencil * out_rows, channels),
             shape((stencil - 1) * out_rows, 3 * channels, dtype=jnp.bfloat16),
             shape(*neighbours.shape, dtype=jnp.int32),
+            shape(*neighbours.shape, dtype=jnp.int32),
         ],
         cost=100_000_000,
     )
+    own_b = lax.ppermute(pack_again, axes, far(0))
     mean, mean_a = call(
         mean_kernel,
         [stats, other],
@@ -445,7 +507,7 @@
     partial = call(own_kernel, [mean, hpv, code], shape(out_rows, cells), cost=200_000_000)
     return call(
         bound(halo_kernel),
-        [halo_a, own_b, other_b, partial, taps, code],
+        [halo_a, own_b, other_b, partial, taps, lanes],
         shape(out_rows, cells),
     )
 

time: 15.9 us -> 14.6 us (0.918)
  waiting for transfers between devices: 2.27 us -> 1.58 us
  Pallas kernels: 6.35 us -> 5.79 us
    ppermute x1, waiting for transfers between devices: 2.26 us -> 0.01 us  [on_device(): other_b = lax.ppermute(pack, axes, far(flip))]
    ppermute x1, waiting for transfers between devices: 0.01 us -> 1.54 us  [on_device(): own_b = lax.ppermute(pack_again, axes, far(0))]
    ppermute x1, starting transfers between devices: 1.91 us -> 0.56 us  [on_device(): own_b = lax.ppermute(pack_again, axes, far(0))]
    ppermute x1, starting transfers between devices: 0.7 us -> 2.05 us  [on_device(): other_b = lax.ppermute(pack, axes, far(flip))]
    pallas_call x7 -> x8, Pallas kernels: 6.35 us -> 5.79 us  [call(): pl.pallas_call(kernel, out_shape=outs, compiler_params=pltpu.CompilerPara...]
where the time goes in v5:
time: 14.6 us; the launch traced here: 14.4 us
  starting transfers between devices  6.36 us (44%)
  Pallas kernels  5.79 us (40%)
  waiting for transfers between devices  1.58 us (11%)
  between operations  0.69 us (5%)
    pallas_call x8, Pallas kernels, call(): pl.pallas_call(kernel, out_shape=outs, compiler_params=pltpu.CompilerPara...  5.79 us
    ppermute x1, starting transfers between devices, on_device(): other_b = lax.ppermute(pack, axes, far(flip))  2.05 us
    ppermute x1, starting transfers between devices, on_device(): tail_b = lax.ppermute(tail, axes, far(0))  1.86 us
    ppermute x1, waiting for transfers between devices, on_device(): own_b = lax.ppermute(pack_again, axes, far(0))  1.54 us
    ppermute x1, starting transfers between devices, on_device(): other = lax.ppermute(stats, axes, across(flip))  1.28 us
    ppermute x1, starting transfers between devices, on_device(): halo_a = lax.ppermute(mean_a, axes, near)  0.6 us
    ppermute x1, starting transfers between devices, on_device(): own_b = lax.ppermute(pack_again, axes, far(0))  0.56 us
  transfers between devices with their start and end apart: 6, of which 1 were waited for; matrix products, arithmetic and copies ran while one was open for 0% of the time, Pallas kernels for 19%

profile of v5, /device:TPU:13, one launch (start us, length us, event | category | flops | bytes accessed | tf_op | source)
XLA Modules:
  0.0 14.4 jit_solution(4552865588638008480)
XLA Ops:
  0.0 1.2 %shard_map.100 = (f32[1,64,512]{2,1,0:T(8,128)S(1)}, f32[1,64,192]{2,1,0:T(8,128)S(1)}, f32[64,64]{1,0:T(8,128)S(1)}, f32[64,64]{1,0:T(8,128)S(1)}, f32[64,256]{...) custom-call(f32[1,64,512]{2,1,0:T(8,128)} %refs_0_.1, ...), custom_call_target="tpu_custom_call" | custom-call | tf_op jit(solution)/shard_map/pallas_call | solution.py:409
  1.2 1.9 %collective-permute-start.1 = (f32[8,128]{1,0:T(8,128)S(1)}, f32[8,128]{1,0:T(8,128)S(1)}, u32[]{:S(2)}, u32[]{:S(2)}) collective-permute-start(f32[8,128]{1,0:T(8,128)S(1)} %get-tuple-element.30), channel_id=1, source_target_pairs={{0,16},{1,2},{2,1},{3,4},{4,3},{5,6},{6,5},{7,8},{8,7},{9,10},{10,... | collective-permute-start | bytes 12296 | tf_op jit(solution)/shard_map/ppermute | solution.py:444
  3.1 0.0 collective-permute-start
  3.7 1.4 %shard_map.101 = (f32[8,64]{1,0:T(8,128)S(1)}, s32[1,128]{1,0:T(1,128)S(1)}, f32[8,128]{1,0:T(8,128)S(1)}, f32[8,128]{1,0:T(8,128)S(1)}, f32[136,128]{1,0:T(8,128)S(1)}, /*index=5*/f32[16,128]{1,0:T(8,128)S(1)}) custom-call(f32[1,64,512]{2,1,0:T(8,128)S(1)} %get-tuple-element.31.swath_ref, f32[1,64,192]{2,1,0:T(8,128)S(1)} %get-tuple-element.29.enc_ref, ...), custom_call_target="tpu_custom_call" | custom-call | flops 200000000 | bytes 2000000 | tf_op jit(solution)/shard_map/pallas_call | solution.py:409
  5.2 0.0 collective-permute-done.1.tail_b_ref
  5.2 0.0 collective-permute-done.tail_a_ref
  5.2 0.7 %shard_map.102 = (f32[136,128]{1,0:T(8,128)S(1)}, f32[16,128]{1,0:T(8,128)S(1)}) custom-call(f32[1,64,192]{2,1,0:T(8,128)S(1)} %get-tuple-element.29.enc_ref, f32[8,128]{1,0:T(8,128)S(1)} %collective-permute-done.tail_a_ref, f32[8,128]{1,0:T(8,128)S(1)} %collective-permute-done.1.tail_b_ref, f32[8,64]{1,0:T(8,128)S(1)} %get-tuple-element.36.before_ref, ...), custom_call_target="tpu_custom_call" | custom-call | tf_op jit(solution)/shard_map/pallas_call | solution.py:409
  5.9 1.3 %collective-permute-start.2 = (f32[136,128]{1,0:T(8,128)S(1)}, f32[136,128]{1,0:T(8,128)S(1)}, u32[]{:S(2)}, u32[]{:S(2)}) collective-permute-start(f32[136,128]{1,0:T(8,128)S(1)} %get-tuple-element.42.own_ref), channel_id=1, source_target_pairs={{0,16},{1,17},{2,18},{3,19},{4,20},{5,21},{6,22},{7,23},{8,24},{9,... | collective-permute-start | bytes 208904 | tf_op jit(solution)/shard_map/ppermute | solution.py:486
  7.2 2.1 %collective-permute-start.5 = (f32[16,128]{1,0:T(8,128)S(1)}, f32[16,128]{1,0:T(8,128)S(1)}, u32[]{:S(2)}, u32[]{:S(2)}) collective-permute-start(f32[16,128]{1,0:T(8,128)S(1)} %get-tuple-element.44.in_ref), channel_id=1, source_target_pairs={{0,16},{1,18},{2,17},{3,20},{4,19},{5,22},{6,21},{7,24},{8,23},{9,... | collective-permute-start | bytes 24584 | tf_op jit(solution)/shard_map/ppermute | solution.py:487
  9.2 0.6 %collective-permute-start.4 = (f32[16,128]{1,0:T(8,128)S(1)}, f32[16,128]{1,0:T(8,128)S(1)}, u32[]{:S(2)}, u32[]{:S(2)}) collective-permute-start(f32[16,128]{1,0:T(8,128)S(1)} %shard_map.104.after_ref), channel_id=1, source_target_pairs={{0,16},{1,2},{2,1},{3,4},{4,3},{5,6},{6,5},{7,8},{8,7},{9,10},{10,... | collective-permute-start | bytes 24584 | tf_op jit(solution)/shard_map/ppermute | solution.py:500
  9.8 0.4 %shard_map.105 = (f32[288,64]{1,0:T(8,128)S(1)}, bf16[256,192]{1,0:T(8,128)(2,1)S(1)}, s32[8,256]{1,0:T(8,128)S(1)}, s32[8,256]{1,0:T(8,128)S(1)}) custom-call(f32[64,64]{1,0:T(8,128)S(1)} %get-tuple-element.46.value_ref, s32[8,256]{1,0:T(8,128)S(1)} %get-tuple-element.47.near_ref, f32[64,576]{1,0:T(8,128)S(1)} %get-tuple-element.48.hp_ref, ...), custom_call_target="tpu_custom_call" | custom-call | flops 100000000 | bytes 1000000 | tf_op jit(solution)/shard_map/pallas_call | solution.py:409
  10.2 0.0 collective-permute-done.2.other_ref
  10.2 0.2 %shard_map.103 = (f32[128,128]{1,0:T(8,128)S(1)}, f32[8,128]{1,0:T(8,128)S(1)}) custom-call(f32[136,128]{1,0:T(8,128)S(1)} %get-tuple-element.42.own_ref, f32[136,128]{1,0:T(8,128)S(1)} %collective-permute-done.2.other_ref), custom_call_target="tpu_custom_call" | custom-call | tf_op jit(solution)/shard_map/pallas_call | solution.py:409
  10.5 0.6 %collective-permute-start.3 = (f32[8,128]{1,0:T(8,128)S(1)}, f32[8,128]{1,0:T(8,128)S(1)}, u32[]{:S(2)}, u32[]{:S(2)}) collective-permute-start(f32[8,128]{1,0:T(8,128)S(1)} %get-tuple-element.43), channel_id=1, source_target_pairs={{0,1},{1,0},{2,3},{3,2},{4,5},{5,4},{6,7},{7,6},{8,9},{9,8},{10,11... | collective-permute-start | bytes 12296 | tf_op jit(solution)/shard_map/ppermute | solution.py:506
  11.1 0.6 %shard_map.106.refs_3_ = f32[32,256]{1,0:T(8,128)S(1)} custom-call(f32[128,128]{1,0:T(8,128)S(1)} %get-tuple-element.45.mean_ref, f32[288,64]{1,0:T(8,128)S(1)} %get-tuple-element.49.hpv_ref, s32[8,256]{1,0:T(8,128)S(1)} %get-tuple-element.50.code_ref), custom_call_target="tpu_custom_call" | custom-call | flops 200000000 | bytes 2000000 | tf_op jit(solution)/shard_map/pallas_call | solution.py:409
  11.7 1.5 %collective-permute-done.4.refs_1_ = f32[16,128]{1,0:T(8,128)S(1)} collective-permute-done((f32[16,128]{1,0:T(8,128)S(1)}, f32[16,128]{1,0:T(8,128)S(1)}, u32[]{:S(2)}, u32[]{:S(2)}) %collective-permute-start.4) | collective-permute-done | bytes 8224 | tf_op jit(solution)/shard_map/ppermute | solution.py:500
  13.2 0.0 collective-permute-done.5.refs_2_
  13.2 0.0 collective-permute-done.3.refs_0_
  13.2 1.2 %shard_map.107 = f32[32,256]{1,0:T(8,128)} custom-call(f32[8,128]{1,0:T(8,128)S(1)} %collective-permute-done.3.refs_0_, f32[16,128]{1,0:T(8,128)S(1)} %collective-permute-done.4.refs_1_, f32[16,128]{1,0:T(8,128)S(1)} %collective-permute-done.5.refs_2_, f32[32,256]{1,0:T(8,128)S(1)} %shard_map.106.refs_3_, bf16[256,192]{1,0:T(8,128)(2,1)S(1)} %get-tuple-element.51.refs_4_, ...), custom_call_target="tpu_custom_call" | custom-call | tf_op jit(solution)/shard_map/pallas_call | solution.py:409
  (1 shorter events, 0.0 us)
Async XLA Ops:
  1.2 4.0 %collective-permute-start.1 = (f32[8,128]{1,0:T(8,128)S(1)}, f32[8,128]{1,0:T(8,128)S(1)}, u32[]{:S(2)}, u32[]{:S(2)}) collective-permute-start(f32[8,128]{1,0:T(8,128)S(1)} %get-tuple-element.30), channel_id=1, source_target_pairs={{0,16},{1,2},{2,1},{3,4},{4,3},{5,6},{6,5},{7,8},{8,7},{9,10},{10,... | collective-permute-start | bytes 12296 | tf_op jit(solution)/shard_map/ppermute | solution.py:444
  3.1 2.1 %collective-permute-start = (f32[8,128]{1,0:T(8,128)S(1)}, f32[8,128]{1,0:T(8,128)S(1)}, u32[]{:S(2)}, u32[]{:S(2)}) collective-permute-start(f32[8,128]{1,0:T(8,128)S(1)} %get-tuple-element.30), channel_id=1, source_target_pairs={{0,1},{1,0},{2,3},{3,2},{4,5},{5,4},{6,7},{7,6},{8,9},{9,8},{10,11... | collective-permute-start | bytes 12296 | tf_op jit(solution)/shard_map/ppermute | solution.py:445
  5.9 4.3 %collective-permute-start.2 = (f32[136,128]{1,0:T(8,128)S(1)}, f32[136,128]{1,0:T(8,128)S(1)}, u32[]{:S(2)}, u32[]{:S(2)}) collective-permute-start(f32[136,128]{1,0:T(8,128)S(1)} %get-tuple-element.42.own_ref), channel_id=1, source_target_pairs={{0,16},{1,17},{2,18},{3,19},{4,20},{5,21},{6,22},{7,23},{8,24},{9,... | collective-permute-start | bytes 208904 | tf_op jit(solution)/shard_map/ppermute | solution.py:486
  7.2 6.0 %collective-permute-start.5 = (f32[16,128]{1,0:T(8,128)S(1)}, f32[16,128]{1,0:T(8,128)S(1)}, u32[]{:S(2)}, u32[]{:S(2)}) collective-permute-start(f32[16,128]{1,0:T(8,128)S(1)} %get-tuple-element.44.in_ref), channel_id=1, source_target_pairs={{0,16},{1,18},{2,17},{3,20},{4,19},{5,22},{6,21},{7,24},{8,23},{9,... | collective-permute-start | bytes 24584 | tf_op jit(solution)/shard_map/ppermute | solution.py:487
  9.2 4.0 %collective-permute-start.4 = (f32[16,128]{1,0:T(8,128)S(1)}, f32[16,128]{1,0:T(8,128)S(1)}, u32[]{:S(2)}, u32[]{:S(2)}) collective-permute-start(f32[16,128]{1,0:T(8,128)S(1)} %shard_map.104.after_ref), channel_id=1, source_target_pairs={{0,16},{1,2},{2,1},{3,4},{4,3},{5,6},{6,5},{7,8},{8,7},{9,10},{10,... | collective-permute-start | bytes 24584 | tf_op jit(solution)/shard_map/ppermute | solution.py:500
  10.5 2.7 %collective-permute-start.3 = (f32[8,128]{1,0:T(8,128)S(1)}, f32[8,128]{1,0:T(8,128)S(1)}, u32[]{:S(2)}, u32[]{:S(2)}) collective-permute-start(f32[8,128]{1,0:T(8,128)S(1)} %get-tuple-element.43), channel_id=1, source_target_pairs={{0,1},{1,0},{2,3},{3,2},{4,5},{5,4},{6,7},{7,6},{8,9},{9,8},{10,11... | collective-permute-start | bytes 12296 | tf_op jit(solution)/shard_map/ppermute | solution.py:506

commit v6 on v5

--- a/solution.py
+++ b/solution.py
@@ -1,3 +1,4 @@
+import functools
 import math
 
 import jax
@@ -68,11 +69,10 @@
     for copy in copies:
         copy.start()
     copies[0].wait()
-    last = last_ref[...]
-    row, lane = iota((ROWS, LANES), 0), iota((ROWS, LANES), 1)
-    first = ((lane == LANES - 2 + row) & (row < 2)).astype(jnp.float32)
-    second = ((lane == LANES - 1) & (row == 0)).astype(jnp.float32)
-    tail_ref[...] = jnp.concatenate([dot(first, last, NT), dot(second, last, NT)], axis=1)
+    last = jnp.transpose(last_ref[...])[LANES - LATE :, :]
+    gap = jnp.zeros(last.shape, jnp.float32)
+    two = jnp.concatenate([last, jnp.concatenate([last[1:], gap[1:]], axis=0)], axis=1)
+    tail_ref[...] = jnp.concatenate([two] + [jnp.zeros(two.shape, jnp.float32)] * 3, axis=0)
     for copy in copies[1:]:
         copy.wait()
 
@@ -107,15 +107,27 @@
     quality_ref,
     cell_ref,
     live_ref,
+    value_ref,
+    near_ref,
+    hp_ref,
     before_ref,
+    taps_ref,
     ids_ref,
     late_kq_ref,
     late_rest_ref,
     stats_ref,
     pack_ref,
+    loaded_value_ref,
+    loaded_near_ref,
+    loaded_hp_ref,
     kq_ref,
     block_ref,
+    sems,
 ):
+    ends = ((value_ref, loaded_value_ref), (near_ref, loaded_near_ref), (hp_ref, loaded_hp_ref))
+    copies = [pltpu.make_async_copy(*pair, sems.at[i]) for i, pair in enumerate(ends)]
+    for copy in copies:
+        copy.start()
     sensor = lax.axis_index("sensor")
     odd = lax.rem(lax.axis_index("cell"), 2)
     channels, slots = swath_ref.shape[1:]
@@ -175,10 +187,14 @@
         at = cell_ref[0, j]
         late_kq_ref[j : j + 1, :] = kq_ref[pl.ds(at, 1), :]
         late_rest_ref[j : j + 1, :] = block_ref[pl.ds(at, 1), :]
+    high, middle, low = parts(enc_ref[0, :, : LATE * channels])
+    taps_ref[...] = jnp.concatenate([high, high, middle, high, middle, low], axis=1)
+    for copy in copies:
+        copy.wait()
 
 
 def pool_kernel(
-    enc_ref,
+    taps_ref,
     tail_a_ref,
     tail_b_ref,
     before_ref,
@@ -197,7 +213,9 @@
     side, half = pack_ref.shape[0], stats_ref.shape[0] - ROWS
     tail = jnp.where(odd == 1, tail_a_ref[...], tail_b_ref[...])
     tail = jnp.where(cell == 0, 0.0, tail)
-    before = before_ref[...] + dot(tail, enc_ref[0, :, : 2 * channels], NT)
+    high, middle, low = parts(jnp.concatenate([tail, jnp.zeros(tail.shape, jnp.float32)], axis=0))
+    tail = jnp.concatenate([high, middle, high, low, middle, high], axis=1)
+    before = before_ref[...] + dot(tail, taps_ref[...], NT, None)[:ROWS, :]
     tokens = widened(gelu(before))
     score = jnp.sum(tokens * late_kq_ref[...], axis=1, keepdims=True)
     tokens = jnp.where(iota(tokens.shape, 1) == channels, 1.0, tokens)
@@ -243,13 +261,15 @@
     return first_factor, second_factor, total, peak
 
 
-def spread(row_pair, width):
-    square = jnp.concatenate(
-        [row_pair, jnp.zeros((LANES - row_pair.shape[0], row_pair.shape[1]), jnp.float32)], axis=0
-    )
-    columns = jnp.transpose(square)
-    lane = iota((columns.shape[0], width), 1)
-    return jnp.where(lane < width // 2, columns[:, 0:1], columns[:, 1:2])
+def spread(*row_pairs):
+    rows = jnp.concatenate(row_pairs, axis=0)
+    gap = jnp.zeros((LANES - rows.shape[0], rows.shape[1]), jnp.float32)
+    columns = jnp.transpose(jnp.concatenate([rows, gap], axis=0))
+    left = iota((columns.shape[0], LANES), 1) < LANES // 2
+    return [
+        jnp.where(left, columns[:, 2 * i : 2 * i + 1], columns[:, 2 * i + 1 : 2 * i + 2])
+        for i in range(len(row_pairs))
+    ]
 
 
 def merge_pack_kernel(channels, own_ref, other_ref, out_ref):
@@ -260,8 +280,8 @@
 def merge_kernel(own_ref, other_ref, out_ref):
     half = own_ref.shape[0] - ROWS
     first_factor, second_factor, total, peak = shares(own_ref[half:, :], other_ref[half:, :])
-    first_sum = own_ref[:half, :] * spread(first_factor, LANES)
-    out_ref[:half, :] = first_sum + other_ref[:half, :] * spread(second_factor, LANES)
+    first_factor, second_factor = spread(first_factor, second_factor)
+    out_ref[:half, :] = own_ref[:half, :] * first_factor + other_ref[:half, :] * second_factor
     rest = jnp.zeros((ROWS - 4, total.shape[1]), jnp.float32)
     out_ref[half:, :] = jnp.concatenate([total, peak, rest], axis=0)
 
@@ -270,7 +290,7 @@
     out_ref[...] = in_ref[...]
 
 
-def weights_kernel(value_ref, near_ref, hp_ref, after_ref, hpv_ref, taps_ref, code_ref, halo_ref):
+def weights_kernel(value_ref, near_ref, hp_ref, after_ref, hpv_ref, taps_ref, code_ref, pick_ref):
     del after_ref
     sensor = lax.axis_index("sensor")
     cell = lax.axis_index("cell")
@@ -294,8 +314,11 @@
     after = cells + odd * side + lax.shift_right_arithmetic(offset - cells, shift)
     ahead = cells + (1 - odd) * side + lax.shift_right_arithmetic(offset + cells, shift)
     code_ref[...] = jnp.where(offset < 0, ahead, jnp.where(offset < cells, offset, after))
-    halo = jnp.where(offset < 0, ahead, after) - cells
-    halo_ref[...] = jnp.where((offset < 0) | (offset >= cells), halo, LANES - 1)
+    halo = code_ref[...] - cells
+    place = iota((2 * side, cells), 0)
+    for k in range(halo.shape[0]):
+        here = (place == halo[k : k + 1, :]).astype(jnp.float32).astype(jnp.bfloat16)
+        pick_ref[2 * side * k : 2 * side * (k + 1), :] = here
 
 
 def mean_kernel(own_ref, other_ref, mean_ref, pack_ref):
@@ -303,8 +326,8 @@
     half = mean_ref.shape[0]
     side = half // pack_ref.shape[0]
     first_factor, second_factor, total, _ = shares(own_ref[half:, :], other_ref[half:, :])
-    mean = own_ref[:half, :] * spread(first_factor / total, LANES)
-    mean_ref[...] = mean + other_ref[:half, :] * spread(second_factor / total, LANES)
+    first_share, second_share = spread(first_factor / total, second_factor / total)
+    mean_ref[...] = own_ref[:half, :] * first_share + other_ref[:half, :] * second_share
     left = mean_ref[pl.ds(0, half // side, stride=side), :]
     right = mean_ref[pl.ds(side - 1, half // side, stride=side), :]
     pack_ref[...] = jnp.where(odd == 1, left, right)
@@ -340,21 +363,30 @@
 
 
 def halo_kernel(
-    channels, a_ref, own_b_ref, other_b_ref, partial_ref, taps_ref, lanes_ref, out_ref
+    channels, last, a_ref, own_b_ref, other_b_ref, partial_ref, taps_ref, pick_ref, out_ref
 ):
-    out_rows, cells = out_ref.shape
-    a, b = a_ref[...], mean_of(own_b_ref[...], other_b_ref[...], channels)
+    out_rows = out_ref.shape[0]
+    cell = lax.axis_index("cell")
+    b = mean_of(own_b_ref[...], other_b_ref[...], channels)
+    b = jnp.where((cell == 0) | (cell == last), 0.0, b)
+    a = a_ref[...]
     halo = jnp.concatenate([a[:, :channels], a[:, channels:], b[:, :channels]], axis=0)
-    gap = jnp.zeros((LANES - halo.shape[0], channels), jnp.float32)
-    high, low = halves(jnp.concatenate([halo, gap], axis=0))
-    edge = dot(taps_ref[...], jnp.concatenate([high, low, high], axis=1), NT, None)
-    lanes = lanes_ref[...]
-    for start in range(0, cells, LANES):
-        total = partial_ref[:, start : start + LANES]
-        for k in range(lanes.shape[0]):
-            lane = jnp.broadcast_to(lanes[k : k + 1, start : start + LANES], total.shape)
-            total = total + taken_lanes(edge[k * out_rows : (k + 1) * out_rows], lane)
-        out_ref[:, start : start + LANES] = total
+    high, low = halves(halo)
+    cells = halo.shape[0]
+    turns = LANES // cells
+    halo = jnp.concatenate([jnp.concatenate([high, low, high], axis=1)] * turns, axis=0)
+    edge = dot(taps_ref[...], halo, NT, None)
+    lane = iota((out_rows, LANES), 1)
+    groups = []
+    for start in range(0, edge.shape[0], turns * out_rows):
+        group = edge[start : start + out_rows]
+        for turn in range(1, turns):
+            rows = edge[start + turn * out_rows : start + (turn + 1) * out_rows]
+            group = jnp.where(lane >= turn * cells, rows, group)
+        groups.append(group)
+    high, low = halves(jnp.concatenate(groups, axis=1))
+    pick = pick_ref[...]
+    out_ref[...] = partial_ref[...] + (dot(high, pick, NN, None) + dot(low, pick, NN, None))
 
 
 def swaps(sensors, cells):
@@ -418,51 +450,52 @@
     def bound(kernel):
         return lambda *refs: kernel(channels, *refs)
 
-    args = [
-        swath,
-        enc_weight,
-        key_weight,
-        value_weight,
-        cell_query,
-        quality,
-        sample_cell,
-        neighbours,
-        hp_weight,
-    ]
-    loaded = call(
+    hbm = pl.BlockSpec(memory_space=pltpu.HBM)
+
+    def pinned(*args):
+        return [pltpu.with_memory_space_constraint(a, pltpu.HBM) for a in args]
+
+    def like(*args):
+        return [shape(*a.shape, dtype=a.dtype) for a in args]
+
+    args = [swath, enc_weight, key_weight, cell_query, quality, sample_cell]
+    swath, enc_weight, key_weight, cell_query, quality, sample_cell, tail = call(
         load_kernel,
-        [pltpu.with_memory_space_constraint(a, pltpu.HBM) for a in args],
-        [shape(*a.shape, dtype=a.dtype) for a in args] + [shape(ROWS, LANES)],
-        in_specs=[pl.BlockSpec(memory_space=pltpu.HBM)] * len(args),
+        pinned(*args),
+        like(*args) + [shape(ROWS, LANES)],
+        in_specs=[hbm] * len(args),
         scratch_shapes=[
             pltpu.VMEM((channels, LANES), jnp.float32),
             pltpu.SemaphoreType.DMA((len(args) + 1,)),
         ],
     )
-    swath, enc_weight, key_weight, value_weight, cell_query = loaded[:5]
-    quality, sample_cell, neighbours, hp_weight, tail = loaded[5:]
     tail_b = lax.ppermute(tail, axes, far(0))
-    tail_a = lax.ppermute(tail, axes, near)
-
-    before, ids, late_kq, late_rest, rest, rest_pack = call(
+    tail_again = call(copy_kernel, [tail], shape(*tail.shape), cost=100_000_000)
+    tail_a = lax.ppermute(tail_again, axes, near)
+
+    args = [value_weight, neighbours, hp_weight]
+    before, late_taps, ids, late_kq, late_rest, rest, rest_pack, *loaded = call(
         prepare_kernel,
-        [swath, enc_weight, key_weight, cell_query, quality, sample_cell, live],
+        [swath, enc_weight, key_weight, cell_query, quality, sample_cell, live] + pinned(*args),
         [
             shape(ROWS, channels),
+            shape(channels, 6 * LATE * channels, dtype=jnp.bfloat16),
             shape(1, LANES, dtype=jnp.int32),
             shape(ROWS, LANES),
             shape(ROWS, LANES),
             shape(cells // 2 + ROWS, LANES),
             shape(side, LANES),
-        ],
+        ]
+        + like(*args),
         cost=200_000_000,
-        in_specs=[vmem] * 6 + [pl.BlockSpec(memory_space=pltpu.SMEM)],
-        scratch_shapes=[pltpu.VMEM((cells, LANES), jnp.float32)] * 2,
+        in_specs=[vmem] * 6 + [pl.BlockSpec(memory_space=pltpu.SMEM)] + [hbm] * len(args),
+        scratch_shapes=[pltpu.VMEM((cells, LANES), jnp.float32)] * 2
+        + [pltpu.SemaphoreType.DMA((len(args),))],
     )
     stats, pack = call(
         pool_kernel,
         [
-            enc_weight,
+            late_taps,
             tail_a,
             tail_b,
             before,
@@ -486,14 +519,14 @@
     other = lax.ppermute(stats, axes, across(flip))
     other_b = lax.ppermute(pack, axes, far(flip))
     pack_again = call(copy_kernel, [pack], shape(*pack.shape), cost=100_000_000)
-    hpv, taps, code, lanes = call(
+    hpv, taps, code, pick = call(
         weights_kernel,
-        [value_weight, neighbours, hp_weight, pack_again],
+        loaded + [pack_again],
         [
             shape(stencil * out_rows, channels),
             shape((stencil - 1) * out_rows, 3 * channels, dtype=jnp.bfloat16),
             shape(*neighbours.shape, dtype=jnp.int32),
-            shape(*neighbours.shape, dtype=jnp.int32),
+            shape((stencil - 1) * 2 * side, cells, dtype=jnp.bfloat16),
         ],
         cost=100_000_000,
     )
@@ -506,8 +539,8 @@
     halo_a = lax.ppermute(mean_a, axes, near)
     partial = call(own_kernel, [mean, hpv, code], shape(out_rows, cells), cost=200_000_000)
     return call(
-        bound(halo_kernel),
-        [halo_a, own_b, other_b, partial, taps, lanes],
+        functools.partial(halo_kernel, channels, ranges - 1),
+        [halo_a, own_b, other_b, partial, taps, pick],
         shape(out_rows, cells),
     )
 

time: 14.6 us -> 14.4 us (0.986)
    pallas_call x8 -> x9, Pallas kernels: 5.79 us -> 5.68 us  [call(): pl.pallas_call(kernel, out_shape=outs, compiler_params=pltpu.CompilerPara...]
  transfers between devices with their start and end apart: 6 -> 6, of which waited for: 1 -> 1; matrix products, arithmetic and copies ran while one was open for 0% -> 0% of each run, Pallas kernels for 19% -> 20%
where the time goes in v6:
time: 14.4 us; the launch traced here: 14.2 us
  starting transfers between devices  6.39 us (44%)
  Pallas kernels  5.68 us (39%)
  waiting for transfers between devices  1.44 us (10%)
  between operations  0.72 us (5%)
    pallas_call x9, Pallas kernels, call(): pl.pallas_call(kernel, out_shape=outs, compiler_params=pltpu.CompilerPara...  5.68 us
    ppermute x1, starting transfers between devices, on_device(): other_b = lax.ppermute(pack, axes, far(flip))  2.01 us
    ppermute x1, starting transfers between devices, on_device(): tail_b = lax.ppermute(tail, axes, far(0))  1.86 us
    ppermute x1, waiting for transfers between devices, on_device(): own_b = lax.ppermute(pack_again, axes, far(0))  1.43 us
    ppermute x1, starting transfers between devices, on_device(): other = lax.ppermute(stats, axes, across(flip))  1.27 us
    ppermute x1, starting transfers between devices, on_device(): halo_a = lax.ppermute(mean_a, axes, near)  0.63 us
    ppermute x1, starting transfers between devices, on_device(): own_b = lax.ppermute(pack_again, axes, far(0))  0.61 us
  transfers between devices with their start and end apart: 6, of which 1 were waited for; matrix products, arithmetic and copies ran while one was open for 0% of the time, Pallas kernels for 20%

profile of v6, /device:TPU:13, one launch (start us, length us, event | category | flops | bytes accessed | tf_op | source)
XLA Modules:
  0.0 14.2 jit_solution(10077343020775223409)
XLA Ops:
  0.0 1.1 %shard_map.100 = (f32[1,64,512]{2,1,0:T(8,128)S(1)}, f32[1,64,192]{2,1,0:T(8,128)S(1)}, f32[64,64]{1,0:T(8,128)S(1)}, f32[64,256]{1,0:T(8,128)S(1)}, f32[1,512]{...) custom-call(f32[1,64,512]{2,1,0:T(8,128)} %refs_0_.1, f32[1,64,192]{2,1,0:T(8,128)} %refs_1_.1, ...), custom_call_target="tpu_custom_call" | custom-call | tf_op jit(solution)/shard_map/pallas_call | solution.py:441
  1.1 1.9 %collective-permute-start.1 = (f32[8,128]{1,0:T(8,128)S(1)}, f32[8,128]{1,0:T(8,128)S(1)}, u32[]{:S(2)}, u32[]{:S(2)}) collective-permute-start(f32[8,128]{1,0:T(8,128)S(1)} %get-tuple-element.37.in_ref), channel_id=1, source_target_pairs={{0,16},{1,2},{2,1},{3,4},{4,3},{5,6},{6,5},{7,8},{8,7},{9,10},{10,... | collective-permute-start | bytes 12296 | tf_op jit(solution)/shard_map/ppermute | solution.py:472
  2.9 0.0 collective-permute-start
  3.6 1.5 %shard_map.101 = (f32[8,64]{1,0:T(8,128)S(1)}, bf16[64,768]{1,0:T(8,128)(2,1)S(1)}, s32[1,128]{1,0:T(1,128)S(1)}, f32[8,128]{1,0:T(8,128)S(1)}, f32[8,128]{1,0:T...) custom-call(f32[1,64,512]{2,1,0:T(8,128)S(1)} %get-tuple-element.30., ...), custom_call_target="tpu_custom_call" | custom-call | flops 200000000 | bytes 2000000 | tf_op jit(solution)/shard_map/pallas_call | solution.py:441
  5.1 0.0 collective-permute-done.tail_a_ref
  5.1 0.0 collective-permute-done.1.tail_b_ref
  5.1 0.6 %shard_map.103 = (f32[136,128]{1,0:T(8,128)S(1)}, f32[16,128]{1,0:T(8,128)S(1)}) custom-call(bf16[64,768]{1,0:T(8,128)(2,1)S(1)} %get-tuple-element.36.taps_ref, f32[8,128]{1,0:T(8,128)S(1)} %collective-permute-done.tail_a_ref, f32[8,128]{1,0:T(8,128)S(1)} %collective-permute-done.1.tail_b_ref, f32[8,64]{1,0:T(8,128)S(1)} %get-tuple-element.38.before_ref, ...), custom_call_target="tpu_custom_call" | custom-call | tf_op jit(solution)/shard_map/pallas_call | solution.py:441
  5.7 1.3 %collective-permute-start.2 = (f32[136,128]{1,0:T(8,128)S(1)}, f32[136,128]{1,0:T(8,128)S(1)}, u32[]{:S(2)}, u32[]{:S(2)}) collective-permute-start(f32[136,128]{1,0:T(8,128)S(1)} %get-tuple-element.44.own_ref), channel_id=1, source_target_pairs={{0,16},{1,17},{2,18},{3,19},{4,20},{5,21},{6,22},{7,23},{8,24},{9,... | collective-permute-start | bytes 208904 | tf_op jit(solution)/shard_map/ppermute | solution.py:519
  7.0 2.0 %collective-permute-start.5 = (f32[16,128]{1,0:T(8,128)S(1)}, f32[16,128]{1,0:T(8,128)S(1)}, u32[]{:S(2)}, u32[]{:S(2)}) collective-permute-start(f32[16,128]{1,0:T(8,128)S(1)} %get-tuple-element.46.in_ref), channel_id=1, source_target_pairs={{0,16},{1,18},{2,17},{3,20},{4,19},{5,22},{6,21},{7,24},{8,23},{9,... | collective-permute-start | bytes 24584 | tf_op jit(solution)/shard_map/ppermute | solution.py:520
  9.0 0.6 %collective-permute-start.4 = (f32[16,128]{1,0:T(8,128)S(1)}, f32[16,128]{1,0:T(8,128)S(1)}, u32[]{:S(2)}, u32[]{:S(2)}) collective-permute-start(f32[16,128]{1,0:T(8,128)S(1)} %shard_map.105.after_ref), channel_id=1, source_target_pairs={{0,16},{1,2},{2,1},{3,4},{4,3},{5,6},{6,5},{7,8},{8,7},{9,10},{10,... | collective-permute-start | bytes 24584 | tf_op jit(solution)/shard_map/ppermute | solution.py:533
  9.6 0.4 %shard_map.106 = (f32[288,64]{1,0:T(8,128)S(1)}, bf16[256,192]{1,0:T(8,128)(2,1)S(1)}, s32[8,256]{1,0:T(8,128)S(1)}, bf16[256,256]{1,0:T(8,128)(2,1)S(1)}) custom-call(f32[64,64]{1,0:T(8,128)S(1)} %get-tuple-element.48.value_ref, s32[8,256]{1,0:T(8,128)S(1)} %get-tuple-element.49.near_ref, f32[64,576]{1,0:T(8,128)S(1)} %get-tuple-element.50.hp_ref, ...), custom_call_target="tpu_custom_call" | custom-call | flops 100000000 | bytes 1000000 | tf_op jit(solution)/shard_map/pallas_call | solution.py:441
  10.1 0.0 collective-permute-done.2.other_ref
  10.1 0.3 %shard_map.104 = (f32[128,128]{1,0:T(8,128)S(1)}, f32[8,128]{1,0:T(8,128)S(1)}) custom-call(f32[136,128]{1,0:T(8,128)S(1)} %get-tuple-element.44.own_ref, f32[136,128]{1,0:T(8,128)S(1)} %collective-permute-done.2.other_ref), custom_call_target="tpu_custom_call" | custom-call | tf_op jit(solution)/shard_map/pallas_call | solution.py:441
  10.4 0.6 %collective-permute-start.3 = (f32[8,128]{1,0:T(8,128)S(1)}, f32[8,128]{1,0:T(8,128)S(1)}, u32[]{:S(2)}, u32[]{:S(2)}) collective-permute-start(f32[8,128]{1,0:T(8,128)S(1)} %get-tuple-element.45), channel_id=1, source_target_pairs={{0,1},{1,0},{2,3},{3,2},{4,5},{5,4},{6,7},{7,6},{8,9},{9,8},{10,11... | collective-permute-start | bytes 12296 | tf_op jit(solution)/shard_map/ppermute | solution.py:539
  11.0 0.6 %shard_map.107.partial_ref = f32[32,256]{1,0:T(8,128)S(1)} custom-call(f32[128,128]{1,0:T(8,128)S(1)} %get-tuple-element.47.mean_ref, f32[288,64]{1,0:T(8,128)S(1)} %get-tuple-element.51.hpv_ref, s32[8,256]{1,0:T(8,128)S(1)} %get-tuple-element.52.code_ref), custom_call_target="tpu_custom_call" | custom-call | flops 200000000 | bytes 2000000 | tf_op jit(solution)/shard_map/pallas_call | solution.py:441
  11.6 1.4 %collective-permute-done.4.own_b_ref = f32[16,128]{1,0:T(8,128)S(1)} collective-permute-done((f32[16,128]{1,0:T(8,128)S(1)}, f32[16,128]{1,0:T(8,128)S(1)}, u32[]{:S(2)}, u32[]{:S(2)}) %collective-permute-start.4) | collective-permute-done | bytes 8224 | tf_op jit(solution)/shard_map/ppermute | solution.py:533
  13.0 0.0 collective-permute-done.5.other_b_ref
  13.0 0.0 collective-permute-done.3.a_ref
  13.0 1.2 %shard_map.108 = f32[32,256]{1,0:T(8,128)} custom-call(f32[8,128]{1,0:T(8,128)S(1)} %collective-permute-done.3.a_ref, f32[16,128]{1,0:T(8,128)S(1)} %collective-permute-done.4.own_b_ref, f32[16,128]{1,0:T(8,128)S(1)} %collective-permute-done.5.other_b_ref, f32[32,256]{1,0:T(8,128)S(1)} %shard_map.107.partial_ref, ...), custom_call_target="tpu_custom_call" | custom-call | tf_op jit(solution)/shard_map/pallas_call | solution.py:441
  (2 shorter events, 0.0 us)
Async XLA Ops:
  1.1 4.0 %collective-permute-start.1 = (f32[8,128]{1,0:T(8,128)S(1)}, f32[8,128]{1,0:T(8,128)S(1)}, u32[]{:S(2)}, u32[]{:S(2)}) collective-permute-start(f32[8,128]{1,0:T(8,128)S(1)} %get-tuple-element.37.in_ref), channel_id=1, source_target_pairs={{0,16},{1,2},{2,1},{3,4},{4,3},{5,6},{6,5},{7,8},{8,7},{9,10},{10,... | collective-permute-start | bytes 12296 | tf_op jit(solution)/shard_map/ppermute | solution.py:472
  2.9 2.2 %collective-permute-start = (f32[8,128]{1,0:T(8,128)S(1)}, f32[8,128]{1,0:T(8,128)S(1)}, u32[]{:S(2)}, u32[]{:S(2)}) collective-permute-start(f32[8,128]{1,0:T(8,128)S(1)} %shard_map.102), channel_id=1, source_target_pairs={{0,1},{1,0},{2,3},{3,2},{4,5},{5,4},{6,7},{7,6},{8,9},{9,8},{10,11... | collective-permute-start | bytes 12296 | tf_op jit(solution)/shard_map/ppermute | solution.py:474
  5.7 4.3 %collective-permute-start.2 = (f32[136,128]{1,0:T(8,128)S(1)}, f32[136,128]{1,0:T(8,128)S(1)}, u32[]{:S(2)}, u32[]{:S(2)}) collective-permute-start(f32[136,128]{1,0:T(8,128)S(1)} %get-tuple-element.44.own_ref), channel_id=1, source_target_pairs={{0,16},{1,17},{2,18},{3,19},{4,20},{5,21},{6,22},{7,23},{8,24},{9,... | collective-permute-start | bytes 208904 | tf_op jit(solution)/shard_map/ppermute | solution.py:519
  7.0 6.0 %collective-permute-start.5 = (f32[16,128]{1,0:T(8,128)S(1)}, f32[16,128]{1,0:T(8,128)S(1)}, u32[]{:S(2)}, u32[]{:S(2)}) collective-permute-start(f32[16,128]{1,0:T(8,128)S(1)} %get-tuple-element.46.in_ref), channel_id=1, source_target_pairs={{0,16},{1,18},{2,17},{3,20},{4,19},{5,22},{6,21},{7,24},{8,23},{9,... | collective-permute-start | bytes 24584 | tf_op jit(solution)/shard_map/ppermute | solution.py:520
  9.0 4.0 %collective-permute-start.4 = (f32[16,128]{1,0:T(8,128)S(1)}, f32[16,128]{1,0:T(8,128)S(1)}, u32[]{:S(2)}, u32[]{:S(2)}) collective-permute-start(f32[16,128]{1,0:T(8,128)S(1)} %shard_map.105.after_ref), channel_id=1, source_target_pairs={{0,16},{1,2},{2,1},{3,4},{4,3},{5,6},{6,5},{7,8},{8,7},{9,10},{10,... | collective-permute-start | bytes 24584 | tf_op jit(solution)/shard_map/ppermute | solution.py:533
  10.4 2.7 %collective-permute-start.3 = (f32[8,128]{1,0:T(8,128)S(1)}, f32[8,128]{1,0:T(8,128)S(1)}, u32[]{:S(2)}, u32[]{:S(2)}) collective-permute-start(f32[8,128]{1,0:T(8,128)S(1)} %get-tuple-element.45), channel_id=1, source_target_pairs={{0,1},{1,0},{2,3},{3,2},{4,5},{5,4},{6,7},{7,6},{8,9},{9,8},{10,11... | collective-permute-start | bytes 12296 | tf_op jit(solution)/shard_map/ppermute | solution.py:539

commit v7 on v6

--- a/solution.py
+++ b/solution.py
@@ -53,9 +53,19 @@
     return both, peak
 
 
+def twice(value):
+    half = value[:, : LANES // 2]
+    return jnp.concatenate([half, half], axis=1)
+
+
 def mean_of(first, second, channels):
-    both, _ = merged(first, second, channels)
-    return both / both[:, channels : channels + 1]
+    (first_total, first_peak), (second_total, second_peak) = (
+        [v[:, channels + i : channels + i + 1] for i in range(2)] for v in (first, second)
+    )
+    peak = jnp.maximum(first_peak, second_peak)
+    first_factor, second_factor = jnp.exp(first_peak - peak), jnp.exp(second_peak - peak)
+    total = first_total * first_factor + second_total * second_factor
+    return twice(first) * (first_factor / total) + twice(second) * (second_factor / total)
 
 
 def load_kernel(*refs):
@@ -64,7 +74,11 @@
     sources, targets = refs[:count], refs[count:]
     swath_ref = sources[0]
     copies = [(swath_ref.at[0, :, pl.ds(swath_ref.shape[2] - LANES, LANES)], last_ref)]
-    copies += list(zip(sources, targets))
+    hp_ref, own_hp_ref = sources[-1], targets[-1]
+    out_rows = own_hp_ref.shape[0]
+    start = pl.multiple_of(lax.axis_index("sensor") * out_rows, ROWS)
+    copies += [(hp_ref.at[pl.ds(start, out_rows), :], own_hp_ref)]
+    copies += list(zip(sources[:-1], targets[:-1]))
     copies = [pltpu.make_async_copy(*ends, sems.at[i]) for i, ends in enumerate(copies)]
     for copy in copies:
         copy.start()
@@ -107,27 +121,15 @@
     quality_ref,
     cell_ref,
     live_ref,
-    value_ref,
-    near_ref,
-    hp_ref,
     before_ref,
     taps_ref,
     ids_ref,
-    late_kq_ref,
-    late_rest_ref,
+    late_ref,
     stats_ref,
     pack_ref,
-    loaded_value_ref,
-    loaded_near_ref,
-    loaded_hp_ref,
     kq_ref,
     block_ref,
-    sems,
 ):
-    ends = ((value_ref, loaded_value_ref), (near_ref, loaded_near_ref), (hp_ref, loaded_hp_ref))
-    copies = [pltpu.make_async_copy(*pair, sems.at[i]) for i, pair in enumerate(ends)]
-    for copy in copies:
-        copy.start()
     sensor = lax.axis_index("sensor")
     odd = lax.rem(lax.axis_index("cell"), 2)
     channels, slots = swath_ref.shape[1:]
@@ -139,7 +141,8 @@
     two = jnp.concatenate([jnp.zeros((channels, 2), jnp.float32), signal[:, : slots - 2]], axis=1)
     stacked = jnp.concatenate([two, one, signal], axis=0)
     before = dot(enc_ref[0], stacked, NN)
-    before_ref[...] = jnp.transpose(before[:, :LANES])[:ROWS, :]
+    first = before[:, :LANES]
+    before_ref[...] = jnp.transpose(jnp.concatenate([first, first], axis=0))[:ROWS, :]
     encoded = gelu(before)
 
     query = query_ref[...]
@@ -163,7 +166,7 @@
     )
     slot = iota((1, slots), 1)
     ids = jnp.where(slot < live_ref[0, 0], cell_ref[...], -1)
-    ids_ref[...] = ids[:, :LANES]
+    late_ids = [ids[:, j : j + 1] for j in range(LATE)]
     ids = jnp.where(slot < LATE, -1, ids)
     score = jnp.where(iota((cells, slots), 0) == ids, score + quality_ref[...], -jnp.inf)
     peak = jnp.maximum(jnp.max(score, axis=1, keepdims=True), jnp.maximum(own_score, FLOOR))
@@ -181,16 +184,31 @@
     left = block_ref[pl.ds(0, side, stride=side), :]
     right = block_ref[pl.ds(side - 1, side, stride=side), :]
     pack_ref[...] = jnp.where(odd == 1, right, left)
-    late_kq_ref[...] = jnp.zeros(late_kq_ref.shape, jnp.float32)
-    late_rest_ref[...] = jnp.zeros(late_rest_ref.shape, jnp.float32)
-    for j in range(LATE):
-        at = cell_ref[0, j]
-        late_kq_ref[j : j + 1, :] = kq_ref[pl.ds(at, 1), :]
-        late_rest_ref[j : j + 1, :] = block_ref[pl.ds(at, 1), :]
+    gap = jnp.zeros((ROWS - LATE, LANES), jnp.float32)
+
+    def listed(rows):
+        return jnp.concatenate([jnp.broadcast_to(r, (1, LANES)) for r in rows] + [gap], axis=0)
+
+    at = [pl.ds(cell_ref[0, j], 1) for j in range(LATE)]
+    key_query = listed([kq_ref[a, :] for a in at])
+    rest = listed([block_ref[a, :] for a in at])
+    late_ref[0] = jnp.where(iota(key_query.shape, 1) < channels, key_query, 0.0)
+    late_ref[1] = twice(rest)
+    for i in range(2):
+        late_ref[2 + i] = jnp.broadcast_to(rest[:, channels + i : channels + i + 1], rest.shape)
+    late_ref[4] = listed([quality_ref[:, j : j + 1] for j in range(LATE)])
+    same = jnp.where(late_ids[0] == late_ids[1], 0.0, -jnp.inf)
+    late_ref[5] = listed([same] * LATE)
+    ids_ref[...] = jnp.concatenate(
+        [jnp.broadcast_to(i, (1, LANES)) for i in late_ids] + [gap.astype(jnp.int32)], axis=0
+    )
     high, middle, low = parts(enc_ref[0, :, : LATE * channels])
-    taps_ref[...] = jnp.concatenate([high, high, middle, high, middle, low], axis=1)
-    for copy in copies:
-        copy.wait()
+    taps = jnp.concatenate([high, high, middle, high, middle, low], axis=1)
+    taps_ref[...] = jnp.concatenate([taps, taps], axis=0)
+
+
+def swapped(value):
+    return jnp.concatenate([value[1:2], value[0:1], value[2:]], axis=0)
 
 
 def pool_kernel(
@@ -199,9 +217,7 @@
     tail_b_ref,
     before_ref,
     ids_ref,
-    quality_ref,
-    late_kq_ref,
-    late_rest_ref,
+    late_ref,
     rest_ref,
     rest_pack_ref,
     stats_ref,
@@ -209,45 +225,34 @@
 ):
     cell = lax.axis_index("cell")
     odd = lax.rem(cell, 2)
-    channels = before_ref.shape[1]
     side, half = pack_ref.shape[0], stats_ref.shape[0] - ROWS
+    channels = LANES // 2
     tail = jnp.where(odd == 1, tail_a_ref[...], tail_b_ref[...])
     tail = jnp.where(cell == 0, 0.0, tail)
     high, middle, low = parts(jnp.concatenate([tail, jnp.zeros(tail.shape, jnp.float32)], axis=0))
     tail = jnp.concatenate([high, middle, high, low, middle, high], axis=1)
-    before = before_ref[...] + dot(tail, taps_ref[...], NT, None)[:ROWS, :]
-    tokens = widened(gelu(before))
-    score = jnp.sum(tokens * late_kq_ref[...], axis=1, keepdims=True)
-    tokens = jnp.where(iota(tokens.shape, 1) == channels, 1.0, tokens)
-    rest = late_rest_ref[...]
-    rest_peak = rest[:, channels + 1 : channels + 2]
-    ids = ids_ref[...]
-    rows = []
-    for j in range(LATE):
-        rest_peak = rest[j : j + 1, channels + 1 : channels + 2]
-        peak, found = rest_peak, []
-        for i in range(LATE):
-            here = score[i : i + 1] + quality_ref[:, i : i + 1]
-            if i != j:
-                here = jnp.where(ids[:, i : i + 1] == ids[:, j : j + 1], here, -jnp.inf)
-            found.append(here)
-            peak = jnp.maximum(peak, here)
-        row = rest[j : j + 1] * jnp.exp(rest_peak - peak)
-        for i, here in enumerate(found):
-            row = row + tokens[i : i + 1] * jnp.exp(here - peak)
-        rows.append(with_peak(row, peak, channels))
+    tokens = gelu(before_ref[...] + dot(tail, taps_ref[...], NT, None)[:ROWS, :])
+
+    key_query, rest, rest_total, rest_peak, quality, same = (late_ref[i] for i in range(6))
+    score = jnp.sum(tokens * key_query, axis=1, keepdims=True) + quality
+    other = swapped(score) + same
+    peak = jnp.maximum(rest_peak, jnp.maximum(score, other))
+    rest_factor, weight, other_weight = (jnp.exp(v - peak) for v in (rest_peak, score, other))
+    rows = rest * rest_factor + tokens * weight + swapped(tokens) * other_weight
+    totals = rest_total * rest_factor + weight + other_weight
+
     sums, ends, pack = rest_ref[:half, :], rest_ref[half:, :], rest_pack_ref[...]
-    lane = iota(sums.shape, 1)
-    of_sum = iota(sums.shape, 0) + jnp.where(lane < channels, 0, half)
+    of_sum = iota(sums.shape, 0) + jnp.where(iota(sums.shape, 1) < channels, 0, half)
     kind = iota(ends.shape, 0)
     of_end = iota(ends.shape, 1) + jnp.where(lax.rem(kind, 2) == 0, 0, half)
-    of_pack = iota((side, 1), 0) * side + jnp.where(odd == 1, side - 1, 0)
-    for j, row in enumerate(rows):
-        at = ids[:, j : j + 1]
-        twice = jnp.concatenate([row[:, :channels], row[:, :channels]], axis=1)
-        sums = jnp.where(of_sum == at, twice, sums)
-        total, peak = (row[:, channels + i : channels + i + 1] for i in range(2))
-        ends = jnp.where((of_end == at) & (kind < 4), jnp.where(kind < 2, total, peak), ends)
+    of_end = jnp.where(kind < 4, of_end, 2 * half)
+    of_pack = iota(pack.shape, 0) * side + jnp.where(odd == 1, side - 1, 0)
+    lane = iota((1, LANES), 1)
+    for j in range(LATE):
+        at, row, total, top = (v[j : j + 1] for v in (ids_ref[...], rows, totals, peak))
+        sums = jnp.where(of_sum == at, row, sums)
+        ends = jnp.where(of_end == at, jnp.where(kind < 2, total, top), ends)
+        row = jnp.where(lane < channels, row, jnp.where(lane == channels, total, top))
         pack = jnp.where(of_pack == at, row, pack)
     stats_ref[:half, :], stats_ref[half:, :] = sums, ends
     pack_ref[...] = pack
@@ -261,14 +266,17 @@
     return first_factor, second_factor, total, peak
 
 
-def spread(*row_pairs):
-    rows = jnp.concatenate(row_pairs, axis=0)
+def turned(*rows):
+    rows = jnp.concatenate(rows, axis=0)
     gap = jnp.zeros((LANES - rows.shape[0], rows.shape[1]), jnp.float32)
-    columns = jnp.transpose(jnp.concatenate([rows, gap], axis=0))
+    return jnp.transpose(jnp.concatenate([rows, gap], axis=0))
+
+
+def spread(columns, count):
     left = iota((columns.shape[0], LANES), 1) < LANES // 2
     return [
         jnp.where(left, columns[:, 2 * i : 2 * i + 1], columns[:, 2 * i + 1 : 2 * i + 2])
-        for i in range(len(row_pairs))
+        for i in range(count)
     ]
 
 
@@ -280,7 +288,7 @@
 def merge_kernel(own_ref, other_ref, out_ref):
     half = own_ref.shape[0] - ROWS
     first_factor, second_factor, total, peak = shares(own_ref[half:, :], other_ref[half:, :])
-    first_factor, second_factor = spread(first_factor, second_factor)
+    first_factor, second_factor = spread(turned(first_factor, second_factor), 2)
     out_ref[:half, :] = own_ref[:half, :] * first_factor + other_ref[:half, :] * second_factor
     rest = jnp.zeros((ROWS - 4, total.shape[1]), jnp.float32)
     out_ref[half:, :] = jnp.concatenate([total, peak, rest], axis=0)
@@ -292,13 +300,11 @@
 
 def weights_kernel(value_ref, near_ref, hp_ref, after_ref, hpv_ref, taps_ref, code_ref, pick_ref):
     del after_ref
-    sensor = lax.axis_index("sensor")
     cell = lax.axis_index("cell")
     channels = value_ref.shape[0]
     cells = near_ref.shape[1]
     side = math.isqrt(cells)
-    out_rows = hpv_ref.shape[0] * channels // hp_ref.shape[1]
-    own_hp = hp_ref[pl.ds(pl.multiple_of(sensor * out_rows, ROWS), out_rows), :]
+    out_rows, own_hp = hp_ref.shape[0], hp_ref[...]
     value = value_ref[...]
     taps = [
         own_hp[:, k * channels : (k + 1) * channels] for k in range(hp_ref.shape[1] // channels)
@@ -306,7 +312,8 @@
     hpv = dot(jnp.concatenate(taps, axis=0), value, NN)
     hpv_ref[...] = hpv
     high, low = halves(hpv[out_rows:])
-    taps_ref[...] = jnp.concatenate([high, high, low], axis=1)
+    gap = jnp.zeros(low.shape, jnp.float32).astype(jnp.bfloat16)
+    taps_ref[...] = jnp.concatenate([high, high, low, gap], axis=1)
 
     shift = side.bit_length() - 1
     odd = lax.rem(cell, 2)
@@ -321,21 +328,30 @@
         pick_ref[2 * side * k : 2 * side * (k + 1), :] = here
 
 
-def mean_kernel(own_ref, other_ref, mean_ref, pack_ref):
+def mean_kernel(own_ref, other_ref, pack_ref, columns_ref):
     odd = lax.rem(lax.axis_index("cell"), 2)
-    half = mean_ref.shape[0]
-    side = half // pack_ref.shape[0]
+    half = own_ref.shape[0] - ROWS
+    count = pack_ref.shape[0]
+    side = half // count
     first_factor, second_factor, total, _ = shares(own_ref[half:, :], other_ref[half:, :])
-    first_share, second_share = spread(first_factor / total, second_factor / total)
-    mean_ref[...] = own_ref[:half, :] * first_share + other_ref[:half, :] * second_share
-    left = mean_ref[pl.ds(0, half // side, stride=side), :]
-    right = mean_ref[pl.ds(side - 1, half // side, stride=side), :]
-    pack_ref[...] = jnp.where(odd == 1, left, right)
-
-
-def own_kernel(mean_ref, hpv_ref, code_ref, out_ref):
+    columns_ref[...] = turned(first_factor / total, second_factor / total)
+
+    def column(ref):
+        left = ref[pl.ds(0, count, stride=side), :]
+        return jnp.where(odd == 1, left, ref[pl.ds(side - 1, count, stride=side), :])
+
+    first_share, second_share = spread(column(columns_ref), 2)
+    pack_ref[...] = column(own_ref) * first_share + column(other_ref) * second_share
+
+
+def own_kernel(own_ref, other_ref, hpv_ref, code_ref, out_ref):
     out_rows, cells = out_ref.shape
-    mean, hpv = mean_ref[...], hpv_ref[...]
+    half = own_ref.shape[0] - ROWS
+    first_factor, second_factor, total, _ = shares(own_ref[half:, :], other_ref[half:, :])
+    columns = turned(first_factor / total, second_factor / total)
+    first_share, second_share = spread(columns, 2)
+    mean = own_ref[:half, :] * first_share + other_ref[:half, :] * second_share
+    hpv = hpv_ref[...]
     gap = jnp.zeros(hpv.shape, jnp.float32)
     mixed = [
         dot(jnp.concatenate(pair, axis=1), mean, NT, CLOSE) for pair in ((hpv, gap), (gap, hpv))
@@ -370,12 +386,16 @@
     b = mean_of(own_b_ref[...], other_b_ref[...], channels)
     b = jnp.where((cell == 0) | (cell == last), 0.0, b)
     a = a_ref[...]
-    halo = jnp.concatenate([a[:, :channels], a[:, channels:], b[:, :channels]], axis=0)
-    high, low = halves(halo)
+    a = [twice(a), twice(jnp.concatenate([a[:, channels:], a[:, :channels]], axis=1))]
+    halo = jnp.concatenate(a + [b], axis=0)
     cells = halo.shape[0]
     turns = LANES // cells
-    halo = jnp.concatenate([jnp.concatenate([high, low, high], axis=1)] * turns, axis=0)
-    edge = dot(taps_ref[...], halo, NT, None)
+    left = iota(halo.shape, 1) < channels
+    high = halo.astype(jnp.bfloat16).astype(jnp.float32)
+    halo = jnp.concatenate(
+        [jnp.where(left, high, halo - high), jnp.where(left, high, 0.0)], axis=1
+    ).astype(jnp.bfloat16)
+    edge = dot(taps_ref[...], jnp.concatenate([halo] * turns, axis=0), NT, None)
     lane = iota((out_rows, LANES), 1)
     groups = []
     for start in range(0, edge.shape[0], turns * out_rows):
@@ -458,39 +478,46 @@
     def like(*args):
         return [shape(*a.shape, dtype=a.dtype) for a in args]
 
-    args = [swath, enc_weight, key_weight, cell_query, quality, sample_cell]
-    swath, enc_weight, key_weight, cell_query, quality, sample_cell, tail = call(
+    args = [
+        swath,
+        cell_query,
+        enc_weight,
+        key_weight,
+        quality,
+        sample_cell,
+        value_weight,
+        neighbours,
+        hp_weight,
+    ]
+    *loaded, tail = call(
         load_kernel,
         pinned(*args),
-        like(*args) + [shape(ROWS, LANES)],
+        like(*args[:-1]) + [shape(out_rows, hp_weight.shape[1]), shape(ROWS, LANES)],
         in_specs=[hbm] * len(args),
         scratch_shapes=[
             pltpu.VMEM((channels, LANES), jnp.float32),
             pltpu.SemaphoreType.DMA((len(args) + 1,)),
         ],
     )
+    swath, cell_query, enc_weight, key_weight, quality, sample_cell, *loaded = loaded
     tail_b = lax.ppermute(tail, axes, far(0))
     tail_again = call(copy_kernel, [tail], shape(*tail.shape), cost=100_000_000)
     tail_a = lax.ppermute(tail_again, axes, near)
 
-    args = [value_weight, neighbours, hp_weight]
-    before, late_taps, ids, late_kq, late_rest, rest, rest_pack, *loaded = call(
+    before, late_taps, ids, late, rest, rest_pack = call(
         prepare_kernel,
-        [swath, enc_weight, key_weight, cell_query, quality, sample_cell, live] + pinned(*args),
+        [swath, enc_weight, key_weight, cell_query, quality, sample_cell, live],
         [
-            shape(ROWS, channels),
-            shape(channels, 6 * LATE * channels, dtype=jnp.bfloat16),
-            shape(1, LANES, dtype=jnp.int32),
-            shape(ROWS, LANES),
-            shape(ROWS, LANES),
+            shape(ROWS, 2 * channels),
+            shape(2 * channels, 6 * LATE * channels, dtype=jnp.bfloat16),
+            shape(ROWS, LANES, dtype=jnp.int32),
+            shape(6, ROWS, LANES),
             shape(cells // 2 + ROWS, LANES),
             shape(side, LANES),
-        ]
-        + like(*args),
+        ],
         cost=200_000_000,
-        in_specs=[vmem] * 6 + [pl.BlockSpec(memory_space=pltpu.SMEM)] + [hbm] * len(args),
-        scratch_shapes=[pltpu.VMEM((cells, LANES), jnp.float32)] * 2
-        + [pltpu.SemaphoreType.DMA((len(args),))],
+        in_specs=[vmem] * 6 + [pl.BlockSpec(memory_space=pltpu.SMEM)],
+        scratch_shapes=[pltpu.VMEM((cells, LANES), jnp.float32)] * 2,
     )
     stats, pack = call(
         pool_kernel,
@@ -500,9 +527,7 @@
             tail_b,
             before,
             ids,
-            quality,
-            late_kq,
-            late_rest,
+            late,
             rest,
             rest_pack,
         ],
@@ -524,20 +549,21 @@
         loaded + [pack_again],
         [
             shape(stencil * out_rows, channels),
-            shape((stencil - 1) * out_rows, 3 * channels, dtype=jnp.bfloat16),
+            shape((stencil - 1) * out_rows, 4 * channels, dtype=jnp.bfloat16),
             shape(*neighbours.shape, dtype=jnp.int32),
             shape((stencil - 1) * 2 * side, cells, dtype=jnp.bfloat16),
         ],
         cost=100_000_000,
     )
     own_b = lax.ppermute(pack_again, axes, far(0))
-    mean, mean_a = call(
+    mean_a = call(
         mean_kernel,
         [stats, other],
-        [shape(cells // 2, LANES), shape(side // 2, LANES)],
+        shape(side // 2, LANES),
+        scratch_shapes=[pltpu.VMEM((cells // 2, LANES), jnp.float32)],
     )
     halo_a = lax.ppermute(mean_a, axes, near)
-    partial = call(own_kernel, [mean, hpv, code], shape(out_rows, cells), cost=200_000_000)
+    partial = call(own_kernel, [stats, other, hpv, code], shape(out_rows, cells), cost=200_000_000)
     return call(
         functools.partial(halo_kernel, channels, ranges - 1),
         [halo_a, own_b, other_b, partial, taps, pick],

time: 14.4 us -> 14.1 us (0.979)
  Pallas kernels: 5.68 us -> 5.46 us
    pallas_call x9, Pallas kernels: 5.68 us -> 5.46 us  [call(): pl.pallas_call(kernel, out_shape=outs, compiler_params=pltpu.CompilerPara...]
  transfers between devices with their start and end apart: 6 -> 6, of which waited for: 1 -> 1; matrix products, arithmetic and copies ran while one was open for 0% -> 0% of each run, Pallas kernels for 20% -> 21%
where the time goes in v7:
time: 14.1 us; the launch traced here: 13.9 us
  starting transfers between devices  6.34 us (45%)
  Pallas kernels  5.46 us (39%)
  waiting for transfers between devices  1.42 us (10%)
  between operations  0.69 us (5%)
    pallas_call x9, Pallas kernels, call(): pl.pallas_call(kernel, out_shape=outs, compiler_params=pltpu.CompilerPara...  5.46 us
    ppermute x1, starting transfers between devices, on_device(): other_b = lax.ppermute(pack, axes, far(flip))  2.05 us
    ppermute x1, starting transfers between devices, on_device(): tail_b = lax.ppermute(tail, axes, far(0))  1.86 us
    ppermute x1, waiting for transfers between devices, on_device(): own_b = lax.ppermute(pack_again, axes, far(0))  1.39 us
    ppermute x1, starting transfers between devices, on_device(): other = lax.ppermute(stats, axes, across(flip))  1.28 us
    ppermute x1, starting transfers between devices, on_device(): halo_a = lax.ppermute(mean_a, axes, near)  0.58 us
    ppermute x1, starting transfers between devices, on_device(): own_b = lax.ppermute(pack_again, axes, far(0))  0.56 us
  transfers between devices with their start and end apart: 6, of which 1 were waited for; matrix products, arithmetic and copies ran while one was open for 0% of the time, Pallas kernels for 21%

profile of v7, /device:TPU:13, one launch (start us, length us, event | category | flops | bytes accessed | tf_op | source)
XLA Modules:
  0.0 13.9 jit_solution(10900577153260593306)
XLA Ops:
  0.0 1.1 %shard_map.100 = (f32[1,64,512]{2,1,0:T(8,128)S(1)}, f32[64,256]{1,0:T(8,128)S(1)}, f32[1,64,192]{2,1,0:T(8,128)S(1)}, f32[64,64]{1,0:T(8,128)S(1)}, f32[1,512]{...) custom-call(f32[1,64,512]{2,1,0:T(8,128)} %refs_0_.1, ...), custom_call_target="tpu_custom_call" | custom-call | tf_op jit(solution)/shard_map/pallas_call | solution.py:461
  1.1 1.9 %collective-permute-start.1 = (f32[8,128]{1,0:T(8,128)S(1)}, f32[8,128]{1,0:T(8,128)S(1)}, u32[]{:S(2)}, u32[]{:S(2)}) collective-permute-start(f32[8,128]{1,0:T(8,128)S(1)} %get-tuple-element.34.in_ref), channel_id=1, source_target_pairs={{0,16},{1,2},{2,1},{3,4},{4,3},{5,6},{6,5},{7,8},{8,7},{9,10},{10,... | collective-permute-start | bytes 12296 | tf_op jit(solution)/shard_map/ppermute | solution.py:503
  3.0 0.0 collective-permute-start
  3.6 1.4 %shard_map.101 = (f32[8,128]{1,0:T(8,128)S(1)}, bf16[128,768]{1,0:T(8,128)(2,1)S(1)}, s32[8,128]{1,0:T(8,128)S(1)}, f32[6,8,128]{2,1,0:T(8,128)S(1)}, f32[136,128]{1,0:T(8,128)S(1)}, /*index=5*/f32[16,128]{1,0:T(8,128)S(1)}) custom-call(f32[1,64,512]{2,1,0:T(8,128)S(1)} %get-tuple-element.27.swath_ref, f32[1,64,192]{2,1,0:T(8,128)S(1)} %get-tuple-element.28.enc_ref, ...), custom_call_target="tpu_custom_call" | custom-call | flops 200000000 | bytes 2000000 | tf_op jit(solution)/shard_map/pallas_call | solution.py:461
  5.1 0.0 collective-permute-done.tail_a_ref
  5.1 0.0 collective-permute-done.1.tail_b_ref
  5.1 0.3 %shard_map.103 = (f32[136,128]{1,0:T(8,128)S(1)}, f32[16,128]{1,0:T(8,128)S(1)}) custom-call(bf16[128,768]{1,0:T(8,128)(2,1)S(1)} %get-tuple-element.33.taps_ref, f32[8,128]{1,0:T(8,128)S(1)} %collective-permute-done.tail_a_ref, f32[8,128]{1,0:T(8,128)S(1)} %collective-permute-done.1.tail_b_ref, f32[8,128]{1,0:T(8,128)S(1)} %get-tuple-element.35.before_ref, ...), custom_call_target="tpu_custom_call" | custom-call | tf_op jit(solution)/shard_map/pallas_call | solution.py:461
  5.4 1.3 %collective-permute-start.2 = (f32[136,128]{1,0:T(8,128)S(1)}, f32[136,128]{1,0:T(8,128)S(1)}, u32[]{:S(2)}, u32[]{:S(2)}) collective-permute-start(f32[136,128]{1,0:T(8,128)S(1)} %get-tuple-element.40.own_ref), channel_id=1, source_target_pairs={{0,16},{1,17},{2,18},{3,19},{4,20},{5,21},{6,22},{7,23},{8,24},{9,... | collective-permute-start | bytes 208904 | tf_op jit(solution)/shard_map/ppermute | solution.py:544
  6.7 2.1 %collective-permute-start.5 = (f32[16,128]{1,0:T(8,128)S(1)}, f32[16,128]{1,0:T(8,128)S(1)}, u32[]{:S(2)}, u32[]{:S(2)}) collective-permute-start(f32[16,128]{1,0:T(8,128)S(1)} %get-tuple-element.41.in_ref), channel_id=1, source_target_pairs={{0,16},{1,18},{2,17},{3,20},{4,19},{5,22},{6,21},{7,24},{8,23},{9,... | collective-permute-start | bytes 24584 | tf_op jit(solution)/shard_map/ppermute | solution.py:545
  8.7 0.6 %collective-permute-start.4 = (f32[16,128]{1,0:T(8,128)S(1)}, f32[16,128]{1,0:T(8,128)S(1)}, u32[]{:S(2)}, u32[]{:S(2)}) collective-permute-start(f32[16,128]{1,0:T(8,128)S(1)} %shard_map.105.after_ref), channel_id=1, source_target_pairs={{0,16},{1,2},{2,1},{3,4},{4,3},{5,6},{6,5},{7,8},{8,7},{9,10},{10,... | collective-permute-start | bytes 24584 | tf_op jit(solution)/shard_map/ppermute | solution.py:558
  9.3 0.4 %shard_map.106 = (f32[288,64]{1,0:T(8,128)S(1)}, bf16[256,256]{1,0:T(8,128)(2,1)S(1)}, s32[8,256]{1,0:T(8,128)S(1)}, bf16[256,256]{1,0:T(8,128)(2,1)S(1)}) custom-call(f32[64,64]{1,0:T(8,128)S(1)} %get-tuple-element.42.value_ref, s32[8,256]{1,0:T(8,128)S(1)} %get-tuple-element.43.near_ref, f32[32,576]{1,0:T(8,128)S(1)} %get-tuple-element.44.hp_ref, ...), custom_call_target="tpu_custom_call" | custom-call | flops 100000000 | bytes 1000000 | tf_op jit(solution)/shard_map/pallas_call | solution.py:461
  9.7 0.0 collective-permute-done.2.other_ref
  9.7 0.2 %shard_map.104 = f32[8,128]{1,0:T(8,128)S(1)} custom-call(f32[136,128]{1,0:T(8,128)S(1)} %get-tuple-element.40.own_ref, f32[136,128]{1,0:T(8,128)S(1)} %collective-permute-done.2.other_ref), custom_call_target="tpu_custom_call" | custom-call | tf_op jit(solution)/shard_map/pallas_call | solution.py:461
  9.9 0.6 %collective-permute-start.3 = (f32[8,128]{1,0:T(8,128)S(1)}, f32[8,128]{1,0:T(8,128)S(1)}, u32[]{:S(2)}, u32[]{:S(2)}) collective-permute-start(f32[8,128]{1,0:T(8,128)S(1)} %shard_map.104), channel_id=1, source_target_pairs={{0,1},{1,0},{2,3},{3,2},{4,5},{5,4},{6,7},{7,6},{8,9},{9,8},{10,11... | collective-permute-start | bytes 12296 | tf_op jit(solution)/shard_map/ppermute | solution.py:565
  10.5 0.8 %shard_map.107.partial_ref = f32[32,256]{1,0:T(8,128)S(1)} custom-call(f32[136,128]{1,0:T(8,128)S(1)} %get-tuple-element.40.own_ref, f32[136,128]{1,0:T(8,128)S(1)} %collective-permute-done.2.other_ref, f32[288,64]{1,0:T(8,128)S(1)} %get-tuple-element.45.hpv_ref, s32[8,256]{1,0:T(8,128)S(1)} %get-tuple-element.46.code_ref), custom_call_target="tpu_custom_call" | custom-call | flops 200000000 | bytes 2000000 | tf_op jit(solution)/shard_map/pallas_call | solution.py:461
  11.3 1.4 %collective-permute-done.4.own_b_ref = f32[16,128]{1,0:T(8,128)S(1)} collective-permute-done((f32[16,128]{1,0:T(8,128)S(1)}, f32[16,128]{1,0:T(8,128)S(1)}, u32[]{:S(2)}, u32[]{:S(2)}) %collective-permute-start.4) | collective-permute-done | bytes 8224 | tf_op jit(solution)/shard_map/ppermute | solution.py:558
  12.7 0.0 collective-permute-done.5.other_b_ref
  12.7 0.0 collective-permute-done.3.a_ref
  12.7 1.2 %shard_map.108 = f32[32,256]{1,0:T(8,128)} custom-call(f32[8,128]{1,0:T(8,128)S(1)} %collective-permute-done.3.a_ref, f32[16,128]{1,0:T(8,128)S(1)} %collective-permute-done.4.own_b_ref, f32[16,128]{1,0:T(8,128)S(1)} %collective-permute-done.5.other_b_ref, f32[32,256]{1,0:T(8,128)S(1)} %shard_map.107.partial_ref, ...), custom_call_target="tpu_custom_call" | custom-call | tf_op jit(solution)/shard_map/pallas_call | solution.py:461
  (2 shorter events, 0.0 us)
Async XLA Ops:
  1.1 4.0 %collective-permute-start.1 = (f32[8,128]{1,0:T(8,128)S(1)}, f32[8,128]{1,0:T(8,128)S(1)}, u32[]{:S(2)}, u32[]{:S(2)}) collective-permute-start(f32[8,128]{1,0:T(8,128)S(1)} %get-tuple-element.34.in_ref), channel_id=1, source_target_pairs={{0,16},{1,2},{2,1},{3,4},{4,3},{5,6},{6,5},{7,8},{8,7},{9,10},{10,... | collective-permute-start | bytes 12296 | tf_op jit(solution)/shard_map/ppermute | solution.py:503
  3.0 2.1 %collective-permute-start = (f32[8,128]{1,0:T(8,128)S(1)}, f32[8,128]{1,0:T(8,128)S(1)}, u32[]{:S(2)}, u32[]{:S(2)}) collective-permute-start(f32[8,128]{1,0:T(8,128)S(1)} %shard_map.102), channel_id=1, source_target_pairs={{0,1},{1,0},{2,3},{3,2},{4,5},{5,4},{6,7},{7,6},{8,9},{9,8},{10,11... | collective-permute-start | bytes 12296 | tf_op jit(solution)/shard_map/ppermute | solution.py:505
  5.4 4.3 %collective-permute-start.2 = (f32[136,128]{1,0:T(8,128)S(1)}, f32[136,128]{1,0:T(8,128)S(1)}, u32[]{:S(2)}, u32[]{:S(2)}) collective-permute-start(f32[136,128]{1,0:T(8,128)S(1)} %get-tuple-element.40.own_ref), channel_id=1, source_target_pairs={{0,16},{1,17},{2,18},{3,19},{4,20},{5,21},{6,22},{7,23},{8,24},{9,... | collective-permute-start | bytes 208904 | tf_op jit(solution)/shard_map/ppermute | solution.py:544
  6.7 6.0 %collective-permute-start.5 = (f32[16,128]{1,0:T(8,128)S(1)}, f32[16,128]{1,0:T(8,128)S(1)}, u32[]{:S(2)}, u32[]{:S(2)}) collective-permute-start(f32[16,128]{1,0:T(8,128)S(1)} %get-tuple-element.41.in_ref), channel_id=1, source_target_pairs={{0,16},{1,18},{2,17},{3,20},{4,19},{5,22},{6,21},{7,24},{8,23},{9,... | collective-permute-start | bytes 24584 | tf_op jit(solution)/shard_map/ppermute | solution.py:545
  8.7 4.0 %collective-permute-start.4 = (f32[16,128]{1,0:T(8,128)S(1)}, f32[16,128]{1,0:T(8,128)S(1)}, u32[]{:S(2)}, u32[]{:S(2)}) collective-permute-start(f32[16,128]{1,0:T(8,128)S(1)} %shard_map.105.after_ref), channel_id=1, source_target_pairs={{0,16},{1,2},{2,1},{3,4},{4,3},{5,6},{6,5},{7,8},{8,7},{9,10},{10,... | collective-permute-start | bytes 24584 | tf_op jit(solution)/shard_map/ppermute | solution.py:558
  9.9 2.8 %collective-permute-start.3 = (f32[8,128]{1,0:T(8,128)S(1)}, f32[8,128]{1,0:T(8,128)S(1)}, u32[]{:S(2)}, u32[]{:S(2)}) collective-permute-start(f32[8,128]{1,0:T(8,128)S(1)} %shard_map.104), channel_id=1, source_target_pairs={{0,1},{1,0},{2,3},{3,2},{4,5},{5,4},{6,7},{7,6},{8,9},{9,8},{10,11... | collective-permute-start | bytes 12296 | tf_op jit(solution)/shard_map/ppermute | solution.py:565

commit v8 on v7

--- a/solution.py
+++ b/solution.py
@@ -16,7 +16,6 @@
 CLOSE = lax.Precision.HIGH
 NN = ((1,), (0,))
 NT = ((1,), (1,))
-TN = ((0,), (0,))
 
 
 def dot(left, right, contract, precision=EXACT):
@@ -26,6 +25,13 @@
         (contract, ((), ())),
         precision=precision,
         preferred_element_type=jnp.float32,
+    )
+
+
+def by_half(left, right, contract):
+    half = left.shape[0] // 2
+    return jnp.concatenate(
+        [dot(rows, right, contract, None) for rows in (left[:half], left[half:])], axis=0
     )
 
 
@@ -101,6 +107,20 @@
     rest = value - high.astype(jnp.float32)
     middle = rest.astype(jnp.bfloat16)
     return high, middle, (rest - middle.astype(jnp.float32)).astype(jnp.bfloat16)
+
+
+def exact(twofold, right):
+    high, middle, low = parts(twofold)
+    mixed = jnp.where(iota(high.shape, 1) < right.shape[0], high, low)
+    right_high, right_middle, right_low = parts(right)
+    return dot(
+        jnp.concatenate([high, middle, mixed], axis=1),
+        jnp.concatenate(
+            [right_high, right_middle, right_high, right_middle, right_low, right_high], axis=0
+        ),
+        NN,
+        None,
+    )
 
 
 def packed(block, channels):
@@ -146,24 +166,15 @@
     encoded = gelu(before)
 
     query = query_ref[...]
-    key_query = dot(key_ref[...], query, TN) * (1.0 / math.sqrt(channels))
-    key_query = jnp.transpose(jnp.concatenate([key_query, key_query], axis=0))
+    key = jnp.concatenate([key_ref[...]] * 2, axis=1)
+    key = jnp.transpose(jnp.concatenate([key, key], axis=0))
+    key_query = jnp.transpose(exact(key, query) * (1.0 / math.sqrt(channels)))
     query = jnp.transpose(jnp.concatenate([query, jnp.zeros(query.shape, jnp.float32)], axis=0))
     kq_ref[...] = key_query
     own_score = jnp.sum(query * key_query, axis=1, keepdims=True)
     own_score = jnp.where(sensor == 0, own_score, -jnp.inf)
 
-    high, middle, low = parts(key_query)
-    mixed = jnp.where(iota(high.shape, 1) < channels, high, low)
-    token_high, token_middle, token_low = parts(encoded)
-    score = dot(
-        jnp.concatenate([high, middle, mixed], axis=1),
-        jnp.concatenate(
-            [token_high, token_middle, token_high, token_middle, token_low, token_high], axis=0
-        ),
-        NN,
-        None,
-    )
+    score = exact(key_query, encoded)
     slot = iota((1, slots), 1)
     ids = jnp.where(slot < live_ref[0, 0], cell_ref[...], -1)
     late_ids = [ids[:, j : j + 1] for j in range(LATE)]
@@ -175,8 +186,9 @@
     tokens = jnp.concatenate([encoded, (place == 0).astype(jnp.float32)], axis=0)
     high, low = halves(jnp.transpose(tokens))
     weights_high, weights_low = halves(weights)
-    wide = dot(weights_high, jnp.concatenate([high, low], axis=1), NN, None)
-    block = wide[:, :LANES] + wide[:, LANES:] + dot(weights_low, high, NN, None)
+    both = jnp.concatenate([high, low], axis=1)
+    wide = by_half(weights_high, both, NN)
+    block = wide[:, :LANES] + wide[:, LANES:] + by_half(weights_low, high, NN)
     own = jnp.where(iota(query.shape, 1) == channels, 1.0, query)
     block = with_peak(block + own * jnp.exp(own_score - peak), peak, channels)
     block_ref[...] = block
@@ -395,7 +407,7 @@
     halo = jnp.concatenate(
         [jnp.where(left, high, halo - high), jnp.where(left, high, 0.0)], axis=1
     ).astype(jnp.bfloat16)
-    edge = dot(taps_ref[...], jnp.concatenate([halo] * turns, axis=0), NT, None)
+    edge = by_half(taps_ref[...], jnp.concatenate([halo] * turns, axis=0), NT)
     lane = iota((out_rows, LANES), 1)
     groups = []
     for start in range(0, edge.shape[0], turns * out_rows):
@@ -406,7 +418,8 @@
         groups.append(group)
     high, low = halves(jnp.concatenate(groups, axis=1))
     pick = pick_ref[...]
-    out_ref[...] = partial_ref[...] + (dot(high, pick, NN, None) + dot(low, pick, NN, None))
+    both = dot(jnp.concatenate([high, low], axis=0), pick, NN, None)
+    out_ref[...] = partial_ref[...] + (both[:out_rows] + both[out_rows:])
 
 
 def swaps(sensors, cells):

time: 14.1 us -> 14.1 us (level)
  waiting for transfers between devices: 1.42 us -> 1.57 us
  transfers between devices with their start and end apart: 6 -> 6, of which waited for: 1 -> 2; matrix products, arithmetic and copies ran while one was open for 0% -> 0% of each run, Pallas kernels for 21% -> 20%
where the time goes in v8:
time: 14.1 us; the launch traced here: 13.9 us
  starting transfers between devices  6.27 us (44%)
  Pallas kernels  5.34 us (38%)
  waiting for transfers between devices  1.57 us (11%)
  between operations  0.69 us (5%)
    pallas_call x9, Pallas kernels, call(): pl.pallas_call(kernel, out_shape=outs, compiler_params=pltpu.CompilerPara...  5.34 us
    ppermute x1, starting transfers between devices, on_device(): other_b = lax.ppermute(pack, axes, far(flip))  2.05 us
    ppermute x1, starting transfers between devices, on_device(): tail_b = lax.ppermute(tail, axes, far(0))  1.86 us
    ppermute x1, waiting for transfers between devices, on_device(): own_b = lax.ppermute(pack_again, axes, far(0))  1.46 us
    ppermute x1, starting transfers between devices, on_device(): other = lax.ppermute(stats, axes, across(flip))  1.28 us
    ppermute x1, starting transfers between devices, on_device(): own_b = lax.ppermute(pack_again, axes, far(0))  0.56 us
    ppermute x1, starting transfers between devices, on_device(): halo_a = lax.ppermute(mean_a, axes, near)  0.51 us
  transfers between devices with their start and end apart: 6, of which 2 were waited for; matrix products, arithmetic and copies ran while one was open for 0% of the time, Pallas kernels for 20%

profile of v8, /device:TPU:13, one launch (start us, length us, event | category | flops | bytes accessed | tf_op | source)
XLA Modules:
  0.0 13.9 jit_solution(11381049984689594218)
XLA Ops:
  0.0 1.1 %shard_map.100 = (f32[1,64,512]{2,1,0:T(8,128)S(1)}, f32[64,256]{1,0:T(8,128)S(1)}, f32[1,64,192]{2,1,0:T(8,128)S(1)}, f32[64,64]{1,0:T(8,128)S(1)}, f32[1,512]{...) custom-call(f32[1,64,512]{2,1,0:T(8,128)} %refs_0_.1, ...), custom_call_target="tpu_custom_call" | custom-call | tf_op jit(solution)/shard_map/pallas_call | solution.py:474
  1.1 1.9 %collective-permute-start.1 = (f32[8,128]{1,0:T(8,128)S(1)}, f32[8,128]{1,0:T(8,128)S(1)}, u32[]{:S(2)}, u32[]{:S(2)}) collective-permute-start(f32[8,128]{1,0:T(8,128)S(1)} %get-tuple-element.34.in_ref), channel_id=1, source_target_pairs={{0,16},{1,2},{2,1},{3,4},{4,3},{5,6},{6,5},{7,8},{8,7},{9,10},{10,... | collective-permute-start | bytes 12296 | tf_op jit(solution)/shard_map/ppermute | solution.py:516
  3.0 0.0 collective-permute-start
  3.6 1.4 %shard_map.101 = (f32[8,128]{1,0:T(8,128)S(1)}, bf16[128,768]{1,0:T(8,128)(2,1)S(1)}, s32[8,128]{1,0:T(8,128)S(1)}, f32[6,8,128]{2,1,0:T(8,128)S(1)}, f32[136,128]{1,0:T(8,128)S(1)}, /*index=5*/f32[16,128]{1,0:T(8,128)S(1)}) custom-call(f32[1,64,512]{2,1,0:T(8,128)S(1)} %get-tuple-element.27.swath_ref, f32[1,64,192]{2,1,0:T(8,128)S(1)} %get-tuple-element.28.enc_ref, ...), custom_call_target="tpu_custom_call" | custom-call | flops 200000000 | bytes 2000000 | tf_op jit(solution)/shard_map/pallas_call | solution.py:474
  5.0 0.0 collective-permute-done.tail_a_ref
  5.0 0.1 collective-permute-done.1.tail_b_ref
  5.1 0.3 %shard_map.103 = (f32[136,128]{1,0:T(8,128)S(1)}, f32[16,128]{1,0:T(8,128)S(1)}) custom-call(bf16[128,768]{1,0:T(8,128)(2,1)S(1)} %get-tuple-element.33.taps_ref, f32[8,128]{1,0:T(8,128)S(1)} %collective-permute-done.tail_a_ref, f32[8,128]{1,0:T(8,128)S(1)} %collective-permute-done.1.tail_b_ref, f32[8,128]{1,0:T(8,128)S(1)} %get-tuple-element.35.before_ref, ...), custom_call_target="tpu_custom_call" | custom-call | tf_op jit(solution)/shard_map/pallas_call | solution.py:474
  5.4 1.3 %collective-permute-start.2 = (f32[136,128]{1,0:T(8,128)S(1)}, f32[136,128]{1,0:T(8,128)S(1)}, u32[]{:S(2)}, u32[]{:S(2)}) collective-permute-start(f32[136,128]{1,0:T(8,128)S(1)} %get-tuple-element.40.own_ref), channel_id=1, source_target_pairs={{0,16},{1,17},{2,18},{3,19},{4,20},{5,21},{6,22},{7,23},{8,24},{9,... | collective-permute-start | bytes 208904 | tf_op jit(solution)/shard_map/ppermute | solution.py:557
  6.7 2.1 %collective-permute-start.5 = (f32[16,128]{1,0:T(8,128)S(1)}, f32[16,128]{1,0:T(8,128)S(1)}, u32[]{:S(2)}, u32[]{:S(2)}) collective-permute-start(f32[16,128]{1,0:T(8,128)S(1)} %get-tuple-element.41.in_ref), channel_id=1, source_target_pairs={{0,16},{1,18},{2,17},{3,20},{4,19},{5,22},{6,21},{7,24},{8,23},{9,... | collective-permute-start | bytes 24584 | tf_op jit(solution)/shard_map/ppermute | solution.py:558
  8.7 0.6 %collective-permute-start.4 = (f32[16,128]{1,0:T(8,128)S(1)}, f32[16,128]{1,0:T(8,128)S(1)}, u32[]{:S(2)}, u32[]{:S(2)}) collective-permute-start(f32[16,128]{1,0:T(8,128)S(1)} %shard_map.105.after_ref), channel_id=1, source_target_pairs={{0,16},{1,2},{2,1},{3,4},{4,3},{5,6},{6,5},{7,8},{8,7},{9,10},{10,... | collective-permute-start | bytes 24584 | tf_op jit(solution)/shard_map/ppermute | solution.py:571
  9.3 0.4 %shard_map.106 = (f32[288,64]{1,0:T(8,128)S(1)}, bf16[256,256]{1,0:T(8,128)(2,1)S(1)}, s32[8,256]{1,0:T(8,128)S(1)}, bf16[256,256]{1,0:T(8,128)(2,1)S(1)}) custom-call(f32[64,64]{1,0:T(8,128)S(1)} %get-tuple-element.42.value_ref, s32[8,256]{1,0:T(8,128)S(1)} %get-tuple-element.43.near_ref, f32[32,576]{1,0:T(8,128)S(1)} %get-tuple-element.44.hp_ref, ...), custom_call_target="tpu_custom_call" | custom-call | flops 100000000 | bytes 1000000 | tf_op jit(solution)/shard_map/pallas_call | solution.py:474
  9.7 0.0 collective-permute-done.2.other_ref
  9.7 0.2 %shard_map.104 = f32[8,128]{1,0:T(8,128)S(1)} custom-call(f32[136,128]{1,0:T(8,128)S(1)} %get-tuple-element.40.own_ref, f32[136,128]{1,0:T(8,128)S(1)} %collective-permute-done.2.other_ref), custom_call_target="tpu_custom_call" | custom-call | tf_op jit(solution)/shard_map/pallas_call | solution.py:474
  9.9 0.5 %collective-permute-start.3 = (f32[8,128]{1,0:T(8,128)S(1)}, f32[8,128]{1,0:T(8,128)S(1)}, u32[]{:S(2)}, u32[]{:S(2)}) collective-permute-start(f32[8,128]{1,0:T(8,128)S(1)} %shard_map.104), channel_id=1, source_target_pairs={{0,1},{1,0},{2,3},{3,2},{4,5},{5,4},{6,7},{7,6},{8,9},{9,8},{10,11... | collective-permute-start | bytes 12296 | tf_op jit(solution)/shard_map/ppermute | solution.py:578
  10.4 0.8 %shard_map.107.partial_ref = f32[32,256]{1,0:T(8,128)S(1)} custom-call(f32[136,128]{1,0:T(8,128)S(1)} %get-tuple-element.40.own_ref, f32[136,128]{1,0:T(8,128)S(1)} %collective-permute-done.2.other_ref, f32[288,64]{1,0:T(8,128)S(1)} %get-tuple-element.45.hpv_ref, s32[8,256]{1,0:T(8,128)S(1)} %get-tuple-element.46.code_ref), custom_call_target="tpu_custom_call" | custom-call | flops 200000000 | bytes 2000000 | tf_op jit(solution)/shard_map/pallas_call | solution.py:474
  11.2 1.5 %collective-permute-done.4.own_b_ref = f32[16,128]{1,0:T(8,128)S(1)} collective-permute-done((f32[16,128]{1,0:T(8,128)S(1)}, f32[16,128]{1,0:T(8,128)S(1)}, u32[]{:S(2)}, u32[]{:S(2)}) %collective-permute-start.4) | collective-permute-done | bytes 8224 | tf_op jit(solution)/shard_map/ppermute | solution.py:571
  12.7 0.0 collective-permute-done.5.other_b_ref
  12.7 0.0 collective-permute-done.3.a_ref
  12.7 1.2 %shard_map.108 = f32[32,256]{1,0:T(8,128)} custom-call(f32[8,128]{1,0:T(8,128)S(1)} %collective-permute-done.3.a_ref, f32[16,128]{1,0:T(8,128)S(1)} %collective-permute-done.4.own_b_ref, f32[16,128]{1,0:T(8,128)S(1)} %collective-permute-done.5.other_b_ref, f32[32,256]{1,0:T(8,128)S(1)} %shard_map.107.partial_ref, ...), custom_call_target="tpu_custom_call" | custom-call | tf_op jit(solution)/shard_map/pallas_call | solution.py:474
  (2 shorter events, 0.0 us)
Async XLA Ops:
  1.1 4.0 %collective-permute-start.1 = (f32[8,128]{1,0:T(8,128)S(1)}, f32[8,128]{1,0:T(8,128)S(1)}, u32[]{:S(2)}, u32[]{:S(2)}) collective-permute-start(f32[8,128]{1,0:T(8,128)S(1)} %get-tuple-element.34.in_ref), channel_id=1, source_target_pairs={{0,16},{1,2},{2,1},{3,4},{4,3},{5,6},{6,5},{7,8},{8,7},{9,10},{10,... | collective-permute-start | bytes 12296 | tf_op jit(solution)/shard_map/ppermute | solution.py:516
  3.0 2.0 %collective-permute-start = (f32[8,128]{1,0:T(8,128)S(1)}, f32[8,128]{1,0:T(8,128)S(1)}, u32[]{:S(2)}, u32[]{:S(2)}) collective-permute-start(f32[8,128]{1,0:T(8,128)S(1)} %shard_map.102), channel_id=1, source_target_pairs={{0,1},{1,0},{2,3},{3,2},{4,5},{5,4},{6,7},{7,6},{8,9},{9,8},{10,11... | collective-permute-start | bytes 12296 | tf_op jit(solution)/shard_map/ppermute | solution.py:518
  5.4 4.3 %collective-permute-start.2 = (f32[136,128]{1,0:T(8,128)S(1)}, f32[136,128]{1,0:T(8,128)S(1)}, u32[]{:S(2)}, u32[]{:S(2)}) collective-permute-start(f32[136,128]{1,0:T(8,128)S(1)} %get-tuple-element.40.own_ref), channel_id=1, source_target_pairs={{0,16},{1,17},{2,18},{3,19},{4,20},{5,21},{6,22},{7,23},{8,24},{9,... | collective-permute-start | bytes 208904 | tf_op jit(solution)/shard_map/ppermute | solution.py:557
  6.7 6.0 %collective-permute-start.5 = (f32[16,128]{1,0:T(8,128)S(1)}, f32[16,128]{1,0:T(8,128)S(1)}, u32[]{:S(2)}, u32[]{:S(2)}) collective-permute-start(f32[16,128]{1,0:T(8,128)S(1)} %get-tuple-element.41.in_ref), channel_id=1, source_target_pairs={{0,16},{1,18},{2,17},{3,20},{4,19},{5,22},{6,21},{7,24},{8,23},{9,... | collective-permute-start | bytes 24584 | tf_op jit(solution)/shard_map/ppermute | solution.py:558
  8.7 4.0 %collective-permute-start.4 = (f32[16,128]{1,0:T(8,128)S(1)}, f32[16,128]{1,0:T(8,128)S(1)}, u32[]{:S(2)}, u32[]{:S(2)}) collective-permute-start(f32[16,128]{1,0:T(8,128)S(1)} %shard_map.105.after_ref), channel_id=1, source_target_pairs={{0,16},{1,2},{2,1},{3,4},{4,3},{5,6},{6,5},{7,8},{8,7},{9,10},{10,... | collective-permute-start | bytes 24584 | tf_op jit(solution)/shard_map/ppermute | solution.py:571
  9.9 2.8 %collective-permute-start.3 = (f32[8,128]{1,0:T(8,128)S(1)}, f32[8,128]{1,0:T(8,128)S(1)}, u32[]{:S(2)}, u32[]{:S(2)}) collective-permute-start(f32[8,128]{1,0:T(8,128)S(1)} %shard_map.104), channel_id=1, source_target_pairs={{0,1},{1,0},{2,3},{3,2},{4,5},{5,4},{6,7},{7,6},{8,9},{9,8},{10,11... | collective-permute-start | bytes 12296 | tf_op jit(solution)/shard_map/ppermute | solution.py:578

commit v9 on v8

--- a/solution.py
+++ b/solution.py
@@ -64,14 +64,14 @@
     return jnp.concatenate([half, half], axis=1)
 
 
-def mean_of(first, second, channels):
+def shares_of(first, second, channels):
     (first_total, first_peak), (second_total, second_peak) = (
         [v[:, channels + i : channels + i + 1] for i in range(2)] for v in (first, second)
     )
     peak = jnp.maximum(first_peak, second_peak)
     first_factor, second_factor = jnp.exp(first_peak - peak), jnp.exp(second_peak - peak)
     total = first_total * first_factor + second_total * second_factor
-    return twice(first) * (first_factor / total) + twice(second) * (second_factor / total)
+    return first_factor / total, second_factor / total
 
 
 def load_kernel(*refs):
@@ -214,9 +214,9 @@
     ids_ref[...] = jnp.concatenate(
         [jnp.broadcast_to(i, (1, LANES)) for i in late_ids] + [gap.astype(jnp.int32)], axis=0
     )
-    high, middle, low = parts(enc_ref[0, :, : LATE * channels])
-    taps = jnp.concatenate([high, high, middle, high, middle, low], axis=1)
-    taps_ref[...] = jnp.concatenate([taps, taps], axis=0)
+    first = enc_ref[0, :, : LATE * channels]
+    high, middle, low = parts(jnp.transpose(jnp.concatenate([first, first], axis=0)))
+    taps_ref[...] = jnp.concatenate([high, high, middle, high, middle, low], axis=0)
 
 
 def swapped(value):
@@ -243,7 +243,7 @@
     tail = jnp.where(cell == 0, 0.0, tail)
     high, middle, low = parts(jnp.concatenate([tail, jnp.zeros(tail.shape, jnp.float32)], axis=0))
     tail = jnp.concatenate([high, middle, high, low, middle, high], axis=1)
-    tokens = gelu(before_ref[...] + dot(tail, taps_ref[...], NT, None)[:ROWS, :])
+    tokens = gelu(before_ref[...] + dot(tail, taps_ref[...], NN, None)[:ROWS, :])
 
     key_query, rest, rest_total, rest_peak, quality, same = (late_ref[i] for i in range(6))
     score = jnp.sum(tokens * key_query, axis=1, keepdims=True) + quality
@@ -334,10 +334,11 @@
     ahead = cells + (1 - odd) * side + lax.shift_right_arithmetic(offset + cells, shift)
     code_ref[...] = jnp.where(offset < 0, ahead, jnp.where(offset < cells, offset, after))
     halo = code_ref[...] - cells
-    place = iota((2 * side, cells), 0)
+    place = iota((4 * side, cells), 0)
+    place = jnp.where(place < 2 * side, place, jnp.where(place < 3 * side, place - side, -1))
     for k in range(halo.shape[0]):
         here = (place == halo[k : k + 1, :]).astype(jnp.float32).astype(jnp.bfloat16)
-        pick_ref[2 * side * k : 2 * side * (k + 1), :] = here
+        pick_ref[4 * side * k : 4 * side * (k + 1), :] = here
 
 
 def mean_kernel(own_ref, other_ref, pack_ref, columns_ref):
@@ -395,13 +396,20 @@
 ):
     out_rows = out_ref.shape[0]
     cell = lax.axis_index("cell")
-    b = mean_of(own_b_ref[...], other_b_ref[...], channels)
-    b = jnp.where((cell == 0) | (cell == last), 0.0, b)
+    own_b, other_b = own_b_ref[...], other_b_ref[...]
     a = a_ref[...]
     a = [twice(a), twice(jnp.concatenate([a[:, channels:], a[:, :channels]], axis=1))]
-    halo = jnp.concatenate(a + [b], axis=0)
+    gap = jnp.zeros(own_b.shape, jnp.float32)
+    halo = jnp.concatenate(a + [twice(own_b), twice(other_b), gap], axis=0)
     cells = halo.shape[0]
     turns = LANES // cells
+    alone = (cell == 0) | (cell == last)
+    share = [
+        jnp.broadcast_to(jnp.where(alone, 0.0, v), own_b.shape)
+        for v in shares_of(own_b, other_b, channels)
+    ]
+    share = jnp.concatenate([gap + 1.0] + share + [gap], axis=0)
+    share = jnp.transpose(jnp.concatenate([share] * turns, axis=0))[:out_rows]
     left = iota(halo.shape, 1) < channels
     high = halo.astype(jnp.bfloat16).astype(jnp.float32)
     halo = jnp.concatenate(
@@ -415,7 +423,7 @@
         for turn in range(1, turns):
             rows = edge[start + turn * out_rows : start + (turn + 1) * out_rows]
             group = jnp.where(lane >= turn * cells, rows, group)
-        groups.append(group)
+        groups.append(group * share)
     high, low = halves(jnp.concatenate(groups, axis=1))
     pick = pick_ref[...]
     both = dot(jnp.concatenate([high, low], axis=0), pick, NN, None)
@@ -522,7 +530,7 @@
         [swath, enc_weight, key_weight, cell_query, quality, sample_cell, live],
         [
             shape(ROWS, 2 * channels),
-            shape(2 * channels, 6 * LATE * channels, dtype=jnp.bfloat16),
+            shape(6 * LATE * channels, 2 * channels, dtype=jnp.bfloat16),
             shape(ROWS, LANES, dtype=jnp.int32),
             shape(6, ROWS, LANES),
             shape(cells // 2 + ROWS, LANES),
@@ -564,7 +572,7 @@
             shape(stencil * out_rows, channels),
             shape((stencil - 1) * out_rows, 4 * channels, dtype=jnp.bfloat16),
             shape(*neighbours.shape, dtype=jnp.int32),
-            shape((stencil - 1) * 2 * side, cells, dtype=jnp.bfloat16),
+            shape((stencil - 1) * 4 * side, cells, dtype=jnp.bfloat16),
         ],
         cost=100_000_000,
     )

time: 14.1 us -> 14 us (level)
  no operation moved by 1% of the time
where the time goes in v9:
time: 14 us; the launch traced here: 13.8 us
  starting transfers between devices  6.26 us (45%)
  Pallas kernels  5.24 us (37%)
  waiting for transfers between devices  1.59 us (11%)
  between operations  0.7 us (5%)
    pallas_call x9, Pallas kernels, call(): pl.pallas_call(kernel, out_shape=outs, compiler_params=pltpu.CompilerPara...  5.24 us
    ppermute x1, starting transfers between devices, on_device(): other_b = lax.ppermute(pack, axes, far(flip))  2.05 us
    ppermute x1, starting transfers between devices, on_device(): tail_b = lax.ppermute(tail, axes, far(0))  1.86 us
    ppermute x1, waiting for transfers between devices, on_device(): own_b = lax.ppermute(pack_again, axes, far(0))  1.47 us
    ppermute x1, starting transfers between devices, on_device(): other = lax.ppermute(stats, axes, across(flip))  1.28 us
    ppermute x1, starting transfers between devices, on_device(): own_b = lax.ppermute(pack_again, axes, far(0))  0.56 us
    ppermute x1, starting transfers between devices, on_device(): halo_a = lax.ppermute(mean_a, axes, near)  0.5 us
  transfers between devices with their start and end apart: 6, of which 2 were waited for; matrix products, arithmetic and copies ran while one was open for 0% of the time, Pallas kernels for 20%

profile of v9, /device:TPU:13, one launch (start us, length us, event | category | flops | bytes accessed | tf_op | source)
XLA Modules:
  0.0 13.8 jit_solution(14479220413669449276)
XLA Ops:
  0.0 1.1 %shard_map.100 = (f32[1,64,512]{2,1,0:T(8,128)S(1)}, f32[64,256]{1,0:T(8,128)S(1)}, f32[1,64,192]{2,1,0:T(8,128)S(1)}, f32[64,64]{1,0:T(8,128)S(1)}, f32[1,512]{...) custom-call(f32[1,64,512]{2,1,0:T(8,128)} %refs_0_.1, ...), custom_call_target="tpu_custom_call" | custom-call | tf_op jit(solution)/shard_map/pallas_call | solution.py:482
  1.1 1.9 %collective-permute-start.1 = (f32[8,128]{1,0:T(8,128)S(1)}, f32[8,128]{1,0:T(8,128)S(1)}, u32[]{:S(2)}, u32[]{:S(2)}) collective-permute-start(f32[8,128]{1,0:T(8,128)S(1)} %get-tuple-element.34.in_ref), channel_id=1, source_target_pairs={{0,16},{1,2},{2,1},{3,4},{4,3},{5,6},{6,5},{7,8},{8,7},{9,10},{10,... | collective-permute-start | bytes 12296 | tf_op jit(solution)/shard_map/ppermute | solution.py:524
  3.0 0.0 collective-permute-start
  3.6 1.3 %shard_map.101 = (f32[8,128]{1,0:T(8,128)S(1)}, bf16[768,128]{1,0:T(8,128)(2,1)S(1)}, s32[8,128]{1,0:T(8,128)S(1)}, f32[6,8,128]{2,1,0:T(8,128)S(1)}, f32[136,128]{1,0:T(8,128)S(1)}, /*index=5*/f32[16,128]{1,0:T(8,128)S(1)}) custom-call(f32[1,64,512]{2,1,0:T(8,128)S(1)} %get-tuple-element.27.swath_ref, f32[1,64,192]{2,1,0:T(8,128)S(1)} %get-tuple-element.28.enc_ref, ...), custom_call_target="tpu_custom_call" | custom-call | flops 200000000 | bytes 2000000 | tf_op jit(solution)/shard_map/pallas_call | solution.py:482
  5.0 0.0 collective-permute-done.tail_a_ref
  5.0 0.1 collective-permute-done.1.tail_b_ref
  5.1 0.3 %shard_map.103 = (f32[136,128]{1,0:T(8,128)S(1)}, f32[16,128]{1,0:T(8,128)S(1)}) custom-call(bf16[768,128]{1,0:T(8,128)(2,1)S(1)} %get-tuple-element.33.taps_ref, f32[8,128]{1,0:T(8,128)S(1)} %collective-permute-done.tail_a_ref, f32[8,128]{1,0:T(8,128)S(1)} %collective-permute-done.1.tail_b_ref, f32[8,128]{1,0:T(8,128)S(1)} %get-tuple-element.35.before_ref, ...), custom_call_target="tpu_custom_call" | custom-call | tf_op jit(solution)/shard_map/pallas_call | solution.py:482
  5.4 1.3 %collective-permute-start.2 = (f32[136,128]{1,0:T(8,128)S(1)}, f32[136,128]{1,0:T(8,128)S(1)}, u32[]{:S(2)}, u32[]{:S(2)}) collective-permute-start(f32[136,128]{1,0:T(8,128)S(1)} %get-tuple-element.40.own_ref), channel_id=1, source_target_pairs={{0,16},{1,17},{2,18},{3,19},{4,20},{5,21},{6,22},{7,23},{8,24},{9,... | collective-permute-start | bytes 208904 | tf_op jit(solution)/shard_map/ppermute | solution.py:565
  6.6 2.1 %collective-permute-start.5 = (f32[16,128]{1,0:T(8,128)S(1)}, f32[16,128]{1,0:T(8,128)S(1)}, u32[]{:S(2)}, u32[]{:S(2)}) collective-permute-start(f32[16,128]{1,0:T(8,128)S(1)} %get-tuple-element.41.in_ref), channel_id=1, source_target_pairs={{0,16},{1,18},{2,17},{3,20},{4,19},{5,22},{6,21},{7,24},{8,23},{9,... | collective-permute-start | bytes 24584 | tf_op jit(solution)/shard_map/ppermute | solution.py:566
  8.7 0.6 %collective-permute-start.4 = (f32[16,128]{1,0:T(8,128)S(1)}, f32[16,128]{1,0:T(8,128)S(1)}, u32[]{:S(2)}, u32[]{:S(2)}) collective-permute-start(f32[16,128]{1,0:T(8,128)S(1)} %shard_map.105.after_ref), channel_id=1, source_target_pairs={{0,16},{1,2},{2,1},{3,4},{4,3},{5,6},{6,5},{7,8},{8,7},{9,10},{10,... | collective-permute-start | bytes 24584 | tf_op jit(solution)/shard_map/ppermute | solution.py:579
  9.3 0.4 %shard_map.106 = (f32[288,64]{1,0:T(8,128)S(1)}, bf16[256,256]{1,0:T(8,128)(2,1)S(1)}, s32[8,256]{1,0:T(8,128)S(1)}, bf16[512,256]{1,0:T(8,128)(2,1)S(1)}) custom-call(f32[64,64]{1,0:T(8,128)S(1)} %get-tuple-element.42.value_ref, s32[8,256]{1,0:T(8,128)S(1)} %get-tuple-element.43.near_ref, f32[32,576]{1,0:T(8,128)S(1)} %get-tuple-element.44.hp_ref, ...), custom_call_target="tpu_custom_call" | custom-call | flops 100000000 | bytes 1000000 | tf_op jit(solution)/shard_map/pallas_call | solution.py:482
  9.7 0.0 collective-permute-done.2.other_ref
  9.7 0.2 %shard_map.104 = f32[8,128]{1,0:T(8,128)S(1)} custom-call(f32[136,128]{1,0:T(8,128)S(1)} %get-tuple-element.40.own_ref, f32[136,128]{1,0:T(8,128)S(1)} %collective-permute-done.2.other_ref), custom_call_target="tpu_custom_call" | custom-call | tf_op jit(solution)/shard_map/pallas_call | solution.py:482
  9.9 0.5 %collective-permute-start.3 = (f32[8,128]{1,0:T(8,128)S(1)}, f32[8,128]{1,0:T(8,128)S(1)}, u32[]{:S(2)}, u32[]{:S(2)}) collective-permute-start(f32[8,128]{1,0:T(8,128)S(1)} %shard_map.104), channel_id=1, source_target_pairs={{0,1},{1,0},{2,3},{3,2},{4,5},{5,4},{6,7},{7,6},{8,9},{9,8},{10,11... | collective-permute-start | bytes 12296 | tf_op jit(solution)/shard_map/ppermute | solution.py:586
  10.4 0.8 %shard_map.107.partial_ref = f32[32,256]{1,0:T(8,128)S(1)} custom-call(f32[136,128]{1,0:T(8,128)S(1)} %get-tuple-element.40.own_ref, f32[136,128]{1,0:T(8,128)S(1)} %collective-permute-done.2.other_ref, f32[288,64]{1,0:T(8,128)S(1)} %get-tuple-element.45.hpv_ref, s32[8,256]{1,0:T(8,128)S(1)} %get-tuple-element.46.code_ref), custom_call_target="tpu_custom_call" | custom-call | flops 200000000 | bytes 2000000 | tf_op jit(solution)/shard_map/pallas_call | solution.py:482
  11.2 1.5 %collective-permute-done.4.own_b_ref = f32[16,128]{1,0:T(8,128)S(1)} collective-permute-done((f32[16,128]{1,0:T(8,128)S(1)}, f32[16,128]{1,0:T(8,128)S(1)}, u32[]{:S(2)}, u32[]{:S(2)}) %collective-permute-start.4) | collective-permute-done | bytes 8224 | tf_op jit(solution)/shard_map/ppermute | solution.py:579
  12.7 0.0 collective-permute-done.5.other_b_ref
  12.7 0.0 collective-permute-done.3.a_ref
  12.7 1.1 %shard_map.108 = f32[32,256]{1,0:T(8,128)} custom-call(f32[8,128]{1,0:T(8,128)S(1)} %collective-permute-done.3.a_ref, f32[16,128]{1,0:T(8,128)S(1)} %collective-permute-done.4.own_b_ref, f32[16,128]{1,0:T(8,128)S(1)} %collective-permute-done.5.other_b_ref, f32[32,256]{1,0:T(8,128)S(1)} %shard_map.107.partial_ref, ...), custom_call_target="tpu_custom_call" | custom-call | tf_op jit(solution)/shard_map/pallas_call | solution.py:482
  (2 shorter events, 0.0 us)
Async XLA Ops:
  1.1 4.0 %collective-permute-start.1 = (f32[8,128]{1,0:T(8,128)S(1)}, f32[8,128]{1,0:T(8,128)S(1)}, u32[]{:S(2)}, u32[]{:S(2)}) collective-permute-start(f32[8,128]{1,0:T(8,128)S(1)} %get-tuple-element.34.in_ref), channel_id=1, source_target_pairs={{0,16},{1,2},{2,1},{3,4},{4,3},{5,6},{6,5},{7,8},{8,7},{9,10},{10,... | collective-permute-start | bytes 12296 | tf_op jit(solution)/shard_map/ppermute | solution.py:524
  3.0 2.0 %collective-permute-start = (f32[8,128]{1,0:T(8,128)S(1)}, f32[8,128]{1,0:T(8,128)S(1)}, u32[]{:S(2)}, u32[]{:S(2)}) collective-permute-start(f32[8,128]{1,0:T(8,128)S(1)} %shard_map.102), channel_id=1, source_target_pairs={{0,1},{1,0},{2,3},{3,2},{4,5},{5,4},{6,7},{7,6},{8,9},{9,8},{10,11... | collective-permute-start | bytes 12296 | tf_op jit(solution)/shard_map/ppermute | solution.py:526
  5.4 4.3 %collective-permute-start.2 = (f32[136,128]{1,0:T(8,128)S(1)}, f32[136,128]{1,0:T(8,128)S(1)}, u32[]{:S(2)}, u32[]{:S(2)}) collective-permute-start(f32[136,128]{1,0:T(8,128)S(1)} %get-tuple-element.40.own_ref), channel_id=1, source_target_pairs={{0,16},{1,17},{2,18},{3,19},{4,20},{5,21},{6,22},{7,23},{8,24},{9,... | collective-permute-start | bytes 208904 | tf_op jit(solution)/shard_map/ppermute | solution.py:565
  6.6 6.0 %collective-permute-start.5 = (f32[16,128]{1,0:T(8,128)S(1)}, f32[16,128]{1,0:T(8,128)S(1)}, u32[]{:S(2)}, u32[]{:S(2)}) collective-permute-start(f32[16,128]{1,0:T(8,128)S(1)} %get-tuple-element.41.in_ref), channel_id=1, source_target_pairs={{0,16},{1,18},{2,17},{3,20},{4,19},{5,22},{6,21},{7,24},{8,23},{9,... | collective-permute-start | bytes 24584 | tf_op jit(solution)/shard_map/ppermute | solution.py:566
  8.7 4.0 %collective-permute-start.4 = (f32[16,128]{1,0:T(8,128)S(1)}, f32[16,128]{1,0:T(8,128)S(1)}, u32[]{:S(2)}, u32[]{:S(2)}) collective-permute-start(f32[16,128]{1,0:T(8,128)S(1)} %shard_map.105.after_ref), channel_id=1, source_target_pairs={{0,16},{1,2},{2,1},{3,4},{4,3},{5,6},{6,5},{7,8},{8,7},{9,10},{10,... | collective-permute-start | bytes 24584 | tf_op jit(solution)/shard_map/ppermute | solution.py:579
  9.9 2.8 %collective-permute-start.3 = (f32[8,128]{1,0:T(8,128)S(1)}, f32[8,128]{1,0:T(8,128)S(1)}, u32[]{:S(2)}, u32[]{:S(2)}) collective-permute-start(f32[8,128]{1,0:T(8,128)S(1)} %shard_map.104), channel_id=1, source_target_pairs={{0,1},{1,0},{2,3},{3,2},{4,5},{5,4},{6,7},{7,6},{8,9},{9,8},{10,11... | collective-permute-start | bytes 12296 | tf_op jit(solution)/shard_map/ppermute | solution.py:586

commit v10 on v9

--- a/solution.py
+++ b/solution.py
@@ -243,7 +243,12 @@
     tail = jnp.where(cell == 0, 0.0, tail)
     high, middle, low = parts(jnp.concatenate([tail, jnp.zeros(tail.shape, jnp.float32)], axis=0))
     tail = jnp.concatenate([high, middle, high, low, middle, high], axis=1)
-    tokens = gelu(before_ref[...] + dot(tail, taps_ref[...], NN, None)[:ROWS, :])
+    third = tail.shape[1] // 3
+    late = [
+        dot(tail[:, at : at + third], taps_ref[at : at + third, :], NN, None)[:ROWS, :]
+        for at in range(0, 3 * third, third)
+    ]
+    tokens = gelu(before_ref[...] + (late[0] + (late[1] + late[2])))
 
     key_query, rest, rest_total, rest_peak, quality, same = (late_ref[i] for i in range(6))
     score = jnp.sum(tokens * key_query, axis=1, keepdims=True) + quality
@@ -413,7 +418,7 @@
     left = iota(halo.shape, 1) < channels
     high = halo.astype(jnp.bfloat16).astype(jnp.float32)
     halo = jnp.concatenate(
-        [jnp.where(left, high, halo - high), jnp.where(left, high, 0.0)], axis=1
+        [jnp.where(left, high, halo - high), high], axis=1
     ).astype(jnp.bfloat16)
     edge = by_half(taps_ref[...], jnp.concatenate([halo] * turns, axis=0), NT)
     lane = iota((out_rows, LANES), 1)

time: 14 us -> 14 us (level)
  no operation moved by 1% of the time
where the time goes in v10:
time: 14 us; the launch traced here: 13.8 us
  starting transfers between devices  6.26 us (45%)
  Pallas kernels  5.24 us (37%)
  waiting for transfers between devices  1.59 us (11%)
  between operations  0.7 us (5%)
    pallas_call x9, Pallas kernels, call(): pl.pallas_call(kernel, out_shape=outs, compiler_params=pltpu.CompilerPara...  5.24 us
    ppermute x1, starting transfers between devices, on_device(): other_b = lax.ppermute(pack, axes, far(flip))  2.05 us
    ppermute x1, starting transfers between devices, on_device(): tail_b = lax.ppermute(tail, axes, far(0))  1.86 us
    ppermute x1, waiting for transfers between devices, on_device(): own_b = lax.ppermute(pack_again, axes, far(0))  1.47 us
    ppermute x1, starting transfers between devices, on_device(): other = lax.ppermute(stats, axes, across(flip))  1.28 us
    ppermute x1, starting transfers between devices, on_device(): own_b = lax.ppermute(pack_again, axes, far(0))  0.56 us
    ppermute x1, starting transfers between devices, on_device(): halo_a = lax.ppermute(mean_a, axes, near)  0.5 us
  transfers between devices with their start and end apart: 6, of which 2 were waited for; matrix products, arithmetic and copies ran while one was open for 0% of the time, Pallas kernels for 20%

profile of v10, /device:TPU:13, one launch (start us, length us, event | category | flops | bytes accessed | tf_op | source)
XLA Modules:
  0.0 13.8 jit_solution(14996225765558198439)
XLA Ops:
  0.0 1.1 %shard_map.100 = (f32[1,64,512]{2,1,0:T(8,128)S(1)}, f32[64,256]{1,0:T(8,128)S(1)}, f32[1,64,192]{2,1,0:T(8,128)S(1)}, f32[64,64]{1,0:T(8,128)S(1)}, f32[1,512]{...) custom-call(f32[1,64,512]{2,1,0:T(8,128)} %refs_0_.1, ...), custom_call_target="tpu_custom_call" | custom-call | tf_op jit(solution)/shard_map/pallas_call | solution.py:487
  1.1 1.9 %collective-permute-start.1 = (f32[8,128]{1,0:T(8,128)S(1)}, f32[8,128]{1,0:T(8,128)S(1)}, u32[]{:S(2)}, u32[]{:S(2)}) collective-permute-start(f32[8,128]{1,0:T(8,128)S(1)} %get-tuple-element.34.in_ref), channel_id=1, source_target_pairs={{0,16},{1,2},{2,1},{3,4},{4,3},{5,6},{6,5},{7,8},{8,7},{9,10},{10,... | collective-permute-start | bytes 12296 | tf_op jit(solution)/shard_map/ppermute | solution.py:529
  3.0 0.0 collective-permute-start
  3.6 1.3 %shard_map.101 = (f32[8,128]{1,0:T(8,128)S(1)}, bf16[768,128]{1,0:T(8,128)(2,1)S(1)}, s32[8,128]{1,0:T(8,128)S(1)}, f32[6,8,128]{2,1,0:T(8,128)S(1)}, f32[136,128]{1,0:T(8,128)S(1)}, /*index=5*/f32[16,128]{1,0:T(8,128)S(1)}) custom-call(f32[1,64,512]{2,1,0:T(8,128)S(1)} %get-tuple-element.27.swath_ref, f32[1,64,192]{2,1,0:T(8,128)S(1)} %get-tuple-element.28.enc_ref, ...), custom_call_target="tpu_custom_call" | custom-call | flops 200000000 | bytes 2000000 | tf_op jit(solution)/shard_map/pallas_call | solution.py:487
  5.0 0.0 collective-permute-done.tail_a_ref
  5.0 0.1 collective-permute-done.1.tail_b_ref
  5.1 0.3 %shard_map.103 = (f32[136,128]{1,0:T(8,128)S(1)}, f32[16,128]{1,0:T(8,128)S(1)}) custom-call(bf16[768,128]{1,0:T(8,128)(2,1)S(1)} %get-tuple-element.33.taps_ref, f32[8,128]{1,0:T(8,128)S(1)} %collective-permute-done.tail_a_ref, f32[8,128]{1,0:T(8,128)S(1)} %collective-permute-done.1.tail_b_ref, f32[8,128]{1,0:T(8,128)S(1)} %get-tuple-element.35.before_ref, ...), custom_call_target="tpu_custom_call" | custom-call | tf_op jit(solution)/shard_map/pallas_call | solution.py:487
  5.4 1.3 %collective-permute-start.2 = (f32[136,128]{1,0:T(8,128)S(1)}, f32[136,128]{1,0:T(8,128)S(1)}, u32[]{:S(2)}, u32[]{:S(2)}) collective-permute-start(f32[136,128]{1,0:T(8,128)S(1)} %get-tuple-element.40.own_ref), channel_id=1, source_target_pairs={{0,16},{1,17},{2,18},{3,19},{4,20},{5,21},{6,22},{7,23},{8,24},{9,... | collective-permute-start | bytes 208904 | tf_op jit(solution)/shard_map/ppermute | solution.py:570
  6.6 2.1 %collective-permute-start.5 = (f32[16,128]{1,0:T(8,128)S(1)}, f32[16,128]{1,0:T(8,128)S(1)}, u32[]{:S(2)}, u32[]{:S(2)}) collective-permute-start(f32[16,128]{1,0:T(8,128)S(1)} %get-tuple-element.41.in_ref), channel_id=1, source_target_pairs={{0,16},{1,18},{2,17},{3,20},{4,19},{5,22},{6,21},{7,24},{8,23},{9,... | collective-permute-start | bytes 24584 | tf_op jit(solution)/shard_map/ppermute | solution.py:571
  8.7 0.6 %collective-permute-start.4 = (f32[16,128]{1,0:T(8,128)S(1)}, f32[16,128]{1,0:T(8,128)S(1)}, u32[]{:S(2)}, u32[]{:S(2)}) collective-permute-start(f32[16,128]{1,0:T(8,128)S(1)} %shard_map.105.after_ref), channel_id=1, source_target_pairs={{0,16},{1,2},{2,1},{3,4},{4,3},{5,6},{6,5},{7,8},{8,7},{9,10},{10,... | collective-permute-start | bytes 24584 | tf_op jit(solution)/shard_map/ppermute | solution.py:584
  9.3 0.4 %shard_map.106 = (f32[288,64]{1,0:T(8,128)S(1)}, bf16[256,256]{1,0:T(8,128)(2,1)S(1)}, s32[8,256]{1,0:T(8,128)S(1)}, bf16[512,256]{1,0:T(8,128)(2,1)S(1)}) custom-call(f32[64,64]{1,0:T(8,128)S(1)} %get-tuple-element.42.value_ref, s32[8,256]{1,0:T(8,128)S(1)} %get-tuple-element.43.near_ref, f32[32,576]{1,0:T(8,128)S(1)} %get-tuple-element.44.hp_ref, ...), custom_call_target="tpu_custom_call" | custom-call | flops 100000000 | bytes 1000000 | tf_op jit(solution)/shard_map/pallas_call | solution.py:487
  9.7 0.0 collective-permute-done.2.other_ref
  9.7 0.2 %shard_map.104 = f32[8,128]{1,0:T(8,128)S(1)} custom-call(f32[136,128]{1,0:T(8,128)S(1)} %get-tuple-element.40.own_ref, f32[136,128]{1,0:T(8,128)S(1)} %collective-permute-done.2.other_ref), custom_call_target="tpu_custom_call" | custom-call | tf_op jit(solution)/shard_map/pallas_call | solution.py:487
  9.9 0.5 %collective-permute-start.3 = (f32[8,128]{1,0:T(8,128)S(1)}, f32[8,128]{1,0:T(8,128)S(1)}, u32[]{:S(2)}, u32[]{:S(2)}) collective-permute-start(f32[8,128]{1,0:T(8,128)S(1)} %shard_map.104), channel_id=1, source_target_pairs={{0,1},{1,0},{2,3},{3,2},{4,5},{5,4},{6,7},{7,6},{8,9},{9,8},{10,11... | collective-permute-start | bytes 12296 | tf_op jit(solution)/shard_map/ppermute | solution.py:591
  10.4 0.8 %shard_map.107.partial_ref = f32[32,256]{1,0:T(8,128)S(1)} custom-call(f32[136,128]{1,0:T(8,128)S(1)} %get-tuple-element.40.own_ref, f32[136,128]{1,0:T(8,128)S(1)} %collective-permute-done.2.other_ref, f32[288,64]{1,0:T(8,128)S(1)} %get-tuple-element.45.hpv_ref, s32[8,256]{1,0:T(8,128)S(1)} %get-tuple-element.46.code_ref), custom_call_target="tpu_custom_call" | custom-call | flops 200000000 | bytes 2000000 | tf_op jit(solution)/shard_map/pallas_call | solution.py:487
  11.2 1.5 %collective-permute-done.4.own_b_ref = f32[16,128]{1,0:T(8,128)S(1)} collective-permute-done((f32[16,128]{1,0:T(8,128)S(1)}, f32[16,128]{1,0:T(8,128)S(1)}, u32[]{:S(2)}, u32[]{:S(2)}) %collective-permute-start.4) | collective-permute-done | bytes 8224 | tf_op jit(solution)/shard_map/ppermute | solution.py:584
  12.7 0.0 collective-permute-done.5.other_b_ref
  12.7 0.0 collective-permute-done.3.a_ref
  12.7 1.1 %shard_map.108 = f32[32,256]{1,0:T(8,128)} custom-call(f32[8,128]{1,0:T(8,128)S(1)} %collective-permute-done.3.a_ref, f32[16,128]{1,0:T(8,128)S(1)} %collective-permute-done.4.own_b_ref, f32[16,128]{1,0:T(8,128)S(1)} %collective-permute-done.5.other_b_ref, f32[32,256]{1,0:T(8,128)S(1)} %shard_map.107.partial_ref, ...), custom_call_target="tpu_custom_call" | custom-call | tf_op jit(solution)/shard_map/pallas_call | solution.py:487
  (2 shorter events, 0.0 us)
Async XLA Ops:
  1.1 4.0 %collective-permute-start.1 = (f32[8,128]{1,0:T(8,128)S(1)}, f32[8,128]{1,0:T(8,128)S(1)}, u32[]{:S(2)}, u32[]{:S(2)}) collective-permute-start(f32[8,128]{1,0:T(8,128)S(1)} %get-tuple-element.34.in_ref), channel_id=1, source_target_pairs={{0,16},{1,2},{2,1},{3,4},{4,3},{5,6},{6,5},{7,8},{8,7},{9,10},{10,... | collective-permute-start | bytes 12296 | tf_op jit(solution)/shard_map/ppermute | solution.py:529
  3.0 2.0 %collective-permute-start = (f32[8,128]{1,0:T(8,128)S(1)}, f32[8,128]{1,0:T(8,128)S(1)}, u32[]{:S(2)}, u32[]{:S(2)}) collective-permute-start(f32[8,128]{1,0:T(8,128)S(1)} %shard_map.102), channel_id=1, source_target_pairs={{0,1},{1,0},{2,3},{3,2},{4,5},{5,4},{6,7},{7,6},{8,9},{9,8},{10,11... | collective-permute-start | bytes 12296 | tf_op jit(solution)/shard_map/ppermute | solution.py:531
  5.4 4.3 %collective-permute-start.2 = (f32[136,128]{1,0:T(8,128)S(1)}, f32[136,128]{1,0:T(8,128)S(1)}, u32[]{:S(2)}, u32[]{:S(2)}) collective-permute-start(f32[136,128]{1,0:T(8,128)S(1)} %get-tuple-element.40.own_ref), channel_id=1, source_target_pairs={{0,16},{1,17},{2,18},{3,19},{4,20},{5,21},{6,22},{7,23},{8,24},{9,... | collective-permute-start | bytes 208904 | tf_op jit(solution)/shard_map/ppermute | solution.py:570
  6.6 6.0 %collective-permute-start.5 = (f32[16,128]{1,0:T(8,128)S(1)}, f32[16,128]{1,0:T(8,128)S(1)}, u32[]{:S(2)}, u32[]{:S(2)}) collective-permute-start(f32[16,128]{1,0:T(8,128)S(1)} %get-tuple-element.41.in_ref), channel_id=1, source_target_pairs={{0,16},{1,18},{2,17},{3,20},{4,19},{5,22},{6,21},{7,24},{8,23},{9,... | collective-permute-start | bytes 24584 | tf_op jit(solution)/shard_map/ppermute | solution.py:571
  8.7 4.0 %collective-permute-start.4 = (f32[16,128]{1,0:T(8,128)S(1)}, f32[16,128]{1,0:T(8,128)S(1)}, u32[]{:S(2)}, u32[]{:S(2)}) collective-permute-start(f32[16,128]{1,0:T(8,128)S(1)} %shard_map.105.after_ref), channel_id=1, source_target_pairs={{0,16},{1,2},{2,1},{3,4},{4,3},{5,6},{6,5},{7,8},{8,7},{9,10},{10,... | collective-permute-start | bytes 24584 | tf_op jit(solution)/shard_map/ppermute | solution.py:584
  9.9 2.8 %collective-permute-start.3 = (f32[8,128]{1,0:T(8,128)S(1)}, f32[8,128]{1,0:T(8,128)S(1)}, u32[]{:S(2)}, u32[]{:S(2)}) collective-permute-start(f32[8,128]{1,0:T(8,128)S(1)} %shard_map.104), channel_id=1, source_target_pairs={{0,1},{1,0},{2,3},{3,2},{4,5},{5,4},{6,7},{7,6},{8,9},{9,8},{10,11... | collective-permute-start | bytes 12296 | tf_op jit(solution)/shard_map/ppermute | solution.py:591

commit v11 on v10

--- a/solution.py
+++ b/solution.py
@@ -83,8 +83,8 @@
     hp_ref, own_hp_ref = sources[-1], targets[-1]
     out_rows = own_hp_ref.shape[0]
     start = pl.multiple_of(lax.axis_index("sensor") * out_rows, ROWS)
-    copies += [(hp_ref.at[pl.ds(start, out_rows), :], own_hp_ref)]
-    copies += list(zip(sources[:-1], targets[:-1]))
+    copies += [(sources[0], targets[0]), (hp_ref.at[pl.ds(start, out_rows), :], own_hp_ref)]
+    copies += list(zip(sources[1:-1], targets[1:-1]))
     copies = [pltpu.make_async_copy(*ends, sems.at[i]) for i, ends in enumerate(copies)]
     for copy in copies:
         copy.start()
@@ -113,13 +113,12 @@
     high, middle, low = parts(twofold)
     mixed = jnp.where(iota(high.shape, 1) < right.shape[0], high, low)
     right_high, right_middle, right_low = parts(right)
-    return dot(
+    return by_half(
         jnp.concatenate([high, middle, mixed], axis=1),
         jnp.concatenate(
             [right_high, right_middle, right_high, right_middle, right_low, right_high], axis=0
         ),
         NN,
-        None,
     )
 
 

time: 14 us -> 14 us (level)
  no operation moved by 1% of the time
where the time goes in v11:
time: 14 us; the launch traced here: 13.8 us
  starting transfers between devices  6.29 us (45%)
  Pallas kernels  5.29 us (38%)
  waiting for transfers between devices  1.53 us (11%)
  between operations  0.69 us (5%)
    pallas_call x9, Pallas kernels, call(): pl.pallas_call(kernel, out_shape=outs, compiler_params=pltpu.CompilerPara...  5.29 us
    ppermute x1, starting transfers between devices, on_device(): other_b = lax.ppermute(pack, axes, far(flip))  2.05 us
    ppermute x1, starting transfers between devices, on_device(): tail_b = lax.ppermute(tail, axes, far(0))  1.86 us
    ppermute x1, waiting for transfers between devices, on_device(): own_b = lax.ppermute(pack_again, axes, far(0))  1.44 us
    ppermute x1, starting transfers between devices, on_device(): other = lax.ppermute(stats, axes, across(flip))  1.28 us
    ppermute x1, starting transfers between devices, on_device(): own_b = lax.ppermute(pack_again, axes, far(0))  0.56 us
    ppermute x1, starting transfers between devices, on_device(): halo_a = lax.ppermute(mean_a, axes, near)  0.53 us
  transfers between devices with their start and end apart: 6, of which 2 were waited for; matrix products, arithmetic and copies ran while one was open for 0% of the time, Pallas kernels for 20%

profile of v11, /device:TPU:13, one launch (start us, length us, event | category | flops | bytes accessed | tf_op | source)
XLA Modules:
  0.0 13.8 jit_solution(16506751632750916983)
XLA Ops:
  0.0 1.1 %shard_map.100 = (f32[1,64,512]{2,1,0:T(8,128)S(1)}, f32[64,256]{1,0:T(8,128)S(1)}, f32[1,64,192]{2,1,0:T(8,128)S(1)}, f32[64,64]{1,0:T(8,128)S(1)}, f32[1,512]{...) custom-call(f32[1,64,512]{2,1,0:T(8,128)} %refs_0_.1, ...), custom_call_target="tpu_custom_call" | custom-call | tf_op jit(solution)/shard_map/pallas_call | solution.py:486
  1.1 1.9 %collective-permute-start.1 = (f32[8,128]{1,0:T(8,128)S(1)}, f32[8,128]{1,0:T(8,128)S(1)}, u32[]{:S(2)}, u32[]{:S(2)}) collective-permute-start(f32[8,128]{1,0:T(8,128)S(1)} %get-tuple-element.34.in_ref), channel_id=1, source_target_pairs={{0,16},{1,2},{2,1},{3,4},{4,3},{5,6},{6,5},{7,8},{8,7},{9,10},{10,... | collective-permute-start | bytes 12296 | tf_op jit(solution)/shard_map/ppermute | solution.py:528
  3.0 0.0 collective-permute-start
  3.6 1.4 %shard_map.101 = (f32[8,128]{1,0:T(8,128)S(1)}, bf16[768,128]{1,0:T(8,128)(2,1)S(1)}, s32[8,128]{1,0:T(8,128)S(1)}, f32[6,8,128]{2,1,0:T(8,128)S(1)}, f32[136,128]{1,0:T(8,128)S(1)}, /*index=5*/f32[16,128]{1,0:T(8,128)S(1)}) custom-call(f32[1,64,512]{2,1,0:T(8,128)S(1)} %get-tuple-element.27.swath_ref, f32[1,64,192]{2,1,0:T(8,128)S(1)} %get-tuple-element.28.enc_ref, ...), custom_call_target="tpu_custom_call" | custom-call | flops 200000000 | bytes 2000000 | tf_op jit(solution)/shard_map/pallas_call | solution.py:486
  5.0 0.0 collective-permute-done.tail_a_ref
  5.0 0.1 collective-permute-done.1.tail_b_ref
  5.1 0.3 %shard_map.103 = (f32[136,128]{1,0:T(8,128)S(1)}, f32[16,128]{1,0:T(8,128)S(1)}) custom-call(bf16[768,128]{1,0:T(8,128)(2,1)S(1)} %get-tuple-element.33.taps_ref, f32[8,128]{1,0:T(8,128)S(1)} %collective-permute-done.tail_a_ref, f32[8,128]{1,0:T(8,128)S(1)} %collective-permute-done.1.tail_b_ref, f32[8,128]{1,0:T(8,128)S(1)} %get-tuple-element.35.before_ref, ...), custom_call_target="tpu_custom_call" | custom-call | tf_op jit(solution)/shard_map/pallas_call | solution.py:486
  5.4 1.3 %collective-permute-start.2 = (f32[136,128]{1,0:T(8,128)S(1)}, f32[136,128]{1,0:T(8,128)S(1)}, u32[]{:S(2)}, u32[]{:S(2)}) collective-permute-start(f32[136,128]{1,0:T(8,128)S(1)} %get-tuple-element.40.own_ref), channel_id=1, source_target_pairs={{0,16},{1,17},{2,18},{3,19},{4,20},{5,21},{6,22},{7,23},{8,24},{9,... | collective-permute-start | bytes 208904 | tf_op jit(solution)/shard_map/ppermute | solution.py:569
  6.6 2.1 %collective-permute-start.5 = (f32[16,128]{1,0:T(8,128)S(1)}, f32[16,128]{1,0:T(8,128)S(1)}, u32[]{:S(2)}, u32[]{:S(2)}) collective-permute-start(f32[16,128]{1,0:T(8,128)S(1)} %get-tuple-element.41.in_ref), channel_id=1, source_target_pairs={{0,16},{1,18},{2,17},{3,20},{4,19},{5,22},{6,21},{7,24},{8,23},{9,... | collective-permute-start | bytes 24584 | tf_op jit(solution)/shard_map/ppermute | solution.py:570
  8.7 0.6 %collective-permute-start.4 = (f32[16,128]{1,0:T(8,128)S(1)}, f32[16,128]{1,0:T(8,128)S(1)}, u32[]{:S(2)}, u32[]{:S(2)}) collective-permute-start(f32[16,128]{1,0:T(8,128)S(1)} %shard_map.105.after_ref), channel_id=1, source_target_pairs={{0,16},{1,2},{2,1},{3,4},{4,3},{5,6},{6,5},{7,8},{8,7},{9,10},{10,... | collective-permute-start | bytes 24584 | tf_op jit(solution)/shard_map/ppermute | solution.py:583
  9.3 0.4 %shard_map.106 = (f32[288,64]{1,0:T(8,128)S(1)}, bf16[256,256]{1,0:T(8,128)(2,1)S(1)}, s32[8,256]{1,0:T(8,128)S(1)}, bf16[512,256]{1,0:T(8,128)(2,1)S(1)}) custom-call(f32[64,64]{1,0:T(8,128)S(1)} %get-tuple-element.42.value_ref, s32[8,256]{1,0:T(8,128)S(1)} %get-tuple-element.43.near_ref, f32[32,576]{1,0:T(8,128)S(1)} %get-tuple-element.44.hp_ref, ...), custom_call_target="tpu_custom_call" | custom-call | flops 100000000 | bytes 1000000 | tf_op jit(solution)/shard_map/pallas_call | solution.py:486
  9.7 0.0 collective-permute-done.2.other_ref
  9.7 0.2 %shard_map.104 = f32[8,128]{1,0:T(8,128)S(1)} custom-call(f32[136,128]{1,0:T(8,128)S(1)} %get-tuple-element.40.own_ref, f32[136,128]{1,0:T(8,128)S(1)} %collective-permute-done.2.other_ref), custom_call_target="tpu_custom_call" | custom-call | tf_op jit(solution)/shard_map/pallas_call | solution.py:486
  9.9 0.5 %collective-permute-start.3 = (f32[8,128]{1,0:T(8,128)S(1)}, f32[8,128]{1,0:T(8,128)S(1)}, u32[]{:S(2)}, u32[]{:S(2)}) collective-permute-start(f32[8,128]{1,0:T(8,128)S(1)} %shard_map.104), channel_id=1, source_target_pairs={{0,1},{1,0},{2,3},{3,2},{4,5},{5,4},{6,7},{7,6},{8,9},{9,8},{10,11... | collective-permute-start | bytes 12296 | tf_op jit(solution)/shard_map/ppermute | solution.py:590
  10.4 0.8 %shard_map.107.partial_ref = f32[32,256]{1,0:T(8,128)S(1)} custom-call(f32[136,128]{1,0:T(8,128)S(1)} %get-tuple-element.40.own_ref, f32[136,128]{1,0:T(8,128)S(1)} %collective-permute-done.2.other_ref, f32[288,64]{1,0:T(8,128)S(1)} %get-tuple-element.45.hpv_ref, s32[8,256]{1,0:T(8,128)S(1)} %get-tuple-element.46.code_ref), custom_call_target="tpu_custom_call" | custom-call | flops 200000000 | bytes 2000000 | tf_op jit(solution)/shard_map/pallas_call | solution.py:486
  11.2 1.4 %collective-permute-done.4.own_b_ref = f32[16,128]{1,0:T(8,128)S(1)} collective-permute-done((f32[16,128]{1,0:T(8,128)S(1)}, f32[16,128]{1,0:T(8,128)S(1)}, u32[]{:S(2)}, u32[]{:S(2)}) %collective-permute-start.4) | collective-permute-done | bytes 8224 | tf_op jit(solution)/shard_map/ppermute | solution.py:583
  12.7 0.0 collective-permute-done.5.other_b_ref
  12.7 0.0 collective-permute-done.3.a_ref
  12.7 1.1 %shard_map.108 = f32[32,256]{1,0:T(8,128)} custom-call(f32[8,128]{1,0:T(8,128)S(1)} %collective-permute-done.3.a_ref, f32[16,128]{1,0:T(8,128)S(1)} %collective-permute-done.4.own_b_ref, f32[16,128]{1,0:T(8,128)S(1)} %collective-permute-done.5.other_b_ref, f32[32,256]{1,0:T(8,128)S(1)} %shard_map.107.partial_ref, ...), custom_call_target="tpu_custom_call" | custom-call | tf_op jit(solution)/shard_map/pallas_call | solution.py:486
  (2 shorter events, 0.0 us)
Async XLA Ops:
  1.1 4.0 %collective-permute-start.1 = (f32[8,128]{1,0:T(8,128)S(1)}, f32[8,128]{1,0:T(8,128)S(1)}, u32[]{:S(2)}, u32[]{:S(2)}) collective-permute-start(f32[8,128]{1,0:T(8,128)S(1)} %get-tuple-element.34.in_ref), channel_id=1, source_target_pairs={{0,16},{1,2},{2,1},{3,4},{4,3},{5,6},{6,5},{7,8},{8,7},{9,10},{10,... | collective-permute-start | bytes 12296 | tf_op jit(solution)/shard_map/ppermute | solution.py:528
  3.0 2.1 %collective-permute-start = (f32[8,128]{1,0:T(8,128)S(1)}, f32[8,128]{1,0:T(8,128)S(1)}, u32[]{:S(2)}, u32[]{:S(2)}) collective-permute-start(f32[8,128]{1,0:T(8,128)S(1)} %shard_map.102), channel_id=1, source_target_pairs={{0,1},{1,0},{2,3},{3,2},{4,5},{5,4},{6,7},{7,6},{8,9},{9,8},{10,11... | collective-permute-start | bytes 12296 | tf_op jit(solution)/shard_map/ppermute | solution.py:530
  5.4 4.3 %collective-permute-start.2 = (f32[136,128]{1,0:T(8,128)S(1)}, f32[136,128]{1,0:T(8,128)S(1)}, u32[]{:S(2)}, u32[]{:S(2)}) collective-permute-start(f32[136,128]{1,0:T(8,128)S(1)} %get-tuple-element.40.own_ref), channel_id=1, source_target_pairs={{0,16},{1,17},{2,18},{3,19},{4,20},{5,21},{6,22},{7,23},{8,24},{9,... | collective-permute-start | bytes 208904 | tf_op jit(solution)/shard_map/ppermute | solution.py:569
  6.6 6.0 %collective-permute-start.5 = (f32[16,128]{1,0:T(8,128)S(1)}, f32[16,128]{1,0:T(8,128)S(1)}, u32[]{:S(2)}, u32[]{:S(2)}) collective-permute-start(f32[16,128]{1,0:T(8,128)S(1)} %get-tuple-element.41.in_ref), channel_id=1, source_target_pairs={{0,16},{1,18},{2,17},{3,20},{4,19},{5,22},{6,21},{7,24},{8,23},{9,... | collective-permute-start | bytes 24584 | tf_op jit(solution)/shard_map/ppermute | solution.py:570
  8.7 4.0 %collective-permute-start.4 = (f32[16,128]{1,0:T(8,128)S(1)}, f32[16,128]{1,0:T(8,128)S(1)}, u32[]{:S(2)}, u32[]{:S(2)}) collective-permute-start(f32[16,128]{1,0:T(8,128)S(1)} %shard_map.105.after_ref), channel_id=1, source_target_pairs={{0,16},{1,2},{2,1},{3,4},{4,3},{5,6},{6,5},{7,8},{8,7},{9,10},{10,... | collective-permute-start | bytes 24584 | tf_op jit(solution)/shard_map/ppermute | solution.py:583
  9.9 2.8 %collective-permute-start.3 = (f32[8,128]{1,0:T(8,128)S(1)}, f32[8,128]{1,0:T(8,128)S(1)}, u32[]{:S(2)}, u32[]{:S(2)}) collective-permute-start(f32[8,128]{1,0:T(8,128)S(1)} %shard_map.104), channel_id=1, source_target_pairs={{0,1},{1,0},{2,3},{3,2},{4,5},{5,4},{6,7},{7,6},{8,9},{9,8},{10,11... | collective-permute-start | bytes 12296 | tf_op jit(solution)/shard_map/ppermute | solution.py:590
